TPU v7x, 256 devices: a whole 4x4x8 slice. The times are simulated.
256 devices in a mesh: seq: 64 (over x, z, core), head: 4 (over y).
Axes of the slice: x: 4, y: 4, z: 8, core: 2. Of those that a mesh axis runs over, the one named last changes fastest.
Arguments:
- mla_queries: bfloat16 [2, 4096, 36864], P(None, 'seq', 'head'), may hold values from -30 to 30
- latent_keys: bfloat16 [4096, 1152], P('seq'), may hold values from -20 to 20
- index_queries: bfloat16 [2, 4096, 8192], P(None, 'seq'), may hold values from -64 to 64
- index_keys: bfloat16 [4096, 256], P('seq'), may hold values from -20 to 20
- head_weights: float32 [4096, 128], P('seq'), may hold values from -6 to 6
- block_order: int32 [128], replicated, may hold values from 0 to 127, as said below
Outputs:
- key_grad: float32 [4096, 256], P(('seq', 'head'))
Inputs may be any that keep to these rules, and one draw needn't show every extreme that they name: Index d of seq holds, in each sequence, half-block block_order[2 * d] in its first 32 rows and half-block block_order[2 * d + 1] in its last 32 rows; block_order[2 * d] < 64 and block_order[2 * d] + block_order[2 * d + 1] = 127; every half-block number appears once.
All inputs are finite; a program needn't handle non-finite values.
Results may differ from a plain program's by a relative error of at most 0.002.
Values may be sent and summed in bfloat16 or wider, within the bound.
A program may use at most 128 MiB of HBM per device.

v0:
```python
import jax
import jax.numpy as jnp
from jax import lax
from jax.sharding import PartitionSpec as P

MLA_HEADS = 64
SEQS = 2


score_scale = 192.0 ** (-0.5)
loss_scale = 1024.0


def sequence_rows(block_order, tok_dev, seq_count, pieces):
    half_rows = tok_dev // 2
    position = jnp.arange(tok_dev * seq_count, dtype=jnp.int32)
    slot_ids = jnp.arange(2 * seq_count, dtype=jnp.int32)
    slot_of = jnp.sum(
        jnp.where(block_order[None, :] == (position // half_rows)[:, None], slot_ids[None, :], 0),
        axis=1,
    )
    owner_id = slot_of // 2
    local_row = slot_of % 2 * half_rows + position % half_rows
    piece_rows = tok_dev // pieces
    return (
        local_row // piece_rows * (seq_count * piece_rows)
        + owner_id * piece_rows
        + local_row % piece_rows
    )


def storage_places(block_order, tok_dev, seq_count):
    half_rows = tok_dev // 2
    row_ids = jnp.arange(tok_dev * seq_count, dtype=jnp.int32)
    slot_of = 2 * (row_ids // tok_dev) + row_ids % tok_dev // half_rows
    slot_ids = jnp.arange(2 * seq_count, dtype=jnp.int32)
    half_block = jnp.sum(
        jnp.where(slot_of[:, None] == slot_ids[None, :], block_order[None, :], 0), axis=1
    )
    return half_block * half_rows + row_ids % half_rows


def block_total(half_block, half_rows, kblock):
    return ((half_block + 1) * half_rows + kblock - 1) // kblock


def block_dot(query_rows, key_rows, first_key, kblock):
    key_block = lax.dynamic_slice_in_dim(key_rows, first_key, kblock, 0)
    return lax.dot_general(
        query_rows, key_block, (((1,), (1,)), ((), ())), preferred_element_type=jnp.float32
    )


def visible(first_key, kblock, places):
    return (first_key + jnp.arange(kblock, dtype=jnp.int32))[None, :] <= places[:, None]


def row_lse(query_rows, places, key_rows, loop_count, kblock):
    row_count = query_rows.shape[0]

    def step(block_index, carry):
        running_max, running_sum = carry
        first_key = block_index * kblock
        scores = score_scale * block_dot(query_rows, key_rows, first_key, kblock)
        scores = jnp.where(visible(first_key, kblock, places), scores, -jnp.inf)
        new_max = jnp.maximum(running_max, jnp.max(scores, axis=1))
        running_sum = running_sum * jnp.exp(running_max - new_max) + jnp.sum(
            jnp.exp(scores - new_max[:, None]), axis=1
        )
        return (new_max, running_sum)

    initial = (jnp.full((row_count,), -jnp.inf, jnp.float32), jnp.zeros((row_count,), jnp.float32))
    running_max, running_sum = lax.fori_loop(0, loop_count, step, initial)
    return running_max + jnp.log(running_sum)


def row_target(
    query_rows, token_places, log_totals, key_rows, loop_count, kblock, length, heads_dev, all_heads
):
    row_count = token_places.shape[0]
    places = jnp.repeat(token_places, heads_dev)

    def step(block_index, totals):
        first_key = block_index * kblock
        scores = score_scale * block_dot(query_rows, key_rows, first_key, kblock)
        scores = jnp.where(visible(first_key, kblock, places), scores, -jnp.inf)
        probabilities = jnp.exp(scores - log_totals[:, None]).reshape(row_count, heads_dev, kblock)
        return lax.dynamic_update_slice_in_dim(
            totals, jnp.sum(probabilities, axis=1) / all_heads, first_key, 1
        )

    return lax.fori_loop(0, loop_count, step, jnp.zeros((row_count, length), jnp.float32))


def index_part(
    query_rows,
    weights,
    key_rows,
    token_places,
    target,
    loop_count,
    kblock,
    length,
    grad_coef,
    index_norm,
):
    row_count, index_heads = weights.shape

    def forward(block_index, carry):
        logits, positive = carry
        first_key = block_index * kblock
        inner_dot = block_dot(query_rows, key_rows, first_key, kblock)
        mixture = jnp.sum(
            jnp.maximum(inner_dot, 0.0).reshape(row_count, index_heads, kblock)
            * weights[:, :, None],
            axis=1,
        )
        logits = lax.dynamic_update_slice_in_dim(logits, index_norm * mixture, first_key, 1)
        positive = lax.dynamic_update_slice_in_dim(positive, inner_dot > 0.0, first_key, 1)
        return (logits, positive)

    initial = (
        jnp.zeros((row_count, length), jnp.float32),
        jnp.zeros((row_count * index_heads, length), jnp.bool_),
    )
    logits, positive = lax.fori_loop(0, loop_count, forward, initial)
    visible_mask = jnp.arange(length, dtype=jnp.int32)[None, :] <= token_places[:, None]
    logits = jnp.where(visible_mask, logits, -jnp.inf)
    row_max = jnp.max(logits, axis=1, keepdims=True)
    exp_logits = jnp.exp(logits - row_max)
    probabilities = exp_logits / jnp.sum(exp_logits, axis=1, keepdims=True)
    scaled = grad_coef * (probabilities - target)

    def backward(block_index, totals):
        first_key = block_index * kblock
        relu_mask = lax.dynamic_slice_in_dim(positive, first_key, kblock, 1).reshape(
            row_count, index_heads, kblock
        )
        target_part = lax.dynamic_slice_in_dim(scaled, first_key, kblock, 1)
        signal = (target_part[:, None, :] * weights[:, :, None] * relu_mask).astype(jnp.bfloat16)
        signal = signal.reshape(row_count * index_heads, kblock)
        key_part = lax.dot_general(
            signal, query_rows, (((0,), (0,)), ((), ())), preferred_element_type=jnp.float32
        )
        current = lax.dynamic_slice_in_dim(totals, first_key, kblock, 0)
        return lax.dynamic_update_slice_in_dim(totals, current + key_part, first_key, 0)

    return lax.fori_loop(
        0, loop_count, backward, jnp.zeros((length, query_rows.shape[1]), jnp.float32)
    )


def per_device(mla_queries, latent_keys, index_queries, index_keys, head_weights, block_order):
    seq_count = lax.axis_size("seq")
    head_count = lax.axis_size("head")
    tok_dev = latent_keys.shape[0]
    half_rows = tok_dev // 2
    length = tok_dev * seq_count
    kblock = min(256, length)
    latent_width = latent_keys.shape[1] // SEQS
    index_width = index_keys.shape[1] // SEQS
    index_heads = head_weights.shape[1] // SEQS
    heads_dev = mla_queries.shape[2] // latent_width
    my_seq = lax.axis_index("seq")
    my_head = lax.axis_index("head")
    index_norm = (index_width * index_heads) ** (-0.5)
    grad_coef = loss_scale * index_norm
    gathered_latent, gathered_index = (
        lax.all_gather(latent_keys, "seq", axis=0, tiled=True),
        lax.all_gather(index_keys, "seq", axis=0, tiled=True),
    )
    pieces = 1
    rows_in_order = sequence_rows(block_order, tok_dev, seq_count, pieces)
    ordered_latent = jnp.take(gathered_latent, rows_in_order, axis=0)
    ordered_index = jnp.take(gathered_index, rows_in_order, axis=0)
    lse_list = []
    for seq_id in range(SEQS):
        key_rows = ordered_latent[:, seq_id * latent_width : (seq_id + 1) * latent_width]
        for which_half in range(2):
            half_block = block_order[2 * my_seq + which_half]
            token_places = half_block * half_rows + jnp.arange(half_rows, dtype=jnp.int32)
            query_rows = mla_queries[seq_id, which_half * half_rows : (which_half + 1) * half_rows]
            query_rows = query_rows.reshape(half_rows * heads_dev, latent_width)
            loop_count = block_total(half_block, half_rows, kblock)
            lse_list.append(
                row_lse(
                    query_rows, jnp.repeat(token_places, heads_dev), key_rows, loop_count, kblock
                )
            )
    lse_all = jnp.stack(lse_list)
    group_count = 2 * SEQS
    first_group = jnp.int32(0)
    term_list = []
    for offset in range(group_count // head_count * lax.axis_size("head")):
        group_id = first_group + offset
        group_seq_id = group_id // 2
        which_half = group_id % 2
        half_block = block_order[2 * my_seq + which_half]
        token_places = half_block * half_rows + jnp.arange(half_rows, dtype=jnp.int32)
        query_rows = lax.dynamic_slice(
            mla_queries,
            (group_seq_id, which_half * half_rows, 0),
            (1, half_rows, mla_queries.shape[2]),
        )
        query_rows = query_rows.reshape(half_rows * heads_dev, latent_width)
        key_rows = lax.dynamic_slice_in_dim(
            ordered_latent, group_seq_id * latent_width, latent_width, 1
        )
        log_totals = lax.dynamic_index_in_dim(lse_all, group_id, 0, keepdims=False)
        loop_count = block_total(half_block, half_rows, kblock)
        term_list.append(
            row_target(
                query_rows,
                token_places,
                log_totals,
                key_rows,
                loop_count,
                kblock,
                length,
                heads_dev,
                MLA_HEADS,
            )
        )
    target = lax.psum_scatter(jnp.stack(term_list), "head", scatter_dimension=0, tiled=True)[0]
    seq_id = my_head // 2
    which_half = my_head % 2
    half_block = block_order[2 * my_seq + which_half]
    token_places = half_block * half_rows + 0 + jnp.arange(half_rows, dtype=jnp.int32)
    first_row = which_half * half_rows + 0
    query_rows = lax.dynamic_slice(
        index_queries, (seq_id, first_row, 0), (1, half_rows, index_queries.shape[2])
    )
    query_rows = query_rows.reshape(half_rows * index_heads, index_width)
    weights = lax.dynamic_slice(
        head_weights, (first_row, seq_id * index_heads), (half_rows, index_heads)
    )
    key_rows = lax.dynamic_slice_in_dim(ordered_index, seq_id * index_width, index_width, 1)
    loop_count = block_total(half_block, half_rows, kblock)
    key_grads = index_part(
        query_rows,
        weights,
        key_rows,
        token_places,
        target,
        loop_count,
        kblock,
        length,
        grad_coef,
        index_norm,
    )
    places = storage_places(block_order, tok_dev, seq_count)
    stored = jnp.take(key_grads, places, axis=0)
    partial_value = jnp.concatenate(
        [jnp.where(seq_id == slot_id, stored, 0.0) for slot_id in range(SEQS)], axis=1
    )
    result = lax.psum_scatter(partial_value, ("seq", "head"), scatter_dimension=0, tiled=True)
    return result


def solution(mesh):
    return jax.shard_map(
        per_device,
        mesh=mesh,
        in_specs=(
            P(None, "seq", "head"),
            P("seq", None),
            P(None, "seq", None),
            P("seq", None),
            P("seq", None),
            P(),
        ),
        out_specs=P(("seq", "head"), None),
        check_vma=False,
    )
```

profile of v0, /device:TPU:1, one launch (start us, length us, event | category | flops | bytes accessed | tf_op | source)
XLA Modules:
  0.0 1841.8 jit_solution(13354325137103213831)
XLA Ops:
  13.2 2.8 fusion.104
  16.0 2.5 reshape.386
  18.5 2.5 reshape.387
  25.2 2.5 select_reduce_fusion.1
  28.1 63.5 %all-gather.3.cloned.1.call-done = bf16[4096,256]{1,0:T(8,128)(2,1)} async-done(((bf16[64,256]{1,0:T(8,128)(2,1)}), bf16[4096,256]{1,0:T(8,128)(2,1)}) %all-gather.3.cloned.1.call-update) | async-done | bytes 2097168 | tf_op jit(solution)/shard_map/all_gather | solution.py:170
  91.6 14.9 gather_fusion
  106.5 2.9 dynamic-slice_select_fusion
  109.4 67.7 %all-gather.5.cloned.1.call-done = bf16[4096,1152]{1,0:T(8,128)(2,1)} async-done(((bf16[64,1152]{1,0:T(8,128)(2,1)}), bf16[4096,1152]{1,0:T(8,128)(2,1)}) %all-gather.5.cloned.1.call-update) | async-done | bytes 9437200 | tf_op jit(solution)/shard_map/all_gather | solution.py:169
  177.1 26.9 %gather_fusion.1 = bf16[4096,1152]{1,0:T(8,128)(2,1)} fusion(bf16[4096,1152]{1,0:T(8,128)(2,1)} %all-gather.5.cloned.1.call-done, s32[4096]{0:T(1024)S(1)} %broadcast_clamp_fusion.1), kind=kCustom, calls=%fused_computation.1 | custom fusion | bytes 18890752 | tf_op jit(solution)/shard_map/jit(_take)/gather | solution.py:174
  204.0 10.0 broadcast_select_fusion
  214.0 11.2 fusion.103
  225.2 10.4 while.120
  235.7 13.1 while.121
  248.9 19.1 %while.122 = (s32[]{:T(128)}, f32[512]{0:T(512)S(1)}, f32[512]{0:T(512)S(1)}, s32[]{:T(128)}, bf16[4096,576]{1,0:T(8,128)(2,1)}, /*index=5*/bf16[512,576]{1,0:T(...) while((s32[]{:T(128)}, f32[512]{0:T(512)S(1)}, ...), condition=%wide.region_17.18_spmd.clone, body=%wide.region_14.17_spmd.clone.sunk | while | flops 151782656 | bytes 2003235 | solution.py:73
  268.1 23.7 %while.123 = (s32[]{:T(128)}, f32[32,4096]{1,0:T(8,128)S(1)}, s32[]{:T(128)}, bf16[4096,576]{1,0:T(8,128)(2,1)}, bf16[512,576]{1,0:T(8,128)(2,1)}, /*index=5*/f3...) while((s32[]{:T(128)}, f32[32,4096]{1,0:T(8,128)S(1)}, ...), condition=%wide.region_20.21_spmd.clone, body=%wide.region_18.20_spmd.clone.sunk | while | flops 151650560 | bytes 3191079 | solution.py:92
  291.8 10.4 while.124
  302.3 12.9 while.125
  315.3 21.5 %while.126 = (s32[]{:T(128)}, f32[512]{0:T(512)S(1)}, f32[512]{0:T(512)S(1)}, s32[]{:T(128)}, bf16[4096,576]{1,0:T(8,128)(2,1)}, /*index=5*/bf16[512,576]{1,0:T(...) while((s32[]{:T(128)}, f32[512]{0:T(512)S(1)}, ...), condition=%wide.region_31.32_spmd.clone, body=%wide.region_28.31_spmd.clone.sunk | while | flops 151782656 | bytes 2068771 | solution.py:73
  336.9 23.7 %while.127 = (s32[]{:T(128)}, f32[32,4096]{1,0:T(8,128)S(1)}, s32[]{:T(128)}, bf16[4096,576]{1,0:T(8,128)(2,1)}, bf16[512,576]{1,0:T(8,128)(2,1)}, /*index=5*/f3...) while((s32[]{:T(128)}, f32[32,4096]{1,0:T(8,128)S(1)}, ...), condition=%wide.region_34.35_spmd.clone, body=%wide.region_32.34_spmd.clone.sunk | while | flops 151650560 | bytes 3191079 | solution.py:92
  362.2 5.4 broadcast_in_dim.129
  367.6 38.2 %while.119 = (s32[]{:T(128)}, f32[32,4096]{1,0:T(8,128)S(1)}, pred[2048,4096]{0,1:T(32,128)(4,1)}, s32[]{:T(128)}, bf16[4096,128]{1,0:T(8,128)(2,1)}, /*index=5*...) while((s32[]{:T(128)}, f32[32,4096]{1,0:T(8,128)S(1)}, ...), condition=%wide.region_4.5_spmd, body=%wide.region_2.4_spmd.sunk | while | flops 136314880 | bytes 13804703 | solution.py:126
  367.7 2.3 bitcast_dynamic-update-slice_fusion.2
  374.0 2.3 bitcast_dynamic-update-slice_fusion.2
  380.4 2.4 bitcast_dynamic-update-slice_fusion.2
  386.8 2.3 bitcast_dynamic-update-slice_fusion.2
  393.1 2.3 bitcast_dynamic-update-slice_fusion.2
  399.5 2.3 bitcast_dynamic-update-slice_fusion.2
  408.7 30.0 %while.128 = (s32[]{:T(128)}, f32[4096,128]{1,0:T(8,128)S(1)}, s32[]{:T(128)}, pred[2048,4096]{0,1:T(32,128)(4,1)}, f32[32,4096]{1,0:T(8,128)}, /*index=5*/f32[3...) while((s32[]{:T(128)}, f32[4096,128]{1,0:T(8,128)S(1)}, ...), condition=%wide.wide.region_37.38_spmd, body=%wide.wide.region_36.37_spmd.sunk | while | flops 135823360 | bytes 5611695 | solution.py:148
  438.7 14.1 gather_fusion.2
  452.8 3.6 select_select_fusion.1
  456.4 2.2 pad_maximum_fusion
  458.6 1376.6 %reduce-scatter.5.cloned.1.call-done = f32[16,256]{1,0:T(8,128)} async-done(((f32[4096,256]{1,0:T(8,128)}), f32[16,256]{1,0:T(8,128)}) %reduce-scatter.5.cloned.1.call-update) | async-done | bytes 16400 | tf_op jit(solution)/shard_map/reduce_scatter | solution.py:256
  (629 shorter events, 196.6 us)
Async XLA Ops:
  6.5 17.3 copy-start
  6.5 85.1 %all-gather.3.cloned.1.call-start = ((), (), s32[]{:S(2)}) async-start(), calls=%async_computation.2 | async-start | bytes 2129920 | tf_op jit(solution)/shard_map/all_gather | solution.py:170
  7.3 169.8 %all-gather.5.cloned.1.call-start = ((), (), s32[]{:S(2)}) async-start(), calls=%async_computation.3 | async-start | bytes 9584640 | tf_op jit(solution)/shard_map/all_gather | solution.py:169
  8.0 398.4 %reduce-scatter.3.cloned.1.call-start = ((), (), s32[]{:S(2)}) async-start(), calls=%async_computation.4 | async-start | bytes 2621440 | tf_op jit(solution)/shard_map/reduce_scatter | solution.py:224
  21.0 4.0 copy-start.7
  21.0 4.2 copy-start.6
  214.0 11.3 copy-start.5
  235.7 13.2 copy-start.4
  268.1 23.8 %copy-start.3 = (bf16[512,576]{1,0:T(8,128)(2,1)S(1)}, bf16[512,576]{1,0:T(8,128)(2,1)}, u32[]{:S(2)}) copy-start(bf16[512,576]{1,0:T(8,128)(2,1)} %reshape.388) | copy-start | bytes 1769476
  362.2 1473.1 %reduce-scatter.5.cloned.1.call-start = ((), (), s32[]{:S(2)}) async-start(), calls=%async_computation.5 | async-start | bytes 4210688 | tf_op jit(solution)/shard_map/reduce_scatter | solution.py:256
  405.8 2.9 copy-start.2
  458.6 1376.6 %copy-start.1 = (bf16[2,64,8192]{2,1,0:T(8,128)(2,1)S(1)}, bf16[2,64,8192]{2,1,0:T(8,128)(2,1)}, u32[]{:S(2)}) copy-start(bf16[2,64,8192]{2,1,0:T(8,128)(2,1)} %param.28) | copy-start | bytes 6291460
Sparse Core Ops, SparseCore 0:
  10.1 81.4 all-gather.2
  94.3 82.6 all-gather.4
  362.3 29.7 reduce-scatter.2
  458.8 1376.4 reduce-scatter.4
where the time goes:
time: 1850 us; the launch traced here: 1840 us
  waiting for transfers between devices  1510 us (82%)
  local copies, waits for them, and re-layouts  132 us (7%)
  matrix products  129 us (7%)
  other arithmetic  49.3 us (3%)
    reduce_scatter x1, waiting for transfers between devices, per_device(): lax.psum_scatter(partial_value, ('seq', 'head'), scatter_dimension=0, til...  1380 us
    dot_general x74, matrix products, block_dot(): lax.dot_general(query_rows, key_block, (((1,), (1,)), ((), ())), preferre...  120 us
    all_gather x1, waiting for transfers between devices, per_device(): lax.all_gather(latent_keys, 'seq', axis=0, tiled=True)  67.7 us
    all_gather x1, waiting for transfers between devices, per_device(): lax.all_gather(index_keys, 'seq', axis=0, tiled=True)  63.5 us
  transfers between devices with their start and end apart: 4, of which 3 were waited for; matrix products, arithmetic and copies ran while one was open for 4% of the time, Pallas kernels for 0%

commit v1 on v0

v1 whole, which is shorter than its diff:
```python
import functools
import math

import jax
import jax.numpy as jnp
from jax import lax
from jax.experimental import pallas as pl
from jax.experimental.pallas import tpu as pltpu
from jax.sharding import PartitionSpec as P

MESH = pl.DeviceIdType.MESH
NX, NZ, NY = 4, 8, 4
HEADS = 64
HEADS_DEV = 16
KD = 576
KPAD = 640
IDX_HEADS = 64
IDX_DIM = 128
TOK = 64
HALF = 32
HALVES = 128
SLOTS = 36
SCORE_SCALE = 192.0 ** (-0.5)
LOG2E = 1.4426950408889634
INDEX_NORM = (IDX_HEADS * IDX_DIM) ** (-0.5)
GRAD_COEF = 1024.0 * INDEX_NORM
NEG = -1e30
VMEM_BYTES = 60 * 1024 * 1024
F32 = jnp.float32
BF16 = jnp.bfloat16


def coords():
    s = lax.axis_index("seq")
    y = lax.axis_index("head")
    return s // (2 * NZ), (s // 2) % NZ, s % 2, y


def seq_at(x, z, c):
    return (x * NZ + z) * 2 + c


def gather_kernel(
    lat_ref, idx_ref, hw_ref, mq_ref, iq_ref,
    p_out, q_out, mqx_ref, iqx_ref, hwx_ref,
    own_p, own_q, stage_out, stage_in, idx32, idx_stage_in, idx_stage_out,
    pair_send, pair_recv, send_sem, recv_sem, local_sem,
):
    x, z, c, y = coords()
    partner = (seq_at(x, z, 1 - c), y)
    ring = {
        ("x", 1): (seq_at((x + 1) % NX, z, c), y),
        ("x", -1): (seq_at((x + NX - 1) % NX, z, c), y),
        ("z", 1): (seq_at(x, (z + 1) % NZ, c), y),
        ("z", -1): (seq_at(x, (z + NZ - 1) % NZ, c), y),
    }
    barrier = pltpu.get_barrier_semaphore()
    for target in [partner] + list(ring.values()):
        pl.semaphore_signal(barrier, inc=1, device_id=target, device_id_type=MESH)

    lat = lat_ref[...]
    stage_out[:, 0:KD] = jnp.where(c == 0, lat[:, KD:], lat[:, :KD])
    stage_out[:, KD:] = jnp.zeros((TOK, KPAD - KD), BF16)
    idx32[...] = idx_ref[...].astype(F32)
    rows = jnp.concatenate(
        [idx32[pl.ds(pl.multiple_of(y * 8, 8), 8), :], idx32[pl.ds(pl.multiple_of(HALF + y * 8, 8), 8), :]], axis=0
    )
    idx_stage_out[...] = jnp.where(c == 0, rows[:, IDX_DIM:], rows[:, :IDX_DIM]).astype(BF16)
    pl.semaphore_wait(barrier, 5)

    def pair_copy(k, src, dst):
        return pltpu.make_async_remote_copy(
            src_ref=src, dst_ref=dst, send_sem=pair_send.at[k], recv_sem=pair_recv.at[k],
            device_id=partner, device_id_type=MESH,
        )

    pair = [
        pair_copy(0, stage_out, stage_in),
        pair_copy(1, idx_stage_out, idx_stage_in),
        pair_copy(2, mq_ref.at[1 - c], mqx_ref),
        pair_copy(3, iq_ref.at[1 - c], iqx_ref),
        pair_copy(4, hw_ref, hwx_ref),
    ]
    for d in pair:
        d.start()
    mine = jnp.where(c == 0, lat[:, :KD], lat[:, KD:])
    idx_mine = jnp.where(c == 0, rows[:, :IDX_DIM], rows[:, IDX_DIM:]).astype(BF16)
    pair[0].wait_recv()
    pair[1].wait_recv()
    other = stage_in[:, :KD]
    both = jnp.concatenate([jnp.where(c == 0, mine, other), jnp.where(c == 0, other, mine)], axis=1)
    own_p[...] = both[:HALF]
    own_q[:, : 2 * KD] = both[HALF:]
    idx_other = idx_stage_in[...]
    own_q[0:16, 2 * KD :] = jnp.where(c == 0, idx_mine, idx_other)
    own_q[16:32, 2 * KD :] = jnp.where(c == 0, idx_other, idx_mine)
    keep = [
        pltpu.make_async_copy(own_p, p_out.at[x, z], local_sem.at[0]),
        pltpu.make_async_copy(own_q, q_out.at[x, z], local_sem.at[1]),
    ]
    for d in keep:
        d.start()

    counter = [0]
    live = {}

    def block(part, ox, oz, rows_from, rows_to):
        ref = p_out if part == "p" else q_out
        return ref.at[ox, oz, pl.ds(rows_from, rows_to - rows_from)]

    def send(part, axis, way, dx, dz, rows_from, rows_to):
        k = counter[0]
        counter[0] += 1
        ox, oz = (x + dx + NX) % NX, (z + dz + NZ) % NZ
        if dx == 0 and dz == 0:
            src = (own_p if part == "p" else own_q).at[pl.ds(rows_from, rows_to - rows_from)]
        else:
            src = block(part, ox, oz, rows_from, rows_to)
        out = pltpu.make_async_remote_copy(
            src_ref=src, dst_ref=block(part, ox, oz, rows_from, rows_to),
            send_sem=send_sem.at[k], recv_sem=recv_sem.at[k], device_id=ring[(axis, way)], device_id_type=MESH,
        )
        out.start()
        ix, iz = (dx - way, dz) if axis == "x" else (dx, dz - way)
        here = block(part, (x + ix + 2 * NX) % NX, (z + iz + 2 * NZ) % NZ, rows_from, rows_to)
        arrival = pltpu.make_async_remote_copy(
            src_ref=here, dst_ref=here, send_sem=send_sem.at[k], recv_sem=recv_sem.at[k],
            device_id=ring[(axis, way)], device_id_type=MESH,
        )
        live[k] = [out, arrival, False]
        return k

    def arrived(k):
        if not live[k][2]:
            live[k][1].wait_recv()
            live[k][2] = True

    last_x, last_z = NX // 2, NZ // 2

    def hop(part, axis, dx, dz, step, before):
        last = last_x if axis == "x" else last_z
        keys = []
        for way, half in ((1, (0, 16)), (-1, (16, 32))):
            if before is not None:
                arrived(before[0 if way == 1 else 1])
            away = -way * (step - 1)
            ox, oz = (away, dz) if axis == "x" else (dx, away)
            lo, hi = half if step == last else (0, 32)
            keys.append(send(part, axis, way, ox, oz, lo, hi))
        return keys

    zp = {0: {1: hop("p", "z", 0, 0, 1, None)}}
    xp = hop("p", "x", 0, 0, 1, None)
    zq = {1: hop("q", "z", 0, 0, 1, None)}
    xq = {0: {1: hop("q", "x", 0, 0, 1, None)}}

    xp2 = hop("p", "x", 0, 0, 2, xp)
    zp[-1] = {1: hop("p", "z", -1, 0, 1, None)}
    zp[1] = {1: hop("p", "z", 1, 0, 1, None)}

    def advance_p(dx, step):
        zp[dx][step] = hop("p", "z", dx, 0, step, zp[dx][step - 1])

    def advance_q(step):
        arrive = zq[step - 1]
        if step <= last_z:
            zq[step] = hop("q", "z", 0, 0, step, arrive)
        else:
            arrived(arrive[0])
            arrived(arrive[1])
        for dz in ((-(step - 1), step - 1) if step <= last_z else (last_z,)):
            xq[dz] = {1: hop("q", "x", 0, dz, 1, None)}

    def finish_q(dz):
        xq[dz][2] = hop("q", "x", 0, dz, 2, xq[dz][1])

    advance_p(0, 2)
    advance_q(2)
    finish_q(0)
    arrived(xp2[0])
    arrived(xp2[1])
    zp[2] = {1: hop("p", "z", 2, 0, 1, None)}
    advance_p(-1, 2)
    advance_p(1, 2)
    advance_p(0, 3)
    advance_q(3)
    finish_q(-1)
    finish_q(1)
    advance_p(2, 2)
    advance_p(-1, 3)
    advance_p(1, 3)
    advance_p(0, 4)
    advance_q(4)
    finish_q(-2)
    finish_q(2)
    advance_p(2, 3)
    advance_p(-1, 4)
    advance_p(1, 4)
    advance_q(5)
    finish_q(-3)
    finish_q(3)
    advance_p(2, 4)
    finish_q(last_z)

    for k in live:
        arrived(k)
    for k in live:
        live[k][0].wait_send()
    for d in keep:
        d.wait()
    for d in pair[2:]:
        d.wait_recv()
    for d in pair:
        d.wait_send()


GATHER_COPIES = 76


def gather_call(lat, idx, hw, mq, iq):
    any_spec = pl.BlockSpec(memory_space=pl.ANY)
    vmem = pl.BlockSpec(memory_space=pltpu.VMEM)
    return pl.pallas_call(
        gather_kernel,
        name="gather_keys",
        out_shape=[
            jax.ShapeDtypeStruct((NX, NZ, HALF, 2 * KD), BF16),
            jax.ShapeDtypeStruct((NX, NZ, HALF, 2 * KD + IDX_DIM), BF16),
            jax.ShapeDtypeStruct((TOK, HEADS_DEV * KD), BF16),
            jax.ShapeDtypeStruct((TOK, IDX_HEADS * IDX_DIM), BF16),
            jax.ShapeDtypeStruct((TOK, 2 * IDX_HEADS), F32),
        ],
        in_specs=[vmem, vmem, vmem, any_spec, any_spec],
        out_specs=[any_spec, any_spec, any_spec, any_spec, vmem],
        scratch_shapes=[
            pltpu.VMEM((HALF, 2 * KD), BF16),
            pltpu.VMEM((HALF, 2 * KD + IDX_DIM), BF16),
            pltpu.VMEM((TOK, KPAD), BF16),
            pltpu.VMEM((TOK, KPAD), BF16),
            pltpu.VMEM((TOK, 2 * IDX_DIM), F32),
            pltpu.VMEM((16, IDX_DIM), BF16),
            pltpu.VMEM((16, IDX_DIM), BF16),
            pltpu.SemaphoreType.DMA((5,)),
            pltpu.SemaphoreType.DMA((5,)),
            pltpu.SemaphoreType.DMA((GATHER_COPIES,)),
            pltpu.SemaphoreType.DMA((GATHER_COPIES,)),
            pltpu.SemaphoreType.DMA((2,)),
        ],
        compiler_params=pltpu.CompilerParams(
            collective_id=0, has_side_effects=True, vmem_limit_bytes=VMEM_BYTES
        ),
    )(lat, idx, hw, mq, iq)


def forward_kernel(
    info, order, p_any, q_any, mq_any, mqx_any, iq_any, iqx_any, w_ref,
    tgt_ref, logit_ref, stat_ref, idx_keys_ref, idx_q_ref,
    vp, vq, vmq, vidx, keys, queries, scores, keys32, sem,
):
    c = info[4]
    copies = [
        pltpu.make_async_copy(p_any, vp, sem.at[0]),
        pltpu.make_async_copy(q_any, vq, sem.at[1]),
        pltpu.make_async_copy(mq_any.at[c], vmq.at[0], sem.at[2]),
        pltpu.make_async_copy(mqx_any, vmq.at[1], sem.at[3]),
        pltpu.make_async_copy(iq_any.at[c], vidx.at[0], sem.at[4]),
        pltpu.make_async_copy(iqx_any, vidx.at[1], sem.at[5]),
    ]
    for d in copies:
        d.start()
    copies[0].wait()
    copies[1].wait()
    pad = jnp.zeros((HALF, KPAD - KD), BF16)

    def place_keys(chip, carry):
        cx, cz = chip // NZ, chip % NZ
        for half, ref in ((0, vp), (1, vq)):
            for core in range(2):
                place = order[4 * chip + 2 * core + half]
                keys[pl.ds(pl.multiple_of(place * HALF, HALF), HALF), :] = jnp.concatenate(
                    [ref[cx, cz, :, core * KD : (core + 1) * KD], pad], axis=1
                )
        idx_rows = vq[cx, cz, :, 2 * KD :].astype(F32)
        for core in range(2):
            for half in range(2):
                place = order[4 * chip + 2 * core + half]
                at = core * 16 + half * 8
                keys32[pl.ds(pl.multiple_of(place * 8, 8), 8), :] = idx_rows[at : at + 8]
        return carry

    lax.fori_loop(0, NX * NZ, place_keys, 0)
    idx_keys_ref[...] = keys32[...].astype(BF16)
    copies[2].wait()
    copies[3].wait()
    for g in range(4):
        rows = vmq[g // 2, g % 2 * HALF : (g % 2 + 1) * HALF, :]
        for h in range(HEADS_DEV):
            queries[g, h * HALF : (h + 1) * HALF, :] = jnp.concatenate([rows[:, h * KD : (h + 1) * KD], pad], axis=1)

    lanes = HEADS_DEV * HALF
    token = lax.broadcasted_iota(jnp.int32, (256, lanes), 1) % HALF
    key_row = lax.broadcasted_iota(jnp.int32, (256, lanes), 0)
    group_of = lax.broadcasted_iota(jnp.int32, (8, 128), 1) // HALF
    tgt_ref[:, :, SLOTS - 2 :] = jnp.zeros((NY, 2, 2, 8, 128), F32)
    blocks_before = [0, 0, 0, 0]
    for g in range(4):
        pair, half = g // 2, g % 2
        place = info[g]
        total = place // 8 + 1
        first = info[2 * pair] // 8 + 1 if half else 0

        def score_block(b):
            k = keys[pl.ds(pl.multiple_of(b * 256, 256), 256), :]
            return lax.dot_general(k, queries[g], (((1,), (1,)), ((), ())), preferred_element_type=F32)

        def at(b):
            return pl.ds(pl.multiple_of((first + b) * 256, 256), 256)

        def fill(b, top):
            s = score_block(b)
            scores[at(b), :] = s
            return jnp.maximum(top, jnp.max(s.reshape(32, 8, lanes), axis=0))

        top = lax.fori_loop(0, total - 1, fill, jnp.full((8, lanes), NEG, F32))
        last = total - 1
        s = score_block(last)
        s = jnp.where(key_row + last * 256 <= token + place * HALF, s, NEG)
        scores[at(last), :] = s
        top = jnp.maximum(top, jnp.max(s.reshape(32, 8, lanes), axis=0))
        scale = SCORE_SCALE * LOG2E
        shift = jnp.max(top, axis=0, keepdims=True) * scale

        def exponentials(b, sums):
            e = jnp.exp2(scores[at(b), :] * scale - shift)
            scores[at(b), :] = e
            return sums + jnp.sum(e.reshape(32, 8, lanes), axis=0)

        sums = lax.fori_loop(0, total, exponentials, jnp.zeros((8, lanes), F32))
        weight = 1.0 / (HEADS * jnp.sum(sums, axis=0, keepdims=True))

        def head_sum(b, carry):
            for part in range(2):
                rows = pl.ds(pl.multiple_of((first + b) * 256 + part * 128, 128), 128)
                r = scores[rows, 0:128] * weight[:, 0:128]
                for lt in range(1, lanes // 128):
                    r = r + scores[rows, lt * 128 : (lt + 1) * 128] * weight[:, lt * 128 : (lt + 1) * 128]
                r = r + pltpu.roll(r, 64, 1)
                r = r + pltpu.roll(r, 32, 1)
                for y in range(NY):
                    out = r[8 * y : 8 * y + 8]
                    for a in range(1, 4):
                        out = jnp.where(group_of == a, r[32 * a + 8 * y : 32 * a + 8 * y + 8], out)
                    tgt_ref[y, pair, 2 * (first + b) + part] = out
            return carry

        lax.fori_loop(0, total, head_sum, 0)

    y = info[5]
    copies[4].wait()
    copies[5].wait()
    for g in range(4):
        rows = vidx[g // 2, g % 2 * HALF : (g % 2 + 1) * HALF, :]
        for j in range(IDX_HEADS):
            idx_q_ref[g, j * HALF : (j + 1) * HALF, :] = rows[:, j * IDX_DIM : (j + 1) * IDX_DIM]
    row_id = lax.broadcasted_iota(jnp.int32, (128, 128), 0)
    token = lax.broadcasted_iota(jnp.int32, (128, 128), 1) % HALF
    offset = row_id // 8 * HALF + row_id % 8 + 8 * y
    for g in range(4):
        place = info[g]
        total = place // 16 + 1

        def logits(b, top):
            k = idx_keys_ref[pl.ds(pl.multiple_of(b * 128, 128), 128), :]
            acc = jnp.zeros((128, 128), F32)
            for ch in range(8):
                inner = lax.dot_general(
                    k, idx_q_ref[g, ch * 256 : (ch + 1) * 256, :], (((1,), (1,)), ((), ())),
                    preferred_element_type=F32,
                )
                part = jnp.maximum(inner, 0.0) * w_ref[g, :, ch * 256 : (ch + 1) * 256]
                acc = acc + part[:, :128] + part[:, 128:]
            acc = acc + pltpu.roll(acc, 64, 1)
            acc = acc + pltpu.roll(acc, 32, 1)
            acc = jnp.where(offset + b * 512 <= token + place * HALF, acc * INDEX_NORM, NEG)
            logit_ref[g, pl.ds(pl.multiple_of(b * 128, 128), 128), :] = acc
            return jnp.maximum(top, jnp.max(acc.reshape(16, 8, 128), axis=0))

        top = lax.fori_loop(0, total, logits, jnp.full((8, 128), NEG, F32))
        top = jnp.max(top, axis=0, keepdims=True)

        def total_exp(b, sums):
            e = jnp.exp(logit_ref[g, pl.ds(pl.multiple_of(b * 128, 128), 128), :] - top)
            return sums + jnp.sum(e.reshape(16, 8, 128), axis=0)

        sums = lax.fori_loop(0, total, total_exp, jnp.zeros((8, 128), F32))
        stat_ref[g : g + 1, :] = top
        stat_ref[4 + g : 5 + g, :] = jnp.sum(sums, axis=0, keepdims=True)


def forward_call(info, order, p, q, mq, mqx, iq, iqx, w):
    any_spec = pl.BlockSpec(memory_space=pl.ANY)
    vmem = pl.BlockSpec(memory_space=pltpu.VMEM)
    smem = pl.BlockSpec(memory_space=pltpu.SMEM)
    return pl.pallas_call(
        forward_kernel,
        name="targets_and_logits",
        out_shape=[
            jax.ShapeDtypeStruct((NY, 2, SLOTS, 8, 128), F32),
            jax.ShapeDtypeStruct((4, 1024, 128), F32),
            jax.ShapeDtypeStruct((8, 128), F32),
            jax.ShapeDtypeStruct((1024, IDX_DIM), BF16),
            jax.ShapeDtypeStruct((4, IDX_HEADS * HALF, IDX_DIM), BF16),
        ],
        in_specs=[smem, smem] + [any_spec] * 6 + [vmem],
        out_specs=[vmem] * 5,
        scratch_shapes=[
            pltpu.VMEM((NX, NZ, HALF, 2 * KD), BF16),
            pltpu.VMEM((NX, NZ, HALF, 2 * KD + IDX_DIM), BF16),
            pltpu.VMEM((2, TOK, HEADS_DEV * KD), BF16),
            pltpu.VMEM((2, TOK, IDX_HEADS * IDX_DIM), BF16),
            pltpu.VMEM((HALVES * HALF, KPAD), BF16),
            pltpu.VMEM((4, HEADS_DEV * HALF, KPAD), BF16),
            pltpu.VMEM((17 * 256, HEADS_DEV * HALF), F32),
            pltpu.VMEM((1024, IDX_DIM), F32),
            pltpu.SemaphoreType.DMA((6,)),
        ],
        compiler_params=pltpu.CompilerParams(vmem_limit_bytes=VMEM_BYTES),
    )(info, order, p, q, mq, mqx, iq, iqx, w)


def exchange_kernel(tgt_ref, stat_ref, sum_ref, stats_ref, arrive, send_sem, recv_sem, stat_send, stat_recv):
    x, z, c, y = coords()
    seq = lax.axis_index("seq")
    barrier = pltpu.get_barrier_semaphore()
    for d in range(1, NY):
        pl.semaphore_signal(barrier, inc=1, device_id=(seq, (y + d) % NY), device_id_type=MESH)
    pl.semaphore_wait(barrier, NY - 1)
    sends = []
    for d in range(1, NY):
        to = (y + d) % NY
        sends.append(
            pltpu.make_async_remote_copy(
                src_ref=tgt_ref.at[to], dst_ref=arrive.at[d - 1], send_sem=send_sem.at[d - 1],
                recv_sem=recv_sem.at[d - 1], device_id=(seq, to), device_id_type=MESH,
            )
        )
        sends.append(
            pltpu.make_async_remote_copy(
                src_ref=stat_ref, dst_ref=stats_ref.at[d], send_sem=stat_send.at[d - 1],
                recv_sem=stat_recv.at[d - 1], device_id=(seq, to), device_id_type=MESH,
            )
        )
    for d in sends:
        d.start()
    stats_ref[0] = stat_ref[...]
    for d in sends:
        d.wait_recv()
    sum_ref[...] = tgt_ref[y] + arrive[0] + arrive[1] + arrive[2]
    for d in sends:
        d.wait_send()


def exchange_call(tgt, stat):
    vmem = pl.BlockSpec(memory_space=pltpu.VMEM)
    return pl.pallas_call(
        exchange_kernel,
        name="sum_targets",
        out_shape=[
            jax.ShapeDtypeStruct((2, SLOTS, 8, 128), F32),
            jax.ShapeDtypeStruct((NY, 8, 128), F32),
        ],
        in_specs=[vmem] * 2,
        out_specs=[vmem] * 2,
        scratch_shapes=[
            pltpu.VMEM((NY - 1, 2, SLOTS, 8, 128), F32),
            pltpu.SemaphoreType.DMA((NY - 1,)),
            pltpu.SemaphoreType.DMA((NY - 1,)),
            pltpu.SemaphoreType.DMA((NY - 1,)),
            pltpu.SemaphoreType.DMA((NY - 1,)),
        ],
        compiler_params=pltpu.CompilerParams(
            collective_id=1, has_side_effects=True, vmem_limit_bytes=VMEM_BYTES
        ),
    )(tgt, stat)


def backward_kernel(info, order, sum_ref, stats_ref, logit_ref, keys_ref, idx_q_ref, w_ref, out_ref, grads):
    y = info[5]
    row_id = lax.broadcasted_iota(jnp.int32, (128, 128), 0)
    token = lax.broadcasted_iota(jnp.int32, (128, 128), 1) % HALF
    offset = row_id // 8 * HALF + row_id % 8 + 8 * y
    group_of = lax.broadcasted_iota(jnp.int32, (8, 128), 1) // HALF
    grads[...] = jnp.zeros((1024, IDX_DIM), F32)
    for g in range(4):
        pair, half = g // 2, g % 2
        place = info[g]
        total = place // 16 + 1
        first = 2 * (info[2 * pair] // 8 + 1) if half else 0
        tops = [stats_ref[d, g : g + 1, :] for d in range(NY)]
        top = jnp.maximum(jnp.maximum(tops[0], tops[1]), jnp.maximum(tops[2], tops[3]))
        norm = sum(stats_ref[d, 4 + g : 5 + g, :] * jnp.exp(tops[d] - top) for d in range(NY))
        coef = GRAD_COEF / norm

        def block(b, carry):
            rows = pl.ds(pl.multiple_of(b * 128, 128), 128)
            wide = []
            for q in range(4):
                packed = sum_ref[pair, first + 4 * b + q]
                for a in range(4):
                    v = jnp.where(group_of == a, packed, 0.0)
                    v = v + pltpu.roll(v, 64, 1)
                    wide.append(v + pltpu.roll(v, 32, 1))
            target = jnp.concatenate(wide, axis=0)
            prob = jnp.exp(logit_ref[g, rows, :] - top) * coef
            scaled = jnp.where(offset + b * 512 <= token + place * HALF, prob - GRAD_COEF * target, 0.0)
            scaled = jnp.concatenate([scaled, scaled], axis=1)
            k = keys_ref[rows, :]
            acc = grads[rows, :]
            for ch in range(8):
                q_rows = idx_q_ref[g, ch * 256 : (ch + 1) * 256, :]
                inner = lax.dot_general(k, q_rows, (((1,), (1,)), ((), ())), preferred_element_type=F32)
                signal = jnp.where(inner > 0.0, scaled * w_ref[g, :, ch * 256 : (ch + 1) * 256], 0.0).astype(BF16)
                acc = acc + jnp.dot(signal, q_rows, preferred_element_type=F32)
            grads[rows, :] = acc
            return carry

        lax.fori_loop(0, total, block, 0)

    def store(chip, carry):
        for core in range(2):
            for half in range(2):
                place = order[4 * chip + 2 * core + half]
                out_ref[chip, core * 16 + half * 8 : core * 16 + half * 8 + 8, :] = grads[
                    pl.ds(pl.multiple_of(place * 8, 8), 8), :
                ]
        return carry

    lax.fori_loop(0, NX * NZ, store, 0)


def backward_call(info, order, tsum, stats, logit, keys, idx_q, w):
    vmem = pl.BlockSpec(memory_space=pltpu.VMEM)
    smem = pl.BlockSpec(memory_space=pltpu.SMEM)
    return pl.pallas_call(
        backward_kernel,
        name="key_gradients",
        out_shape=jax.ShapeDtypeStruct((NX * NZ, 32, IDX_DIM), F32),
        in_specs=[smem, smem] + [vmem] * 6,
        out_specs=vmem,
        scratch_shapes=[pltpu.VMEM((1024, IDX_DIM), F32)],
        compiler_params=pltpu.CompilerParams(vmem_limit_bytes=VMEM_BYTES),
    )(info, order, tsum, stats, logit, keys, idx_q, w)


def scatter_kernel(
    part_ref, out_ref, xa, za, xb, zb, slab_x, slab_z, tail, pieces,
    xa_sem, za_sem, xb_sem, zb_sem, piece_sem,
):
    x, z, c, y = coords()
    barrier = pltpu.get_barrier_semaphore()
    peers_x = [(seq_at((x + d) % NX, z, c), y) for d in range(1, NX)]
    peers_z = [(seq_at(x, (z + d) % NZ, c), y) for d in range(1, NZ)]
    near = [(half, core) for half in range(2) for core in range(2)]
    targets = [(seq_at(x, z, core), y // 2 + 2 * half) for half, core in near]
    sources = [(seq_at(x, z, core), 2 * (y % 2) + odd) for odd in range(2) for core in range(2)]
    for to in peers_x + peers_z:
        pl.semaphore_signal(barrier, inc=1, device_id=to, device_id_type=MESH)
    for core in range(2):
        for other in range(NY):
            @pl.when(jnp.logical_or(core != c, other != y))
            def _(core=core, other=other):
                pl.semaphore_signal(barrier, inc=1, device_id=(seq_at(x, z, core), other), device_id_type=MESH)
    pl.semaphore_wait(barrier, NX - 1 + NZ - 1 + 2 * NY - 1)

    def remote(src, dst, sems, k, to):
        d = pltpu.make_async_remote_copy(
            src_ref=src, dst_ref=dst, send_sem=sems.at[0, k], recv_sem=sems.at[1, k],
            device_id=to, device_id_type=MESH,
        )
        d.start()
        return d

    first_z = [
        remote(part_ref.at[:, (z + d) % NZ, pl.ds(16, 16)], za.at[d - 1], za_sem, d - 1, peers_z[d - 1])
        for d in range(1, NZ)
    ]
    first_x = [
        remote(part_ref.at[(x + d) % NX, :, pl.ds(0, 16)], xa.at[d - 1], xa_sem, d - 1, peers_x[d - 1])
        for d in range(1, NX)
    ]
    for d in first_x:
        d.wait_recv()
    slab_x[...] = part_ref[x, :, 0:16, :] + xa[0] + xa[1] + xa[2]
    second_z = [
        remote(slab_x.at[(z + d) % NZ], zb.at[d - 1], zb_sem, d - 1, peers_z[d - 1]) for d in range(1, NZ)
    ]
    for d in first_z:
        d.wait_recv()
    total = part_ref[:, z, 16:32, :]
    for k in range(NZ - 1):
        total = total + za[k]
    slab_z[...] = total
    second_x = [
        remote(slab_z.at[(x + d) % NX], xb.at[d - 1], xb_sem, d - 1, peers_x[d - 1]) for d in range(1, NX)
    ]
    for d in second_z:
        d.wait_recv()
    total = slab_x[z]
    for k in range(NZ - 1):
        total = total + zb[k]
    tail[0:16] = total
    for d in second_x:
        d.wait_recv()
    tail[16:32] = slab_z[x] + xb[0] + xb[1] + xb[2]

    slot = 2 * (y % 2) + c

    for k, (half, core) in enumerate(near):
        piece = tail.at[pl.ds(16 * core + 8 * half, 8)]
        local = jnp.logical_and(core == c, y // 2 + 2 * half == y)

        @pl.when(jnp.logical_not(local))
        def _(piece=piece, k=k):
            pltpu.make_async_remote_copy(
                src_ref=piece, dst_ref=pieces.at[slot], send_sem=piece_sem.at[0, k],
                recv_sem=piece_sem.at[1, slot], device_id=targets[k], device_id_type=MESH,
            ).start()

        @pl.when(local)
        def _(piece=piece):
            pieces[slot] = piece[...]

    for k, (odd, core) in enumerate([(odd, core) for odd in range(2) for core in range(2)]):
        away = jnp.logical_not(jnp.logical_and(core == c, 2 * (y % 2) + odd == y))

        @pl.when(away)
        def _(k=k, odd=odd, core=core):
            ref = pieces.at[2 * odd + core]
            pltpu.make_async_remote_copy(
                src_ref=ref, dst_ref=ref, send_sem=piece_sem.at[0, k], recv_sem=piece_sem.at[1, 2 * odd + core],
                device_id=sources[k], device_id_type=MESH,
            ).wait_recv()

    for odd in range(2):
        for core in range(2):
            out_ref[8 * odd : 8 * odd + 8, core * IDX_DIM : (core + 1) * IDX_DIM] = pieces[2 * odd + core]
    for k, (half, core) in enumerate(near):
        away = jnp.logical_not(jnp.logical_and(core == c, y // 2 + 2 * half == y))

        @pl.when(away)
        def _(k=k, half=half, core=core):
            piece = tail.at[pl.ds(16 * core + 8 * half, 8)]
            pltpu.make_async_remote_copy(
                src_ref=piece, dst_ref=pieces.at[slot], send_sem=piece_sem.at[0, k],
                recv_sem=piece_sem.at[1, slot], device_id=targets[k], device_id_type=MESH,
            ).wait_send()

    for d in first_x + first_z + second_x + second_z:
        d.wait_send()


def scatter_call(part):
    vmem = pl.BlockSpec(memory_space=pltpu.VMEM)
    return pl.pallas_call(
        scatter_kernel,
        name="sum_gradients",
        out_shape=jax.ShapeDtypeStruct((16, 2 * IDX_DIM), F32),
        in_specs=[vmem],
        out_specs=vmem,
        scratch_shapes=[
            pltpu.VMEM((NX - 1, NZ, 16, IDX_DIM), F32),
            pltpu.VMEM((NZ - 1, NX, 16, IDX_DIM), F32),
            pltpu.VMEM((NX - 1, 16, IDX_DIM), F32),
            pltpu.VMEM((NZ - 1, 16, IDX_DIM), F32),
            pltpu.VMEM((NZ, 16, IDX_DIM), F32),
            pltpu.VMEM((NX, 16, IDX_DIM), F32),
            pltpu.VMEM((32, IDX_DIM), F32),
            pltpu.VMEM((4, 8, IDX_DIM), F32),
            pltpu.SemaphoreType.DMA((2, NX - 1)),
            pltpu.SemaphoreType.DMA((2, NZ - 1)),
            pltpu.SemaphoreType.DMA((2, NX - 1)),
            pltpu.SemaphoreType.DMA((2, NZ - 1)),
            pltpu.SemaphoreType.DMA((2, 4)),
        ],
        compiler_params=pltpu.CompilerParams(
            collective_id=2, has_side_effects=True, vmem_limit_bytes=VMEM_BYTES
        ),
    )(part)


def per_device(mla_queries, latent_keys, index_queries, index_keys, head_weights, block_order):
    s = lax.axis_index("seq")
    y = lax.axis_index("head")
    c = s % 2
    p, q, mqx, iqx, hwx = gather_call(latent_keys, index_keys, head_weights, mla_queries, index_queries)
    mine = lax.dynamic_slice(block_order, (2 * s,), (2,))
    others = lax.dynamic_slice(block_order, (2 * (s + 1 - 2 * c),), (2,))
    info = jnp.concatenate([mine, others, jnp.stack([c, y]).astype(jnp.int32)])
    w = jnp.stack([head_weights, hwx]).reshape(2, 2, HALF, 2, IDX_HEADS)
    w = lax.dynamic_index_in_dim(w, c, 3, keepdims=False)
    w = w.transpose(0, 1, 3, 2).reshape(4, 1, IDX_HEADS * HALF)
    tgt, logit, stat, keys, idx_q = forward_call(info, block_order, p, q, mla_queries, mqx, index_queries, iqx, w)
    tsum, stats = exchange_call(tgt, stat)
    part = backward_call(info, block_order, tsum, stats, logit, keys, idx_q, w)
    return scatter_call(part.reshape(NX, NZ, 32, IDX_DIM))


def solution(mesh):
    return jax.shard_map(
        per_device,
        mesh=mesh,
        in_specs=(
            P(None, "seq", "head"),
            P("seq", None),
            P(None, "seq", None),
            P("seq", None),
            P("seq", None),
            P(),
        ),
        out_specs=P(("seq", "head"), None),
        check_vma=False,
    )
```

time: 1850 us -> 150 us (0.08)
  waiting for transfers between devices: 1510 us -> 0 us
  Pallas kernels: 0 us -> 144 us
  matrix products: 129 us -> 0 us
  local copies, waits for them, and re-layouts: 132 us -> 4.66 us
  other arithmetic: 49.3 us -> 0.69 us
    reduce_scatter x2 -> x0, waiting for transfers between devices: 1380 us -> none  [the longest x1 1380 us: per_device(): lax.psum_scatter(partial_value, ('seq', 'head'), scatter_dimension=0, til...]
    pallas_call x0 -> x5, Pallas kernels: none -> 144 us  [the longest x1 47.5 us: gather_call(): pl.pallas_call(gather_kernel, name='gather_keys', out_shape=[jax.ShapeDty...]
    all_gather x2 -> x0, waiting for transfers between devices: 131 us -> none  [the longest x1 67.7 us: per_device(): lax.all_gather(latent_keys, 'seq', axis=0, tiled=True)]
    dot_general x80 -> x0, matrix products: 129 us -> none  [the longest x74 120 us: block_dot(): lax.dot_general(query_rows, key_block, (((1,), (1,)), ((), ())), preferre...]
    gather x3 -> x0, local copies, waits for them, and re-layouts: 55.8 us -> none  [the longest x1 26.9 us: per_device(): ordered_latent = jnp.take(gathered_latent, rows_in_order, axis=0)]
    dynamic_slice x23 -> x2, local copies, waits for them, and re-layouts: 33.9 us -> 0.9 us  [the longest x1 0.8 us: per_device(): mine = lax.dynamic_slice(block_order, (2 * s,), (2,))]
    reduce_sum x76 -> x0, other arithmetic: 21.7 us -> none  [the longest x6 12 us: forward(): jnp.sum(jnp.maximum(inner_dot, 0.0).reshape(row_count, index_heads, kbloc...]
  transfers between devices with their start and end apart: 4 -> 0, of which waited for: 3 -> 0; matrix products, arithmetic and copies ran while one was open for 4% -> 0% of each run, Pallas kernels for 0% -> 0%
where the time goes in v1:
time: 150 us; the launch traced here: 149 us
  Pallas kernels  144 us (96%)
  local copies, waits for them, and re-layouts  4.66 us (3%)
    pallas_call x1, Pallas kernels, gather_call(): pl.pallas_call(gather_kernel, name='gather_keys', out_shape=[jax.ShapeDty...  47.5 us
    pallas_call x1, Pallas kernels, forward_call(): pl.pallas_call(forward_kernel, name='targets_and_logits', out_shape=[jax....  41.1 us
    pallas_call x1, Pallas kernels, scatter_call(): pl.pallas_call(scatter_kernel, name='sum_gradients', out_shape=jax.ShapeD...  20.9 us
    pallas_call x1, Pallas kernels, exchange_call(): pl.pallas_call(exchange_kernel, name='sum_targets', out_shape=[jax.ShapeD...  18.7 us
    pallas_call x1, Pallas kernels, backward_call(): pl.pallas_call(backward_kernel, name='key_gradients', out_shape=jax.Shape...  15.6 us

profile of v1, /device:TPU:1, one launch (start us, length us, event | category | flops | bytes accessed | tf_op | source)
XLA Modules:
  0.0 149.2 jit_solution(7761992171625567649)
XLA Ops:
  0.0 0.8 fusion.1
  0.8 0.6 pad_add_fusion.info
  1.4 0.9 stack.17
  2.3 47.5 %gather_keys.1 = (bf16[4,8,32,1152]{3,2,1,0:T(8,128)(2,1)}, bf16[4,8,32,1280]{3,2,1,0:T(8,128)(2,1)}, bf16[64,9216]{1,0:T(8,128)(2,1)}, bf16[64,8192]{1,0:T(8,128)(2,1)}, f32[64,128]{1,0:T(8,128)}) custom-call(bf16[64,1152]{1,0:T(8,128)(2,1)} %lat_ref.1, bf16[64,256]{1,0:T(8,128)(2,1)} %idx_ref.1, f32[64,128]{1,0:T(8,128)} %hw_ref.1, ...), custom_call_target="tpu_custom_call" | custom-call | tf_op jit(solution)/shard_map/gather_keys/pallas_call | solution.py:223
  49.7 0.9 stack.18
  50.6 0.1 fusion
  50.7 0.1 copy.8
  50.8 0.7 reshape.13.w_ref
  51.5 41.1 %targets_and_logits.1 = (f32[4,2,36,8,128]{4,3,2,1,0:T(8,128)}, f32[4,1024,128]{2,1,0:T(8,128)}, f32[8,128]{1,0:T(8,128)}, bf16[1024,128]{1,0:T(8,128)(2,1)}, bf16[4,2048,128]{2,1,0:T(8,128)(2,1)}) custom-call(s32[6]{0:T(128)} %pad_add_fusion.info, s32[128]{0:T(128)} %order.3, bf16[4,8,32,1152]{3,2,1,0:T(8,128)(2,1)} %get-tuple-element.17.p_any, ...), custom_call_target="tpu_custom_call" | custom-call | tf_op jit(solution)/shard_map/targets_and_logits/pallas_call | solution.py:404
  92.6 18.7 %sum_targets.1 = (f32[2,36,8,128]{3,2,1,0:T(8,128)}, f32[4,8,128]{2,1,0:T(8,128)}) custom-call(f32[4,2,36,8,128]{4,3,2,1,0:T(8,128)} %get-tuple-element.22.tgt_ref, f32[8,128]{1,0:T(8,128)} %get-tuple-element.23.stat_ref), custom_call_target="tpu_custom_call" | custom-call | tf_op jit(solution)/shard_map/sum_targets/pallas_call | solution.py:465
  111.3 15.6 %key_gradients.1 = f32[32,32,128]{2,1,0:T(8,128)} custom-call(s32[6]{0:T(128)} %pad_add_fusion.info, s32[128]{0:T(128)} %order.3, f32[2,36,8,128]{3,2,1,0:T(8,128)} %get-tuple-element.24.sum_ref, f32[4,8,128]{2,1,0:T(8,128)} %get-tuple-element.25.stats_ref, f32[4,1024,128]{2,1,0:T(8,128)} %get-tuple-element.26.logit_ref, ...), custom_call_target="tpu_custom_call" | custom-call | tf_op jit(solution)/shard_map/key_gradients/pallas_call | solution.py:544
  126.9 20.9 %sum_gradients.1 = f32[16,256]{1,0:T(8,128)} custom-call(f32[4,8,32,128]{3,2,1,0:T(8,128)} %bitcast.8), custom_call_target="tpu_custom_call" | custom-call | tf_op jit(solution)/shard_map/sum_gradients/pallas_call | solution.py:664
  147.9 1.3 copy.12

commit v2 on v1

v2 whole, which is shorter than its diff:
```python
import functools
import math

import jax
import jax.numpy as jnp
from jax import lax
from jax.experimental import pallas as pl
from jax.experimental.pallas import tpu as pltpu
from jax.sharding import PartitionSpec as P

MESH = pl.DeviceIdType.MESH
NX, NZ, NY = 4, 8, 4
HEADS = 64
HEADS_DEV = 16
KD = 576
KPAD = 640
IDX_HEADS = 64
IDX_DIM = 128
TOK = 64
HALF = 32
HALVES = 128
SLOTS = 36
SCORE_SCALE = 192.0 ** (-0.5)
LOG2E = 1.4426950408889634
INDEX_NORM = (IDX_HEADS * IDX_DIM) ** (-0.5)
GRAD_COEF = 1024.0 * INDEX_NORM
NEG = -1e30
VMEM_BYTES = 60 * 1024 * 1024
F32 = jnp.float32
BF16 = jnp.bfloat16


def coords():
    s = lax.axis_index("seq")
    y = lax.axis_index("head")
    return s // (2 * NZ), (s // 2) % NZ, s % 2, y


def seq_at(x, z, c):
    return (x * NZ + z) * 2 + c


def gather_kernel(
    lat_ref, idx_ref, hw_ref, mq_ref, iq_ref,
    p_out, q_out, mqx_ref, iqx_ref, hwx_ref,
    own_p, own_q, stage_out, stage_in, idx32, idx_stage_in, idx_stage_out,
    pair_send, pair_recv, send_sem, recv_sem, local_sem,
):
    x, z, c, y = coords()
    partner = (seq_at(x, z, 1 - c), y)
    ring = {
        ("x", 1): (seq_at((x + 1) % NX, z, c), y),
        ("x", -1): (seq_at((x + NX - 1) % NX, z, c), y),
        ("z", 1): (seq_at(x, (z + 1) % NZ, c), y),
        ("z", -1): (seq_at(x, (z + NZ - 1) % NZ, c), y),
    }
    barrier = pltpu.get_barrier_semaphore()
    for target in [partner] + list(ring.values()):
        pl.semaphore_signal(barrier, inc=1, device_id=target, device_id_type=MESH)

    lat = lat_ref[...]
    stage_out[:, 0:KD] = jnp.where(c == 0, lat[:, KD:], lat[:, :KD])
    stage_out[:, KD:] = jnp.zeros((TOK, KPAD - KD), BF16)
    idx32[...] = idx_ref[...].astype(F32)
    rows = jnp.concatenate(
        [idx32[pl.ds(pl.multiple_of(y * 8, 8), 8), :], idx32[pl.ds(pl.multiple_of(HALF + y * 8, 8), 8), :]], axis=0
    )
    idx_stage_out[...] = jnp.where(c == 0, rows[:, IDX_DIM:], rows[:, :IDX_DIM]).astype(BF16)
    pl.semaphore_wait(barrier, 5)

    def pair_copy(k, src, dst):
        return pltpu.make_async_remote_copy(
            src_ref=src, dst_ref=dst, send_sem=pair_send.at[k], recv_sem=pair_recv.at[k],
            device_id=partner, device_id_type=MESH,
        )

    pair = [
        pair_copy(0, stage_out, stage_in),
        pair_copy(1, idx_stage_out, idx_stage_in),
        pair_copy(2, mq_ref.at[1 - c], mqx_ref),
        pair_copy(3, iq_ref.at[1 - c], iqx_ref),
        pair_copy(4, hw_ref, hwx_ref),
    ]
    for d in pair:
        d.start()
    mine = jnp.where(c == 0, lat[:, :KD], lat[:, KD:])
    idx_mine = jnp.where(c == 0, rows[:, :IDX_DIM], rows[:, IDX_DIM:]).astype(BF16)
    pair[0].wait_recv()
    pair[1].wait_recv()
    other = stage_in[:, :KD]
    both = jnp.concatenate([jnp.where(c == 0, mine, other), jnp.where(c == 0, other, mine)], axis=1)
    own_p[...] = both[:HALF]
    own_q[:, : 2 * KD] = both[HALF:]
    idx_other = idx_stage_in[...]
    own_q[0:16, 2 * KD :] = jnp.where(c == 0, idx_mine, idx_other)
    own_q[16:32, 2 * KD :] = jnp.where(c == 0, idx_other, idx_mine)
    keep = [
        pltpu.make_async_copy(own_p, p_out.at[x, z], local_sem.at[0]),
        pltpu.make_async_copy(own_q, q_out.at[x, z], local_sem.at[1]),
    ]
    for d in keep:
        d.start()

    counter = [0]
    live = {}

    def block(part, ox, oz, rows_from, rows_to):
        ref = p_out if part == "p" else q_out
        return ref.at[ox, oz, pl.ds(rows_from, rows_to - rows_from)]

    def send(part, axis, way, dx, dz, rows_from, rows_to):
        k = counter[0]
        counter[0] += 1
        ox, oz = (x + dx + NX) % NX, (z + dz + NZ) % NZ
        if dx == 0 and dz == 0:
            src = (own_p if part == "p" else own_q).at[pl.ds(rows_from, rows_to - rows_from)]
        else:
            src = block(part, ox, oz, rows_from, rows_to)
        out = pltpu.make_async_remote_copy(
            src_ref=src, dst_ref=block(part, ox, oz, rows_from, rows_to),
            send_sem=send_sem.at[k], recv_sem=recv_sem.at[k], device_id=ring[(axis, way)], device_id_type=MESH,
        )
        out.start()
        ix, iz = (dx - way, dz) if axis == "x" else (dx, dz - way)
        here = block(part, (x + ix + 2 * NX) % NX, (z + iz + 2 * NZ) % NZ, rows_from, rows_to)
        arrival = pltpu.make_async_remote_copy(
            src_ref=here, dst_ref=here, send_sem=send_sem.at[k], recv_sem=recv_sem.at[k],
            device_id=ring[(axis, way)], device_id_type=MESH,
        )
        live[k] = [out, arrival, False]
        return k

    def arrived(k):
        if not live[k][2]:
            live[k][1].wait_recv()
            live[k][2] = True

    last_x, last_z = NX // 2, NZ // 2

    def hop(part, axis, dx, dz, step, before):
        last = last_x if axis == "x" else last_z
        keys = []
        for way, half in ((1, (0, 16)), (-1, (16, 32))):
            if before is not None:
                arrived(before[0 if way == 1 else 1])
            away = -way * (step - 1)
            ox, oz = (away, dz) if axis == "x" else (dx, away)
            lo, hi = half if step == last else (0, 32)
            keys.append(send(part, axis, way, ox, oz, lo, hi))
        return keys

    zp = {0: {1: hop("p", "z", 0, 0, 1, None)}}
    xp = hop("p", "x", 0, 0, 1, None)
    zq = {1: hop("q", "z", 0, 0, 1, None)}
    xq = {0: {1: hop("q", "x", 0, 0, 1, None)}}

    xp2 = hop("p", "x", 0, 0, 2, xp)
    zp[-1] = {1: hop("p", "z", -1, 0, 1, None)}
    zp[1] = {1: hop("p", "z", 1, 0, 1, None)}

    def advance_p(dx, step):
        zp[dx][step] = hop("p", "z", dx, 0, step, zp[dx][step - 1])

    def advance_q(step):
        arrive = zq[step - 1]
        if step <= last_z:
            zq[step] = hop("q", "z", 0, 0, step, arrive)
        else:
            arrived(arrive[0])
            arrived(arrive[1])
        for dz in ((-(step - 1), step - 1) if step <= last_z else (last_z,)):
            xq[dz] = {1: hop("q", "x", 0, dz, 1, None)}

    def finish_q(dz):
        xq[dz][2] = hop("q", "x", 0, dz, 2, xq[dz][1])

    advance_p(0, 2)
    advance_q(2)
    finish_q(0)
    arrived(xp2[0])
    arrived(xp2[1])
    zp[2] = {1: hop("p", "z", 2, 0, 1, None)}
    advance_p(-1, 2)
    advance_p(1, 2)
    advance_p(0, 3)
    advance_q(3)
    finish_q(-1)
    finish_q(1)
    advance_p(2, 2)
    advance_p(-1, 3)
    advance_p(1, 3)
    advance_p(0, 4)
    advance_q(4)
    finish_q(-2)
    finish_q(2)
    advance_p(2, 3)
    advance_p(-1, 4)
    advance_p(1, 4)
    advance_q(5)
    finish_q(-3)
    finish_q(3)
    advance_p(2, 4)
    finish_q(last_z)

    for k in live:
        arrived(k)
    for k in live:
        live[k][0].wait_send()
    for d in keep:
        d.wait()
    for d in pair[2:]:
        d.wait_recv()
    for d in pair:
        d.wait_send()


GATHER_COPIES = 76


def gather_call(lat, idx, hw, mq, iq):
    any_spec = pl.BlockSpec(memory_space=pl.ANY)
    vmem = pl.BlockSpec(memory_space=pltpu.VMEM)
    return pl.pallas_call(
        gather_kernel,
        name="gather_keys",
        out_shape=[
            jax.ShapeDtypeStruct((NX, NZ, HALF, 2 * KD), BF16),
            jax.ShapeDtypeStruct((NX, NZ, HALF, 2 * KD + IDX_DIM), BF16),
            jax.ShapeDtypeStruct((TOK, HEADS_DEV * KD), BF16),
            jax.ShapeDtypeStruct((TOK, IDX_HEADS * IDX_DIM), BF16),
            jax.ShapeDtypeStruct((TOK, 2 * IDX_HEADS), F32),
        ],
        in_specs=[vmem, vmem, vmem, any_spec, any_spec],
        out_specs=[any_spec, any_spec, any_spec, any_spec, vmem],
        scratch_shapes=[
            pltpu.VMEM((HALF, 2 * KD), BF16),
            pltpu.VMEM((HALF, 2 * KD + IDX_DIM), BF16),
            pltpu.VMEM((TOK, KPAD), BF16),
            pltpu.VMEM((TOK, KPAD), BF16),
            pltpu.VMEM((TOK, 2 * IDX_DIM), F32),
            pltpu.VMEM((16, IDX_DIM), BF16),
            pltpu.VMEM((16, IDX_DIM), BF16),
            pltpu.SemaphoreType.DMA((5,)),
            pltpu.SemaphoreType.DMA((5,)),
            pltpu.SemaphoreType.DMA((GATHER_COPIES,)),
            pltpu.SemaphoreType.DMA((GATHER_COPIES,)),
            pltpu.SemaphoreType.DMA((2,)),
        ],
        compiler_params=pltpu.CompilerParams(
            collective_id=0, has_side_effects=True, vmem_limit_bytes=VMEM_BYTES
        ),
    )(lat, idx, hw, mq, iq)


ENTRIES = 9


def entry_table(places):
    i = jnp.arange(ENTRIES, dtype=jnp.int32)[None, :]
    k = i - 5
    flip = places[:, :1] // 16 + 1 > k
    early = (i == 0) | ((i > 5) & flip)
    block = jnp.where(i == 0, 0, jnp.where(i < 6, i - 1, jnp.where(flip, k, 8 - k)))
    group = 2 * jnp.arange(2, dtype=jnp.int32)[:, None] + jnp.where(early, 0, 1)
    limit = jnp.where(early, places[:, :1], places[:, 1:]) * HALF - block * 512
    return jnp.stack([early.astype(jnp.int32), group, block, limit]).reshape(-1)


def entry(table, pair, i):
    return [table[(field * 2 + pair) * ENTRIES + i] for field in range(4)]


def mask_of(flag, shape):
    return jnp.zeros(shape, jnp.int32) + flag > 0


def sort_keys(inverse, pq, keys, keys32):
    pad = jnp.zeros((HALF, KPAD - KD), BF16)

    def step(p, carry):
        slot = inverse[p]
        chip, core, half = slot // 4, slot // 2 % 2, slot % 2
        first, second = pq[half, chip, :, 0:KD], pq[half, chip, :, KD : 2 * KD]
        at = pl.ds(pl.multiple_of(p * HALF, HALF), HALF)
        keys[at, :] = jnp.concatenate([jnp.where(core == 0, first, second), pad], axis=1)
        idx_rows = pq[1, chip, :, 2 * KD :].astype(F32)
        idx_rows = jnp.where(core == 0, idx_rows[0:16], idx_rows[16:32])
        idx_rows = jnp.where(half == 0, idx_rows[0:8], idx_rows[8:16])
        keys32[pl.ds(pl.multiple_of(p * 8, 8), 8), :] = idx_rows
        return carry

    lax.fori_loop(0, HALVES, step, 0, unroll=2)


def split_heads(vmq, queries):
    pad = jnp.zeros((HALF, KPAD - KD), BF16)
    for g in range(4):
        rows = pl.ds(g % 2 * HALF, HALF)
        for h in range(HEADS_DEV):
            queries[g, h * HALF : (h + 1) * HALF, :] = jnp.concatenate(
                [vmq[g // 2, rows, h * KD : (h + 1) * KD], pad], axis=1
            )


LANES = HEADS_DEV * HALF
EXP_SCALE = SCORE_SCALE * LOG2E


def score_step(table, pair, i, keys, queries, scores, tops):
    early, g, block, limit = entry(table, pair, i)
    early = mask_of(early, (8, LANES))
    k = keys[pl.ds(pl.multiple_of(block * 512, 512), 512), :]
    s = lax.dot_general(k, queries[g], (((1,), (1,)), ((), ())), preferred_element_type=F32)
    row = lax.broadcasted_iota(jnp.int32, (512, LANES), 0)
    token = lax.broadcasted_iota(jnp.int32, (512, LANES), 1) % HALF
    s = jnp.where(row - token <= limit, s, NEG)
    scores[pair, pl.ds(pl.multiple_of(i * 512, 512), 512), :] = s
    m = jnp.max(s.reshape(64, 8, LANES), axis=0)
    return (
        jnp.where(early, jnp.maximum(tops[0], m), tops[0]),
        jnp.where(early, tops[1], jnp.maximum(tops[1], m)),
    )


def exp_step(table, pair, i, scores, shifts, sums):
    early = entry(table, pair, i)[0]
    row = mask_of(early, (1, LANES))
    early = mask_of(early, (8, LANES))
    at = pl.ds(pl.multiple_of(i * 512, 512), 512)
    e = jnp.exp2(scores[pair, at, :] * EXP_SCALE - jnp.where(row, shifts[0], shifts[1]))
    scores[pair, at, :] = e
    m = jnp.sum(e.reshape(64, 8, LANES), axis=0)
    return (sums[0] + jnp.where(early, m, 0.0), sums[1] + jnp.where(early, 0.0, m))


def head_step(table, pair, i, scores, weights, tgt_ref):
    early = mask_of(entry(table, pair, i)[0], (1, LANES))
    group_of = lax.broadcasted_iota(jnp.int32, (8, 128), 1) // HALF
    weight = jnp.where(early, weights[0], weights[1])
    for part in range(4):
        rows = pl.ds(pl.multiple_of(i * 512 + part * 128, 128), 128)
        r = scores[pair, rows, 0:128] * weight[:, 0:128]
        for lt in range(1, LANES // 128):
            r = r + scores[pair, rows, lt * 128 : (lt + 1) * 128] * weight[:, lt * 128 : (lt + 1) * 128]
        r = r + pltpu.roll(r, 64, 1)
        r = r + pltpu.roll(r, 32, 1)
        for y in range(NY):
            out = r[8 * y : 8 * y + 8]
            for a in range(1, 4):
                out = jnp.where(group_of == a, r[32 * a + 8 * y : 32 * a + 8 * y + 8], out)
            tgt_ref[y, pair, 4 * i + part] = out


def start_tops():
    return (jnp.full((8, LANES), NEG, F32),) * 2


def start_sums():
    return (jnp.zeros((8, LANES), F32),) * 2


def shifts_of(tops):
    return tuple(jnp.max(t, axis=0, keepdims=True) * EXP_SCALE for t in tops)


def weights_of(sums):
    return tuple(1.0 / (HEADS * jnp.sum(t, axis=0, keepdims=True)) for t in sums)


def targets(table, keys, queries, scores, tgt_ref):
    tops0 = lax.fori_loop(0, 9, lambda i, t: score_step(table, 0, i, keys, queries, scores, t), start_tops())
    shifts0 = shifts_of(tops0)

    def both(i, carry):
        tops, sums = carry
        tops = score_step(table, 1, i, keys, queries, scores, tops)
        return tops, exp_step(table, 0, i, scores, shifts0, sums)

    tops1, sums0 = lax.fori_loop(0, 9, both, (start_tops(), start_sums()))
    shifts1, weights0 = shifts_of(tops1), weights_of(sums0)

    def later(i, sums):
        head_step(table, 0, i, scores, weights0, tgt_ref)
        return exp_step(table, 1, i, scores, shifts1, sums)

    weights1 = weights_of(lax.fori_loop(0, 9, later, start_sums()))

    def last(i, carry):
        head_step(table, 1, i, scores, weights1, tgt_ref)
        return carry

    lax.fori_loop(0, 9, last, 0)


def target_kernel(
    info, table, inverse, p_any, q_any, mq_any, mqx_any, tgt_ref, idx_keys_ref, pq, vmq, keys, queries, scores, keys32, sem
):
    copies = [
        pltpu.make_async_copy(mq_any.at[info[0]], vmq.at[0], sem.at[2]),
        pltpu.make_async_copy(mqx_any, vmq.at[1], sem.at[3]),
        pltpu.make_async_copy(p_any, pq.at[0, :, :, pl.ds(0, 2 * KD)], sem.at[0]),
        pltpu.make_async_copy(q_any, pq.at[1], sem.at[1]),
    ]
    for d in copies:
        d.start()
    copies[0].wait()
    copies[1].wait()
    split_heads(vmq, queries)
    copies[2].wait()
    copies[3].wait()
    sort_keys(inverse, pq, keys, keys32)
    idx_keys_ref[...] = keys32[...].astype(BF16).reshape(8, 128, IDX_DIM)
    targets(table, keys, queries, scores, tgt_ref)


def target_call(info, table, inverse, p, q, mq, mqx):
    any_spec = pl.BlockSpec(memory_space=pl.ANY)
    vmem = pl.BlockSpec(memory_space=pltpu.VMEM)
    smem = pl.BlockSpec(memory_space=pltpu.SMEM)
    return pl.pallas_call(
        target_kernel,
        name="targets",
        out_shape=[
            jax.ShapeDtypeStruct((NY, 2, SLOTS, 8, 128), F32),
            jax.ShapeDtypeStruct((8, 128, IDX_DIM), BF16),
        ],
        in_specs=[smem, smem, smem] + [any_spec] * 4,
        out_specs=[vmem] * 2,
        scratch_shapes=[
            pltpu.VMEM((2, NX * NZ, HALF, 2 * KD + IDX_DIM), BF16),
            pltpu.VMEM((2, TOK, HEADS_DEV * KD), BF16),
            pltpu.VMEM((HALVES * HALF, KPAD), BF16),
            pltpu.VMEM((4, LANES, KPAD), BF16),
            pltpu.VMEM((2, 9 * 512, LANES), F32),
            pltpu.VMEM((1024, IDX_DIM), F32),
            pltpu.SemaphoreType.DMA((4,)),
        ],
        compiler_params=pltpu.CompilerParams(vmem_limit_bytes=VMEM_BYTES),
    )(info, table, inverse, p, q, mq, mqx)


def split_index_heads(vidx, idx_q):
    for g in range(4):
        for j in range(IDX_HEADS):
            idx_q[g, j * HALF : (j + 1) * HALF, :] = vidx[
                g // 2, g % 2 * HALF : (g % 2 + 1) * HALF, j * IDX_DIM : (j + 1) * IDX_DIM
            ]


def logit_step(table, pair, i, y, idx_keys, idx_q, w_ref, inner_ref, logit_ref, tops):
    early, g, block, limit = entry(table, pair, i)
    early = mask_of(early, (8, 128))
    k = idx_keys[block]
    acc = jnp.zeros((128, 128), F32)
    for ch in range(8):
        cut = slice(ch * 256, (ch + 1) * 256)
        inner = lax.dot_general(k, idx_q[g, cut, :], (((1,), (1,)), ((), ())), preferred_element_type=F32)
        inner_ref[pair, i, :, cut] = inner.astype(BF16)
        part = jnp.maximum(inner, 0.0) * w_ref[g, :, cut]
        acc = acc + part[:, :128] + part[:, 128:]
    acc = acc + pltpu.roll(acc, 64, 1)
    acc = acc + pltpu.roll(acc, 32, 1)
    row = lax.broadcasted_iota(jnp.int32, (128, 128), 0)
    token = lax.broadcasted_iota(jnp.int32, (128, 128), 1) % HALF
    offset = row // 8 * HALF + row % 8 - token
    acc = jnp.where(offset <= limit - 8 * y, acc * INDEX_NORM, NEG)
    logit_ref[pair, i] = acc
    m = jnp.max(acc.reshape(16, 8, 128), axis=0)
    return (
        jnp.where(early, jnp.maximum(tops[0], m), tops[0]),
        jnp.where(early, tops[1], jnp.maximum(tops[1], m)),
    )


def logit_stats(table, pair, logit_ref, stat_ref, tops):
    tops = [jnp.max(t, axis=0, keepdims=True) for t in tops]

    def step(i, sums):
        early = entry(table, pair, i)[0]
        row = mask_of(early, (1, 128))
        early = mask_of(early, (8, 128))
        e = jnp.exp(logit_ref[pair, i] - jnp.where(row, tops[0], tops[1]))
        e = jnp.sum(e.reshape(16, 8, 128), axis=0)
        return (sums[0] + jnp.where(early, e, 0.0), sums[1] + jnp.where(early, 0.0, e))

    sums = lax.fori_loop(0, 9, step, (jnp.zeros((8, 128), F32),) * 2, unroll=3)
    for half in range(2):
        g = 2 * pair + half
        stat_ref[g : g + 1, :] = tops[half]
        stat_ref[4 + g : 5 + g, :] = jnp.sum(sums[half], axis=0, keepdims=True)


def norms_of(stats_ref, g):
    tops = [stats_ref[d, g : g + 1, :] for d in range(NY)]
    top = jnp.maximum(jnp.maximum(tops[0], tops[1]), jnp.maximum(tops[2], tops[3]))
    norm = sum(stats_ref[d, 4 + g : 5 + g, :] * jnp.exp(tops[d] - top) for d in range(NY))
    return top, GRAD_COEF / norm


def gradient_step(table, pair, i, y, idx_q, w_ref, inner_ref, logit_ref, tgt_ref, arrive, norms, grad_ref):
    early, g, block, limit = entry(table, pair, i)
    early = mask_of(early, (1, 128))
    group_of = lax.broadcasted_iota(jnp.int32, (8, 128), 1) // HALF
    wide = []
    for part in range(4):
        at = 4 * i + part
        packed = tgt_ref[y, pair, at] + arrive[0, pair, at] + arrive[1, pair, at] + arrive[2, pair, at]
        for a in range(4):
            v = jnp.where(group_of == a, packed, 0.0)
            v = v + pltpu.roll(v, 64, 1)
            wide.append(v + pltpu.roll(v, 32, 1))
    target = jnp.concatenate(wide, axis=0)
    top = jnp.where(early, norms[0][0], norms[1][0])
    coef = jnp.where(early, norms[0][1], norms[1][1])
    row = lax.broadcasted_iota(jnp.int32, (128, 128), 0)
    token = lax.broadcasted_iota(jnp.int32, (128, 128), 1) % HALF
    offset = row // 8 * HALF + row % 8 - token
    seen = offset <= limit - 8 * y
    scaled = jnp.where(seen, jnp.exp(logit_ref[pair, i] - top) * coef - GRAD_COEF * target, 0.0)
    scaled = jnp.concatenate([scaled, scaled], axis=1)
    acc = jnp.zeros((128, IDX_DIM), F32)
    zero = jnp.zeros((), BF16)
    for ch in range(8):
        cut = slice(ch * 256, (ch + 1) * 256)
        signal = (scaled * w_ref[g, :, cut]).astype(BF16)
        signal = jnp.where(inner_ref[pair, i, :, cut] > zero, signal, zero)
        acc = acc + jnp.dot(signal, idx_q[g, cut, :], preferred_element_type=F32)
    grad_ref[pair, i] = acc


def collect_gradients(table, order, grad_ref, sorted_ref, part_ref):
    total = [grad_ref[0, 0] + grad_ref[1, 0] + grad_ref[0, 1] + grad_ref[1, 1]]
    total += [grad_ref[0, b + 1] + grad_ref[1, b + 1] for b in range(1, 5)] + [0.0] * 3
    for pair in range(2):
        for k in range(1, 4):
            flip = mask_of(entry(table, pair, k + 5)[0], (128, IDX_DIM))
            d = grad_ref[pair, k + 5]
            total[k] = total[k] + jnp.where(flip, d, 0.0)
            total[8 - k] = total[8 - k] + jnp.where(flip, 0.0, d)
    for b in range(8):
        sorted_ref[b * 16 : (b + 1) * 16] = total[b].reshape(16, 8, IDX_DIM)

    def store(chip, carry):
        for core in range(2):
            for half in range(2):
                place = order[4 * chip + 2 * core + half]
                rows = sorted_ref[place]
                part_ref[chip // NZ, chip % NZ, core * 16 + half * 8 : core * 16 + half * 8 + 8, :] = rows
        return carry

    lax.fori_loop(0, NX * NZ, store, 0, unroll=2)


def scatter(
    x, z, c, y, peers_x, peers_z, remote, part_ref, out_ref, xa, za, xb, zb, slab_x, slab_z, tail, pieces,
    xa_sem, za_sem, xb_sem, zb_sem, piece_sem,
):
    near = [(half, core) for half in range(2) for core in range(2)]
    targets = [(seq_at(x, z, core), y // 2 + 2 * half) for half, core in near]
    sources = [(seq_at(x, z, core), 2 * (y % 2) + odd) for odd in range(2) for core in range(2)]
    first_z = [
        remote(part_ref.at[:, (z + d) % NZ, pl.ds(16, 16)], za.at[d - 1], za_sem.at[0, d - 1], za_sem.at[1, d - 1], peers_z[d - 1])
        for d in range(1, NZ)
    ]
    first_x = [
        remote(part_ref.at[(x + d) % NX, :, pl.ds(0, 16)], xa.at[d - 1], xa_sem.at[0, d - 1], xa_sem.at[1, d - 1], peers_x[d - 1])
        for d in range(1, NX)
    ]
    for d in first_x:
        d.wait_recv()
    slab_x[...] = part_ref[x, :, 0:16, :] + xa[0] + xa[1] + xa[2]
    second_z = [
        remote(slab_x.at[(z + d) % NZ], zb.at[d - 1], zb_sem.at[0, d - 1], zb_sem.at[1, d - 1], peers_z[d - 1]) for d in range(1, NZ)
    ]
    for d in first_z:
        d.wait_recv()
    total = part_ref[:, z, 16:32, :]
    for k in range(NZ - 1):
        total = total + za[k]
    slab_z[...] = total
    second_x = [
        remote(slab_z.at[(x + d) % NX], xb.at[d - 1], xb_sem.at[0, d - 1], xb_sem.at[1, d - 1], peers_x[d - 1]) for d in range(1, NX)
    ]
    for d in second_z:
        d.wait_recv()
    total = slab_x[z]
    for k in range(NZ - 1):
        total = total + zb[k]
    tail[0:16] = total
    for d in second_x:
        d.wait_recv()
    tail[16:32] = slab_z[x] + xb[0] + xb[1] + xb[2]

    slot = 2 * (y % 2) + c

    for k, (half, core) in enumerate(near):
        piece = tail.at[pl.ds(16 * core + 8 * half, 8)]
        local = jnp.logical_and(core == c, y // 2 + 2 * half == y)

        @pl.when(jnp.logical_not(local))
        def _(piece=piece, k=k):
            pltpu.make_async_remote_copy(
                src_ref=piece, dst_ref=pieces.at[slot], send_sem=piece_sem.at[0, k],
                recv_sem=piece_sem.at[1, slot], device_id=targets[k], device_id_type=MESH,
            ).start()

        @pl.when(local)
        def _(piece=piece):
            pieces[slot] = piece[...]

    for k, (odd, core) in enumerate([(odd, core) for odd in range(2) for core in range(2)]):
        away = jnp.logical_not(jnp.logical_and(core == c, 2 * (y % 2) + odd == y))

        @pl.when(away)
        def _(k=k, odd=odd, core=core):
            ref = pieces.at[2 * odd + core]
            pltpu.make_async_remote_copy(
                src_ref=ref, dst_ref=ref, send_sem=piece_sem.at[0, k], recv_sem=piece_sem.at[1, 2 * odd + core],
                device_id=sources[k], device_id_type=MESH,
            ).wait_recv()

    for odd in range(2):
        for core in range(2):
            out_ref[8 * odd : 8 * odd + 8, core * IDX_DIM : (core + 1) * IDX_DIM] = pieces[2 * odd + core]
    for k, (half, core) in enumerate(near):
        away = jnp.logical_not(jnp.logical_and(core == c, y // 2 + 2 * half == y))

        @pl.when(away)
        def _(k=k, half=half, core=core):
            piece = tail.at[pl.ds(16 * core + 8 * half, 8)]
            pltpu.make_async_remote_copy(
                src_ref=piece, dst_ref=pieces.at[slot], send_sem=piece_sem.at[0, k],
                recv_sem=piece_sem.at[1, slot], device_id=targets[k], device_id_type=MESH,
            ).wait_send()

    for d in first_x + first_z + second_x + second_z:
        d.wait_send()


def index_kernel(
    table, order, tgt_ref, iq_any, iqx_any, idx_keys, w_ref, out_ref,
    vidx, idx_q, inner_ref, logit_ref, stat_ref, stats_ref, arrive, grad_ref, sorted_ref, part_ref,
    xa, za, xb, zb, slab_x, slab_z, tail, pieces,
    load_sem, tgt_send, tgt_recv, stat_send, stat_recv, xa_sem, za_sem, xb_sem, zb_sem, piece_sem,
):
    x, z, c, y = coords()
    seq = lax.axis_index("seq")
    barrier = pltpu.get_barrier_semaphore()
    peers_y = [(seq, (y + d) % NY) for d in range(1, NY)]
    peers_x = [(seq_at((x + d) % NX, z, c), y) for d in range(1, NX)]
    peers_z = [(seq_at(x, (z + d) % NZ, c), y) for d in range(1, NZ)]
    other = [(seq_at(x, z, 1 - c), t) for t in range(NY)]
    for to in peers_x + peers_z + peers_y + other:
        pl.semaphore_signal(barrier, inc=1, device_id=to, device_id_type=MESH)
    loads = [
        pltpu.make_async_copy(iq_any.at[c], vidx.at[0], load_sem.at[0]),
        pltpu.make_async_copy(iqx_any, vidx.at[1], load_sem.at[1]),
    ]
    for d in loads:
        d.start()
    pl.semaphore_wait(barrier, NX - 1 + NZ - 1 + 2 * NY - 1)

    def remote(src, dst, send, recv, to):
        d = pltpu.make_async_remote_copy(
            src_ref=src, dst_ref=dst, send_sem=send, recv_sem=recv, device_id=to, device_id_type=MESH
        )
        d.start()
        return d

    tgt_copies = [
        [
            remote(
                tgt_ref.at[(y + d) % NY, pair], arrive.at[d - 1, pair], tgt_send.at[pair, d - 1],
                tgt_recv.at[pair, d - 1], peers_y[d - 1],
            )
            for d in range(1, NY)
        ]
        for pair in range(2)
    ]
    for d in loads:
        d.wait()
    split_index_heads(vidx, idx_q)
    start = (jnp.full((8, 128), NEG, F32),) * 2
    for pair in range(2):
        tops = lax.fori_loop(
            0, 9,
            lambda i, t: logit_step(table, pair, i, y, idx_keys, idx_q, w_ref, inner_ref, logit_ref, t),
            start,
        )
        logit_stats(table, pair, logit_ref, stat_ref, tops)
    stat_copies = [
        remote(stat_ref, stats_ref.at[d], stat_send.at[d - 1], stat_recv.at[d - 1], peers_y[d - 1])
        for d in range(1, NY)
    ]
    stats_ref[0] = stat_ref[...]
    for d in stat_copies:
        d.wait_recv()
    for pair in range(2):
        norms = [norms_of(stats_ref, 2 * pair + half) for half in range(2)]
        for d in tgt_copies[pair]:
            d.wait_recv()

        def step(i, carry):
            gradient_step(
                table, pair, i, y, idx_q, w_ref, inner_ref, logit_ref, tgt_ref, arrive, norms, grad_ref
            )
            return carry

        lax.fori_loop(0, 9, step, 0)
    collect_gradients(table, order, grad_ref, sorted_ref, part_ref)
    scatter(
        x, z, c, y, peers_x, peers_z, remote, part_ref, out_ref, xa, za, xb, zb, slab_x, slab_z, tail, pieces,
        xa_sem, za_sem, xb_sem, zb_sem, piece_sem,
    )
    for d in stat_copies + tgt_copies[0] + tgt_copies[1]:
        d.wait_send()


def index_call(table, order, tgt, iq, iqx, idx_keys, w):
    any_spec = pl.BlockSpec(memory_space=pl.ANY)
    vmem = pl.BlockSpec(memory_space=pltpu.VMEM)
    smem = pl.BlockSpec(memory_space=pltpu.SMEM)
    dma = pltpu.SemaphoreType.DMA
    return pl.pallas_call(
        index_kernel,
        name="indexer",
        out_shape=jax.ShapeDtypeStruct((16, 2 * IDX_DIM), F32),
        in_specs=[smem, smem, vmem, any_spec, any_spec, vmem, vmem],
        out_specs=vmem,
        scratch_shapes=[
            pltpu.VMEM((2, TOK, IDX_HEADS * IDX_DIM), BF16),
            pltpu.VMEM((4, IDX_HEADS * HALF, IDX_DIM), BF16),
            pltpu.VMEM((2, 9, 128, IDX_HEADS * HALF), BF16),
            pltpu.VMEM((2, 9, 128, 128), F32),
            pltpu.VMEM((8, 128), F32),
            pltpu.VMEM((NY, 8, 128), F32),
            pltpu.VMEM((NY - 1, 2, SLOTS, 8, 128), F32),
            pltpu.VMEM((2, 9, 128, IDX_DIM), F32),
            pltpu.VMEM((HALVES, 8, IDX_DIM), F32),
            pltpu.VMEM((NX, NZ, 32, IDX_DIM), F32),
            pltpu.VMEM((NX - 1, NZ, 16, IDX_DIM), F32),
            pltpu.VMEM((NZ - 1, NX, 16, IDX_DIM), F32),
            pltpu.VMEM((NX - 1, 16, IDX_DIM), F32),
            pltpu.VMEM((NZ - 1, 16, IDX_DIM), F32),
            pltpu.VMEM((NZ, 16, IDX_DIM), F32),
            pltpu.VMEM((NX, 16, IDX_DIM), F32),
            pltpu.VMEM((32, IDX_DIM), F32),
            pltpu.VMEM((4, 8, IDX_DIM), F32),
            dma((2,)),
            dma((2, NY - 1)),
            dma((2, NY - 1)),
            dma((NY - 1,)),
            dma((NY - 1,)),
            dma((2, NX - 1)),
            dma((2, NZ - 1)),
            dma((2, NX - 1)),
            dma((2, NZ - 1)),
            dma((2, 4)),
        ],
        compiler_params=pltpu.CompilerParams(
            collective_id=1, has_side_effects=True, vmem_limit_bytes=VMEM_BYTES
        ),
    )(table, order, tgt, iq, iqx, idx_keys, w)


def per_device(mla_queries, latent_keys, index_queries, index_keys, head_weights, block_order):
    s = lax.axis_index("seq")
    y = lax.axis_index("head")
    c = s % 2
    p, q, mqx, iqx, hwx = gather_call(latent_keys, index_keys, head_weights, mla_queries, index_queries)
    mine = lax.dynamic_slice(block_order, (2 * s,), (2,))
    others = lax.dynamic_slice(block_order, (2 * (s + 1 - 2 * c),), (2,))
    table = entry_table(jnp.stack([mine, others]))
    info = jnp.stack([c, y]).astype(jnp.int32)
    w = jnp.stack([head_weights, hwx]).reshape(2, 2, HALF, 2, IDX_HEADS)
    w = lax.dynamic_index_in_dim(w, c, 3, keepdims=False)
    w = w.transpose(0, 1, 3, 2).reshape(4, 1, IDX_HEADS * HALF)
    slots = jnp.arange(HALVES, dtype=jnp.int32)
    inverse = jnp.sum(jnp.where(block_order[None, :] == slots[:, None], slots[None, :], 0), axis=1)
    p = p.reshape(NX * NZ, HALF, 2 * KD)
    q = q.reshape(NX * NZ, HALF, 2 * KD + IDX_DIM)
    tgt, idx_keys = target_call(info, table, inverse, p, q, mla_queries, mqx)
    return index_call(table, block_order, tgt, index_queries, iqx, idx_keys, w)


def solution(mesh):
    return jax.shard_map(
        per_device,
        mesh=mesh,
        in_specs=(
            P(None, "seq", "head"),
            P("seq", None),
            P(None, "seq", None),
            P("seq", None),
            P("seq", None),
            P(),
        ),
        out_specs=P(("seq", "head"), None),
        check_vma=False,
    )
```

time: 150 us -> 130 us (0.87)
  Pallas kernels: 144 us -> 124 us
    pallas_call x4 -> x2, Pallas kernels: 96.3 us -> 76.8 us  [the longest x1 46.2 us: index_call(): pl.pallas_call(index_kernel, name='indexer', out_shape=jax.ShapeDtypeStru...]
    another operation x2, local copies, waits for them, and re-layouts: 1.71 us -> 0.19 us  [per_device(): w = jnp.stack([head_weights, hwx]).reshape(2, 2, HALF, 2, IDX_HEADS)]
where the time goes in v2:
time: 130 us
  Pallas kernels  124 us (95%)
  local copies, waits for them, and re-layouts  3.75 us (3%)
  other arithmetic  1.67 us (1%)
    pallas_call x1, Pallas kernels, gather_call(): pl.pallas_call(gather_kernel, name='gather_keys', out_shape=[jax.ShapeDty...  47.3 us
    pallas_call x1, Pallas kernels, index_call(): pl.pallas_call(index_kernel, name='indexer', out_shape=jax.ShapeDtypeStru...  46.2 us
    pallas_call x1, Pallas kernels, target_call(): pl.pallas_call(target_kernel, name='targets', out_shape=[jax.ShapeDtypeSt...  30.6 us

profile of v2, /device:TPU:1, one launch (start us, length us, event | category | flops | bytes accessed | tf_op | source)
XLA Modules:
  0.0 129.7 jit_solution(17713177521573692103)
XLA Ops:
  0.0 0.8 dynamic-slice_bitcast_fusion.1
  0.8 0.2 slice_reduce_fusion.1
  1.0 0.1 fusion.4
  1.1 0.0 copy-start.2
  1.1 0.1 multiply_subtract_fusion
  1.2 0.6 reshape.697.table
  1.8 0.6 pad_add_fusion.2.info
  2.4 47.3 %gather_keys.1 = (bf16[4,8,32,1152]{3,2,1,0:T(8,128)(2,1)}, bf16[4,8,32,1280]{3,2,1,0:T(8,128)(2,1)}, bf16[64,9216]{1,0:T(8,128)(2,1)}, bf16[64,8192]{1,0:T(8,128)(2,1)}, f32[64,128]{1,0:T(8,128)}) custom-call(bf16[64,1152]{1,0:T(8,128)(2,1)} %lat_ref.1, bf16[64,256]{1,0:T(8,128)(2,1)} %idx_ref.1, f32[64,128]{1,0:T(8,128)} %hw_ref.1, ...), custom_call_target="tpu_custom_call" | custom-call | tf_op jit(solution)/shard_map/gather_keys/pallas_call | solution.py:223
  49.7 0.0 copy-done.2
  49.7 0.6 select_reduce_fusion.inverse
  50.4 0.0 copy-start.1
  50.4 0.0 copy-start
  50.4 30.6 %targets.1 = (f32[4,2,36,8,128]{4,3,2,1,0:T(8,128)}, bf16[8,128,128]{2,1,0:T(8,128)(2,1)}) custom-call(s32[2]{0:T(128)} %pad_add_fusion.2.info, s32[72]{0:T(128)} %reshape.697.table, s32[128]{0:T(128)} %select_reduce_fusion.inverse, bf16[32,32,1152]{2,1,0:T(8,128)(2,1)} %bitcast.14, bf16[32,32,1280]{2,1,0:T(8,128)(2,1)} %bitcast.13, ...), custom_call_target="tpu_custom_call" | custom-call | tf_op jit(solution)/shard_map/targets/pallas_call | solution.py:420
  81.0 0.0 copy-done.1
  81.0 0.1 stack.42
  81.1 0.0 copy-done
  81.1 0.1 stack.41
  81.2 0.1 fusion
  81.3 0.1 copy.10
  81.5 0.7 reshape.701.w_ref
  82.2 46.2 %indexer.1 = f32[16,256]{1,0:T(8,128)} custom-call(s32[72]{0:T(128)} %reshape.697.table, s32[128]{0:T(128)} %order.1, f32[4,2,36,8,128]{4,3,2,1,0:T(8,128)} %get-tuple-element.15.tgt_ref, bf16[2,64,8192]{2,1,0:T(8,128)(2,1)} %iq_any.1, bf16[64,8192]{1,0:T(8,128)(2,1)} %get-tuple-element.16.iqx_any, bf16[8,128,128]{2,1,0:T(8,128)(2,1)} %get-tuple-element.17.idx_keys, ...), custom_call_target="tpu_custom_call" | custom-call | tf_op jit(solution)/shard_map/indexer/pallas_call | solution.py:724
  128.3 1.3 %copy.13 = f32[16,256]{1,0:T(8,128)} copy(f32[16,256]{1,0:T(8,128)} %indexer.1) | data formatting | bytes 32768
  (7 shorter events, 0.0 us)
Async XLA Ops:
  1.1 48.6 %copy-start.2 = (s32[128]{0:T(128)S(1)}, s32[128]{0:T(128)}, u32[]{:S(2)}) copy-start(s32[128]{0:T(128)} %order.1) | copy-start | bytes 1540
  50.4 30.6 %copy-start.1 = (f32[64,128]{1,0:T(8,128)S(1)}, f32[64,128]{1,0:T(8,128)}, u32[]{:S(2)}) copy-start(f32[64,128]{1,0:T(8,128)} %get-tuple-element.18) | copy-start | bytes 98308
  50.4 30.8 %copy-start = (f32[64,128]{1,0:T(8,128)S(1)}, f32[64,128]{1,0:T(8,128)}, u32[]{:S(2)}) copy-start(f32[64,128]{1,0:T(8,128)} %hw_ref.1) | copy-start | bytes 98308

commit v3 on v2

v3 whole, which is shorter than its diff:
```python
import functools

import jax
import jax.numpy as jnp
from jax import lax
from jax.experimental import pallas as pl
from jax.experimental.pallas import tpu as pltpu
from jax.sharding import PartitionSpec as P

MESH = pl.DeviceIdType.MESH
NX, NZ, NY = 4, 8, 4
HEADS = 64
HEADS_DEV = 16
KD = 576
KPAD = 640
IDX_HEADS = 64
IDX_DIM = 128
TOK = 64
HALF = 32
HALVES = 128
SLOTS = 36
SCORE_SCALE = 192.0 ** (-0.5)
LOG2E = 1.4426950408889634
INDEX_NORM = (IDX_HEADS * IDX_DIM) ** (-0.5)
GRAD_COEF = 1024.0 * INDEX_NORM
NEG = -1e30
VMEM_BYTES = 60 * 1024 * 1024
F32 = jnp.float32
BF16 = jnp.bfloat16


def coords():
    s = lax.axis_index("seq")
    y = lax.axis_index("head")
    return s // (2 * NZ), (s // 2) % NZ, s % 2, y


def seq_at(x, z, c):
    return (x * NZ + z) * 2 + c


ENTRIES = 9


def entry_table(places):
    i = jnp.arange(ENTRIES, dtype=jnp.int32)[None, :]
    k = i - 5
    flip = places[:, :1] // 16 + 1 > k
    early = (i == 0) | ((i > 5) & flip)
    block = jnp.where(i == 0, 0, jnp.where(i < 6, i - 1, jnp.where(flip, k, 8 - k)))
    group = 2 * jnp.arange(2, dtype=jnp.int32)[:, None] + jnp.where(early, 0, 1)
    limit = jnp.where(early, places[:, :1], places[:, 1:]) * HALF - block * 512
    return jnp.stack([early.astype(jnp.int32), group, block, limit]).reshape(-1)


def entry(table, pair, i):
    return [table[(field * 2 + pair) * ENTRIES + i] for field in range(4)]


def mask_of(flag, shape):
    return jnp.zeros(shape, jnp.int32) + flag > 0


def sort_keys(inverse, pq, keys):
    pad = jnp.zeros((HALF, KPAD - KD), BF16)

    def step(p, carry):
        slot = inverse[p]
        chip, core, half = slot // 4, slot // 2 % 2, slot % 2
        first, second = pq[half, chip, :, 0:KD], pq[half, chip, :, KD : 2 * KD]
        rows = pl.ds(pl.multiple_of(p % 16 * HALF, HALF), HALF)
        keys[p // 16, rows, :] = jnp.concatenate([jnp.where(core == 0, first, second), pad], axis=1)
        return carry

    lax.fori_loop(0, HALVES, step, 0, unroll=2)


def sort_index_keys(inverse, idxg, slots32, sorted32, idx_keys):
    slots32[...] = idxg[...].astype(F32).reshape(HALVES, 8, IDX_DIM)

    def step(p, carry):
        sorted32[p] = slots32[inverse[p]]
        return carry

    lax.fori_loop(0, HALVES, step, 0, unroll=8)
    idx_keys[...] = sorted32[...].reshape(8, 128, IDX_DIM).astype(BF16)


def split_heads(pair, vmq, queries):
    pad = jnp.zeros((HALF, KPAD - KD), BF16)
    for half in range(2):
        for h in range(HEADS_DEV):
            queries[2 * pair + half, h * HALF : (h + 1) * HALF, :] = jnp.concatenate(
                [vmq[pair, half * HALF : (half + 1) * HALF, h * KD : (h + 1) * KD], pad], axis=1
            )


LANES = HEADS_DEV * HALF
EXP_SCALE = SCORE_SCALE * LOG2E


def score_step(table, pair, i, keys, queries, scores, tops):
    early, g, block, limit = entry(table, pair, i)
    early = mask_of(early, (8, LANES))
    k = keys[block]
    s = lax.dot_general(k, queries[g], (((1,), (1,)), ((), ())), preferred_element_type=F32)
    row = lax.broadcasted_iota(jnp.int32, (512, LANES), 0)
    token = lax.broadcasted_iota(jnp.int32, (512, LANES), 1) % HALF
    s = jnp.where(row - token <= limit, s, NEG)
    scores[i] = s
    m = jnp.max(s.reshape(64, 8, LANES), axis=0)
    return (
        jnp.where(early, jnp.maximum(tops[0], m), tops[0]),
        jnp.where(early, tops[1], jnp.maximum(tops[1], m)),
    )


def exp_step(table, pair, i, scores, shifts, sums):
    early = entry(table, pair, i)[0]
    row = mask_of(early, (1, LANES))
    early = mask_of(early, (8, LANES))
    e = jnp.exp2(scores[i] * EXP_SCALE - jnp.where(row, shifts[0], shifts[1]))
    scores[i] = e
    m = jnp.sum(e.reshape(64, 8, LANES), axis=0)
    return (sums[0] + jnp.where(early, m, 0.0), sums[1] + jnp.where(early, 0.0, m))


def head_step(table, pair, i, scores, weights, tgt_ref):
    early = mask_of(entry(table, pair, i)[0], (1, LANES))
    group_of = lax.broadcasted_iota(jnp.int32, (8, 128), 1) // HALF
    weight = jnp.where(early, weights[0], weights[1])
    for part in range(4):
        rows = slice(part * 128, (part + 1) * 128)
        r = scores[i, rows, 0:128] * weight[:, 0:128]
        for lt in range(1, LANES // 128):
            r = r + scores[i, rows, lt * 128 : (lt + 1) * 128] * weight[:, lt * 128 : (lt + 1) * 128]
        r = r + pltpu.roll(r, 64, 1)
        r = r + pltpu.roll(r, 32, 1)
        for y in range(NY):
            out = r[8 * y : 8 * y + 8]
            for a in range(1, 4):
                out = jnp.where(group_of == a, r[32 * a + 8 * y : 32 * a + 8 * y + 8], out)
            tgt_ref[y, pair, 4 * i + part] = out


def start_tops():
    return (jnp.full((8, LANES), NEG, F32),) * 2


def start_sums():
    return (jnp.zeros((8, LANES), F32),) * 2


def shifts_of(tops):
    return tuple(jnp.max(t, axis=0, keepdims=True) * EXP_SCALE for t in tops)


def weights_of(sums):
    return tuple(1.0 / (HEADS * jnp.sum(t, axis=0, keepdims=True)) for t in sums)


def targets(table, pair, keys, queries, scores, tgt_ref):
    tops = lax.fori_loop(0, 9, lambda i, t: score_step(table, pair, i, keys, queries, scores, t), start_tops())
    shifts = shifts_of(tops)
    sums = lax.fori_loop(0, 9, lambda i, t: exp_step(table, pair, i, scores, shifts, t), start_sums())
    weights = weights_of(sums)

    def last(i, carry):
        head_step(table, pair, i, scores, weights, tgt_ref)
        return carry

    lax.fori_loop(0, 9, last, 0)


def split_index_heads(pair, vidx, idx_q):
    for half in range(2):
        for j in range(IDX_HEADS):
            idx_q[2 * pair + half, j * HALF : (j + 1) * HALF, :] = vidx[
                pair, half * HALF : (half + 1) * HALF, j * IDX_DIM : (j + 1) * IDX_DIM
            ]


def logit_step(table, pair, i, y, idx_keys, idx_q, w_ref, inner_ref, logit_ref, tops):
    early, g, block, limit = entry(table, pair, i)
    early = mask_of(early, (8, 128))
    k = idx_keys[block]
    acc = jnp.zeros((128, 128), F32)
    for ch in range(8):
        cut = slice(ch * 256, (ch + 1) * 256)
        inner = lax.dot_general(k, idx_q[g, cut, :], (((1,), (1,)), ((), ())), preferred_element_type=F32)
        inner_ref[pair, i, :, cut] = inner.astype(BF16)
        part = jnp.maximum(inner, 0.0) * w_ref[g, :, cut]
        acc = acc + part[:, :128] + part[:, 128:]
    acc = acc + pltpu.roll(acc, 64, 1)
    acc = acc + pltpu.roll(acc, 32, 1)
    row = lax.broadcasted_iota(jnp.int32, (128, 128), 0)
    token = lax.broadcasted_iota(jnp.int32, (128, 128), 1) % HALF
    offset = row // 8 * HALF + row % 8 - token
    acc = jnp.where(offset <= limit - 8 * y, acc * INDEX_NORM, NEG)
    logit_ref[pair, i] = acc
    m = jnp.max(acc.reshape(16, 8, 128), axis=0)
    return (
        jnp.where(early, jnp.maximum(tops[0], m), tops[0]),
        jnp.where(early, tops[1], jnp.maximum(tops[1], m)),
    )


def logit_stats(table, pair, logit_ref, stat_ref, tops):
    tops = [jnp.max(t, axis=0, keepdims=True) for t in tops]

    def step(i, sums):
        early = entry(table, pair, i)[0]
        row = mask_of(early, (1, 128))
        early = mask_of(early, (8, 128))
        e = jnp.exp(logit_ref[pair, i] - jnp.where(row, tops[0], tops[1]))
        e = jnp.sum(e.reshape(16, 8, 128), axis=0)
        return (sums[0] + jnp.where(early, e, 0.0), sums[1] + jnp.where(early, 0.0, e))

    sums = lax.fori_loop(0, 9, step, (jnp.zeros((8, 128), F32),) * 2, unroll=3)
    for half in range(2):
        g = 2 * pair + half
        stat_ref[g : g + 1, :] = tops[half]
        stat_ref[4 + g : 5 + g, :] = jnp.sum(sums[half], axis=0, keepdims=True)


def norms_of(stats_ref, g):
    tops = [stats_ref[d, g : g + 1, :] for d in range(NY)]
    top = jnp.maximum(jnp.maximum(tops[0], tops[1]), jnp.maximum(tops[2], tops[3]))
    norm = sum(stats_ref[d, 4 + g : 5 + g, :] * jnp.exp(tops[d] - top) for d in range(NY))
    return top, GRAD_COEF / norm


def gradient_step(table, pair, i, y, idx_q, w_ref, inner_ref, logit_ref, tgt_ref, arrive, norms, grad_ref):
    early, g, block, limit = entry(table, pair, i)
    early = mask_of(early, (1, 128))
    group_of = lax.broadcasted_iota(jnp.int32, (8, 128), 1) // HALF
    wide = []
    for part in range(4):
        at = 4 * i + part
        packed = tgt_ref[y, pair, at] + arrive[0, pair, at] + arrive[1, pair, at] + arrive[2, pair, at]
        for a in range(4):
            v = jnp.where(group_of == a, packed, 0.0)
            v = v + pltpu.roll(v, 64, 1)
            wide.append(v + pltpu.roll(v, 32, 1))
    target = jnp.concatenate(wide, axis=0)
    top = jnp.where(early, norms[0][0], norms[1][0])
    coef = jnp.where(early, norms[0][1], norms[1][1])
    row = lax.broadcasted_iota(jnp.int32, (128, 128), 0)
    token = lax.broadcasted_iota(jnp.int32, (128, 128), 1) % HALF
    offset = row // 8 * HALF + row % 8 - token
    seen = offset <= limit - 8 * y
    scaled = jnp.where(seen, jnp.exp(logit_ref[pair, i] - top) * coef - GRAD_COEF * target, 0.0)
    scaled = jnp.concatenate([scaled, scaled], axis=1)
    acc = jnp.zeros((128, IDX_DIM), F32)
    zero = jnp.zeros((), BF16)
    for ch in range(8):
        cut = slice(ch * 256, (ch + 1) * 256)
        signal = (scaled * w_ref[g, :, cut]).astype(BF16)
        signal = jnp.where(inner_ref[pair, i, :, cut] > zero, signal, zero)
        acc = acc + jnp.dot(signal, idx_q[g, cut, :], preferred_element_type=F32)
    grad_ref[pair, i] = acc


def collect_gradients(table, order, grad_ref, sorted_ref, part_ref):
    total = [grad_ref[0, 0] + grad_ref[1, 0] + grad_ref[0, 1] + grad_ref[1, 1]]
    total += [grad_ref[0, b + 1] + grad_ref[1, b + 1] for b in range(1, 5)] + [0.0] * 3
    for pair in range(2):
        for k in range(1, 4):
            flip = mask_of(entry(table, pair, k + 5)[0], (128, IDX_DIM))
            d = grad_ref[pair, k + 5]
            total[k] = total[k] + jnp.where(flip, d, 0.0)
            total[8 - k] = total[8 - k] + jnp.where(flip, 0.0, d)
    for b in range(8):
        sorted_ref[b * 16 : (b + 1) * 16] = total[b].reshape(16, 8, IDX_DIM)

    def store(chip, carry):
        for core in range(2):
            for half in range(2):
                place = order[4 * chip + 2 * core + half]
                rows = sorted_ref[place]
                part_ref[chip // NZ, chip % NZ, core * 16 + half * 8 : core * 16 + half * 8 + 8, :] = rows
        return carry

    lax.fori_loop(0, NX * NZ, store, 0, unroll=2)


def scatter(
    x, z, c, y, peers_x, peers_z, remote, part_ref, out_ref, xa, za, xb, zb, slab_x, slab_z, tail, pieces,
    xa_sem, za_sem, xb_sem, zb_sem, piece_sem,
):
    near = [(half, core) for half in range(2) for core in range(2)]
    targets = [(seq_at(x, z, core), y // 2 + 2 * half) for half, core in near]
    sources = [(seq_at(x, z, core), 2 * (y % 2) + odd) for odd in range(2) for core in range(2)]
    first_z = [
        remote(part_ref.at[:, (z + d) % NZ, pl.ds(16, 16)], za.at[d - 1], za_sem.at[0, d - 1], za_sem.at[1, d - 1], peers_z[d - 1])
        for d in range(1, NZ)
    ]
    first_x = [
        remote(part_ref.at[(x + d) % NX, :, pl.ds(0, 16)], xa.at[d - 1], xa_sem.at[0, d - 1], xa_sem.at[1, d - 1], peers_x[d - 1])
        for d in range(1, NX)
    ]
    for d in first_x:
        d.wait_recv()
    slab_x[...] = part_ref[x, :, 0:16, :] + xa[0] + xa[1] + xa[2]
    second_z = [
        remote(slab_x.at[(z + d) % NZ], zb.at[d - 1], zb_sem.at[0, d - 1], zb_sem.at[1, d - 1], peers_z[d - 1]) for d in range(1, NZ)
    ]
    for d in first_z:
        d.wait_recv()
    total = part_ref[:, z, 16:32, :]
    for k in range(NZ - 1):
        total = total + za[k]
    slab_z[...] = total
    second_x = [
        remote(slab_z.at[(x + d) % NX], xb.at[d - 1], xb_sem.at[0, d - 1], xb_sem.at[1, d - 1], peers_x[d - 1]) for d in range(1, NX)
    ]
    for d in second_z:
        d.wait_recv()
    total = slab_x[z]
    for k in range(NZ - 1):
        total = total + zb[k]
    tail[0:16] = total
    for d in second_x:
        d.wait_recv()
    tail[16:32] = slab_z[x] + xb[0] + xb[1] + xb[2]

    slot = 2 * (y % 2) + c

    for k, (half, core) in enumerate(near):
        piece = tail.at[pl.ds(16 * core + 8 * half, 8)]
        local = jnp.logical_and(core == c, y // 2 + 2 * half == y)

        @pl.when(jnp.logical_not(local))
        def _(piece=piece, k=k):
            pltpu.make_async_remote_copy(
                src_ref=piece, dst_ref=pieces.at[slot], send_sem=piece_sem.at[0, k],
                recv_sem=piece_sem.at[1, slot], device_id=targets[k], device_id_type=MESH,
            ).start()

        @pl.when(local)
        def _(piece=piece):
            pieces[slot] = piece[...]

    for k, (odd, core) in enumerate([(odd, core) for odd in range(2) for core in range(2)]):
        away = jnp.logical_not(jnp.logical_and(core == c, 2 * (y % 2) + odd == y))

        @pl.when(away)
        def _(k=k, odd=odd, core=core):
            ref = pieces.at[2 * odd + core]
            pltpu.make_async_remote_copy(
                src_ref=ref, dst_ref=ref, send_sem=piece_sem.at[0, k], recv_sem=piece_sem.at[1, 2 * odd + core],
                device_id=sources[k], device_id_type=MESH,
            ).wait_recv()

    for odd in range(2):
        for core in range(2):
            out_ref[8 * odd : 8 * odd + 8, core * IDX_DIM : (core + 1) * IDX_DIM] = pieces[2 * odd + core]
    for k, (half, core) in enumerate(near):
        away = jnp.logical_not(jnp.logical_and(core == c, y // 2 + 2 * half == y))

        @pl.when(away)
        def _(k=k, half=half, core=core):
            piece = tail.at[pl.ds(16 * core + 8 * half, 8)]
            pltpu.make_async_remote_copy(
                src_ref=piece, dst_ref=pieces.at[slot], send_sem=piece_sem.at[0, k],
                recv_sem=piece_sem.at[1, slot], device_id=targets[k], device_id_type=MESH,
            ).wait_send()

    for d in first_x + first_z + second_x + second_z:
        d.wait_send()


def whole_kernel(
    table, order, inverse, lat_ref, idx_ref, w_all, mq_any, iq_any, out_ref,
    pq, stage_out, stage_in, idx32, idx_stage_out, idx_stage_in, idxg, slots32, sorted32, idx_keys,
    vmq, queries, keys, scores, tgt_ref, vidx, idx_q, w_ref, inner_ref, logit_ref, stat_ref, stats_ref, arrive,
    grad_ref, part_ref, xa, za, xb, zb, slab_x, slab_z, tail, pieces,
    load_sem, pair_send, pair_recv, ring_send, ring_recv, idx_z_sem, idx_x_sem,
    tgt_send, tgt_recv, stat_send, stat_recv, xa_sem, za_sem, xb_sem, zb_sem, piece_sem,
):
    x, z, c, y = coords()
    seq = lax.axis_index("seq")
    me = x * NZ + z
    barrier = pltpu.get_barrier_semaphore()
    partner = (seq_at(x, z, 1 - c), y)
    peers_y = [(seq, (y + d) % NY) for d in range(1, NY)]
    peers_x = [(seq_at((x + d) % NX, z, c), y) for d in range(1, NX)]
    peers_z = [(seq_at(x, (z + d) % NZ, c), y) for d in range(1, NZ)]
    other = [(seq_at(x, z, 1 - c), t) for t in range(NY)]
    ring = {("x", 1): peers_x[0], ("x", -1): peers_x[-1], ("z", 1): peers_z[0], ("z", -1): peers_z[-1]}
    for to in peers_x + peers_z + peers_y + other:
        pl.semaphore_signal(barrier, inc=1, device_id=to, device_id_type=MESH)
    loads = [
        pltpu.make_async_copy(mq_any.at[c], vmq.at[0], load_sem.at[0]),
        pltpu.make_async_copy(iq_any.at[c], vidx.at[0], load_sem.at[1]),
    ]
    for d in loads:
        d.start()

    lat = lat_ref[...]
    stage_out[:, 0:KD] = jnp.where(c == 0, lat[:, KD:], lat[:, :KD])
    stage_out[:, KD:] = jnp.zeros((TOK, KPAD - KD), BF16)
    idx32[...] = idx_ref[...].astype(F32)
    rows = jnp.concatenate(
        [idx32[pl.ds(pl.multiple_of(y * 8, 8), 8), :], idx32[pl.ds(pl.multiple_of(HALF + y * 8, 8), 8), :]], axis=0
    )
    idx_stage_out[...] = jnp.where(c == 0, rows[:, IDX_DIM:], rows[:, :IDX_DIM]).astype(BF16)
    pl.semaphore_wait(barrier, NX - 1 + NZ - 1 + 2 * NY - 1)

    def remote(src, dst, send, recv, to):
        d = pltpu.make_async_remote_copy(
            src_ref=src, dst_ref=dst, send_sem=send, recv_sem=recv, device_id=to, device_id_type=MESH
        )
        d.start()
        return d

    def to_partner(k, src, dst):
        return remote(src, dst, pair_send.at[k], pair_recv.at[k], partner)

    pair_copies = [
        to_partner(0, stage_out, stage_in),
        to_partner(1, idx_stage_out, idx_stage_in),
        to_partner(2, iq_any.at[1 - c], vidx.at[1]),
        to_partner(3, mq_any.at[1 - c], vmq.at[1]),
        to_partner(4, w_all.at[1 - c], w_ref.at[pl.ds(2, 2)]),
    ]
    mine = jnp.where(c == 0, lat[:, :KD], lat[:, KD:])
    idx_mine = jnp.where(c == 0, rows[:, :IDX_DIM], rows[:, IDX_DIM:]).astype(BF16)
    w_ref[0:2] = w_all[c]
    pair_copies[0].wait_recv()
    pair_copies[1].wait_recv()
    from_partner = stage_in[:, :KD]
    both = jnp.concatenate([jnp.where(c == 0, mine, from_partner), jnp.where(c == 0, from_partner, mine)], axis=1)
    pq[0, me] = both[:HALF]
    pq[1, me] = both[HALF:]
    idx_other = idx_stage_in[...]
    idxg[x, z, 0:16] = jnp.where(c == 0, idx_mine, idx_other)
    idxg[x, z, 16:32] = jnp.where(c == 0, idx_other, idx_mine)

    counter = [0]
    live = {}

    def send(part, axis, way, dx, dz, lo, hi):
        k = counter[0]
        counter[0] += 1

        def block(ox, oz):
            return pq.at[part, (x + ox + 2 * NX) % NX * NZ + (z + oz + 2 * NZ) % NZ, pl.ds(lo, hi - lo)]

        out = remote(block(dx, dz), block(dx, dz), ring_send.at[k], ring_recv.at[k], ring[(axis, way)])
        here = block(dx - way, dz) if axis == "x" else block(dx, dz - way)
        arrival = pltpu.make_async_remote_copy(
            src_ref=here, dst_ref=here, send_sem=ring_send.at[k], recv_sem=ring_recv.at[k],
            device_id=ring[(axis, way)], device_id_type=MESH,
        )
        live[k] = [out, arrival, False]
        return k

    def arrived(k):
        if not live[k][2]:
            live[k][1].wait_recv()
            live[k][2] = True

    last_x, last_z = NX // 2, NZ // 2

    def hop(part, axis, dx, dz, step, before):
        last = last_x if axis == "x" else last_z
        ks = []
        for way, half in ((1, (0, 16)), (-1, (16, 32))):
            if before is not None:
                arrived(before[0 if way == 1 else 1])
            away = -way * (step - 1)
            ox, oz = (away, dz) if axis == "x" else (dx, away)
            lo, hi = half if step == last else (0, 32)
            ks.append(send(part, axis, way, ox, oz, lo, hi))
        return ks

    zp, xq, zq = {}, {}, {}

    def start_p(dx):
        zp[dx] = {1: hop(0, "z", dx, 0, 1, None)}

    def advance_p(dx, step):
        zp[dx][step] = hop(0, "z", dx, 0, step, zp[dx][step - 1])

    def advance_q(step):
        before = zq[step - 1]
        if step <= last_z:
            zq[step] = hop(1, "z", 0, 0, step, before)
        else:
            arrived(before[0])
            arrived(before[1])
        for dz in (-(step - 1), step - 1) if step <= last_z else (last_z,):
            xq[dz] = {1: hop(1, "x", 0, dz, 1, None)}

    def finish_q(dz):
        xq[dz][2] = hop(1, "x", 0, dz, 2, xq[dz][1])

    idx_z = [
        remote(idxg.at[x, z], idxg.at[x, z], idx_z_sem.at[0, d - 1], idx_z_sem.at[1, d - 1], peers_z[d - 1])
        for d in range(1, NZ)
    ]
    idx_x = []

    def spread_index():
        for d in range(1, NZ):
            ref = idxg.at[x, (z - d + NZ) % NZ]
            pltpu.make_async_remote_copy(
                src_ref=ref, dst_ref=ref, send_sem=idx_z_sem.at[0, d - 1], recv_sem=idx_z_sem.at[1, d - 1],
                device_id=peers_z[d - 1], device_id_type=MESH,
            ).wait_recv()
        for d in range(1, NX):
            idx_x.append(
                remote(idxg.at[x], idxg.at[x], idx_x_sem.at[0, d - 1], idx_x_sem.at[1, d - 1], peers_x[d - 1])
            )

    def have_index():
        for d in range(1, NX):
            ref = idxg.at[(x - d + NX) % NX]
            pltpu.make_async_remote_copy(
                src_ref=ref, dst_ref=ref, send_sem=idx_x_sem.at[0, d - 1], recv_sem=idx_x_sem.at[1, d - 1],
                device_id=peers_x[d - 1], device_id_type=MESH,
            ).wait_recv()
        sort_index_keys(inverse, idxg, slots32, sorted32, idx_keys)

    logit_tops = [(jnp.full((8, 128), NEG, F32),) * 2 for _ in range(2)]
    stat_copies = []

    def logits(pair, first, last):
        logit_tops[pair] = lax.fori_loop(
            first, last,
            lambda i, t: logit_step(table, pair, i, y, idx_keys, idx_q, w_ref, inner_ref, logit_ref, t),
            logit_tops[pair],
        )
        if last == ENTRIES:
            logit_stats(table, pair, logit_ref, stat_ref, logit_tops[pair])

    def send_stats():
        for d in range(1, NY):
            stat_copies.append(
                remote(stat_ref, stats_ref.at[d], stat_send.at[d - 1], stat_recv.at[d - 1], peers_y[d - 1])
            )
        stats_ref[0] = stat_ref[...]

    def own_queries():
        loads[0].wait()
        split_heads(0, vmq, queries)

    def own_index_queries():
        loads[1].wait()
        pair_copies[4].wait_recv()
        split_index_heads(0, vidx, idx_q)

    def other_index_queries():
        pair_copies[2].wait_recv()
        split_index_heads(1, vidx, idx_q)

    def other_queries():
        pair_copies[3].wait_recv()
        split_heads(1, vmq, queries)

    work = [own_index_queries, spread_index, own_queries, have_index]
    work += [functools.partial(logits, 0, k, k + 3) for k in (0, 3, 6)]
    work += [other_index_queries]
    work += [functools.partial(logits, 1, k, k + 3) for k in (0, 3, 6)]
    work += [send_stats, other_queries]

    def between():
        if work:
            work.pop(0)()

    start_p(0)
    xp = hop(0, "x", 0, 0, 1, None)
    zq[1] = hop(1, "z", 0, 0, 1, None)
    xq[0] = {1: hop(1, "x", 0, 0, 1, None)}
    between()
    xp2 = hop(0, "x", 0, 0, 2, xp)
    start_p(-1)
    start_p(1)
    between()
    advance_p(0, 2)
    advance_q(2)
    finish_q(0)
    between()
    arrived(xp2[0])
    arrived(xp2[1])
    start_p(2)
    between()
    advance_p(-1, 2)
    advance_p(1, 2)
    between()
    advance_p(0, 3)
    advance_q(3)
    between()
    finish_q(-1)
    finish_q(1)
    advance_p(2, 2)
    between()
    advance_p(-1, 3)
    advance_p(1, 3)
    between()
    advance_p(0, 4)
    advance_q(4)
    between()
    finish_q(-2)
    finish_q(2)
    advance_p(2, 3)
    between()
    advance_p(-1, 4)
    advance_p(1, 4)
    between()
    advance_q(5)
    finish_q(-3)
    finish_q(3)
    between()
    advance_p(2, 4)
    finish_q(last_z)
    while work:
        between()
    for k in live:
        arrived(k)
    sort_keys(inverse, pq, keys)

    tgt_copies = []
    for pair in range(2):
        targets(table, pair, keys, queries, scores, tgt_ref)
        tgt_copies.append(
            [
                remote(
                    tgt_ref.at[(y + d) % NY, pair], arrive.at[d - 1, pair], tgt_send.at[pair, d - 1],
                    tgt_recv.at[pair, d - 1], peers_y[d - 1],
                )
                for d in range(1, NY)
            ]
        )
    for d in stat_copies:
        d.wait_recv()
    for pair in range(2):
        norms = [norms_of(stats_ref, 2 * pair + half) for half in range(2)]
        for d in tgt_copies[pair]:
            d.wait_recv()

        def step(i, carry):
            gradient_step(
                table, pair, i, y, idx_q, w_ref, inner_ref, logit_ref, tgt_ref, arrive, norms, grad_ref
            )
            return carry

        lax.fori_loop(0, 9, step, 0)
    collect_gradients(table, order, grad_ref, sorted32, part_ref)
    scatter(
        x, z, c, y, peers_x, peers_z, remote, part_ref, out_ref, xa, za, xb, zb, slab_x, slab_z, tail, pieces,
        xa_sem, za_sem, xb_sem, zb_sem, piece_sem,
    )
    for k in live:
        live[k][0].wait_send()
    for d in pair_copies + idx_z + idx_x + stat_copies + tgt_copies[0] + tgt_copies[1]:
        d.wait_send()


RING_COPIES = 76


def whole_call(table, order, inverse, lat, idx, w_all, mq, iq):
    any_spec = pl.BlockSpec(memory_space=pl.ANY)
    vmem = pl.BlockSpec(memory_space=pltpu.VMEM)
    smem = pl.BlockSpec(memory_space=pltpu.SMEM)
    dma = pltpu.SemaphoreType.DMA
    return pl.pallas_call(
        whole_kernel,
        name="indexer_key_gradient",
        out_shape=jax.ShapeDtypeStruct((16, 2 * IDX_DIM), F32),
        in_specs=[smem] * 3 + [vmem] * 3 + [any_spec] * 2,
        out_specs=vmem,
        scratch_shapes=[
            pltpu.VMEM((2, NX * NZ, HALF, 2 * KD), BF16),
            pltpu.VMEM((TOK, KPAD), BF16),
            pltpu.VMEM((TOK, KPAD), BF16),
            pltpu.VMEM((TOK, 2 * IDX_DIM), F32),
            pltpu.VMEM((16, IDX_DIM), BF16),
            pltpu.VMEM((16, IDX_DIM), BF16),
            pltpu.VMEM((NX, NZ, 32, IDX_DIM), BF16),
            pltpu.VMEM((HALVES, 8, IDX_DIM), F32),
            pltpu.VMEM((HALVES, 8, IDX_DIM), F32),
            pltpu.VMEM((8, 128, IDX_DIM), BF16),
            pltpu.VMEM((2, TOK, HEADS_DEV * KD), BF16),
            pltpu.VMEM((4, LANES, KPAD), BF16),
            pltpu.VMEM((8, 512, KPAD), BF16),
            pltpu.VMEM((ENTRIES, 512, LANES), F32),
            pltpu.VMEM((NY, 2, SLOTS, 8, 128), F32),
            pltpu.VMEM((2, TOK, IDX_HEADS * IDX_DIM), BF16),
            pltpu.VMEM((4, IDX_HEADS * HALF, IDX_DIM), BF16),
            pltpu.VMEM((4, 1, IDX_HEADS * HALF), F32),
            pltpu.VMEM((2, ENTRIES, 128, IDX_HEADS * HALF), BF16),
            pltpu.VMEM((2, ENTRIES, 128, 128), F32),
            pltpu.VMEM((8, 128), F32),
            pltpu.VMEM((NY, 8, 128), F32),
            pltpu.VMEM((NY - 1, 2, SLOTS, 8, 128), F32),
            pltpu.VMEM((2, ENTRIES, 128, IDX_DIM), F32),
            pltpu.VMEM((NX, NZ, 32, IDX_DIM), F32),
            pltpu.VMEM((NX - 1, NZ, 16, IDX_DIM), F32),
            pltpu.VMEM((NZ - 1, NX, 16, IDX_DIM), F32),
            pltpu.VMEM((NX - 1, 16, IDX_DIM), F32),
            pltpu.VMEM((NZ - 1, 16, IDX_DIM), F32),
            pltpu.VMEM((NZ, 16, IDX_DIM), F32),
            pltpu.VMEM((NX, 16, IDX_DIM), F32),
            pltpu.VMEM((32, IDX_DIM), F32),
            pltpu.VMEM((4, 8, IDX_DIM), F32),
            dma((2,)),
            dma((5,)),
            dma((5,)),
            dma((RING_COPIES,)),
            dma((RING_COPIES,)),
            dma((2, NZ - 1)),
            dma((2, NX - 1)),
            dma((2, NY - 1)),
            dma((2, NY - 1)),
            dma((NY - 1,)),
            dma((NY - 1,)),
            dma((2, NX - 1)),
            dma((2, NZ - 1)),
            dma((2, NX - 1)),
            dma((2, NZ - 1)),
            dma((2, 4)),
        ],
        compiler_params=pltpu.CompilerParams(
            collective_id=0, has_side_effects=True, vmem_limit_bytes=VMEM_BYTES
        ),
    )(table, order, inverse, lat, idx, w_all, mq, iq)


def per_device(mla_queries, latent_keys, index_queries, index_keys, head_weights, block_order):
    s = lax.axis_index("seq")
    mine = lax.dynamic_slice(block_order, (2 * s,), (2,))
    others = lax.dynamic_slice(block_order, (2 * (s + 1 - 2 * (s % 2)),), (2,))
    table = entry_table(jnp.stack([mine, others]))
    slots = jnp.arange(HALVES, dtype=jnp.int32)
    inverse = jnp.sum(jnp.where(block_order[None, :] == slots[:, None], slots[None, :], 0), axis=1)
    w_all = head_weights.reshape(2, HALF, 2, IDX_HEADS).transpose(2, 0, 3, 1).reshape(2, 2, 1, IDX_HEADS * HALF)
    return whole_call(table, block_order, inverse, latent_keys, index_keys, w_all, mla_queries, index_queries)


def solution(mesh):
    return jax.shard_map(
        per_device,
        mesh=mesh,
        in_specs=(
            P(None, "seq", "head"),
            P("seq", None),
            P(None, "seq", None),
            P("seq", None),
            P("seq", None),
            P(),
        ),
        out_specs=P(("seq", "head"), None),
        check_vma=False,
    )
```

time: 130 us -> 110 us (0.85)
  Pallas kernels: 124 us -> 104 us
    pallas_call x3 -> x1, Pallas kernels: 124 us -> 104 us  [whole_call(): pl.pallas_call(whole_kernel, name='indexer_key_gradient', out_shape=jax.S...]
where the time goes in v3:
time: 110 us
  Pallas kernels  104 us (95%)
  local copies, waits for them, and re-layouts  4.4 us (4%)
  other arithmetic  1.72 us (2%)
    pallas_call x1, Pallas kernels, whole_call(): pl.pallas_call(whole_kernel, name='indexer_key_gradient', out_shape=jax.S...  104 us

profile of v3, /device:TPU:1, one launch (start us, length us, event | category | flops | bytes accessed | tf_op | source)
XLA Modules:
  0.0 109.8 jit_solution(16718781338292292301)
XLA Ops:
  0.0 0.8 dynamic-slice_bitcast_fusion.1
  0.8 0.2 slice_reduce_fusion.1
  1.0 0.1 fusion.3
  1.1 0.1 multiply_subtract_fusion
  1.2 0.6 reshape.689.table
  1.8 0.9 reshape.690
  2.7 0.1 copy.10
  2.8 0.7 reshape.692.w_all
  3.5 1.3 %select_reduce_fusion.inverse = s32[128]{0:T(128)} fusion(s32[128]{0:T(128)} %order.1), kind=kLoop, calls=%fused_computation | loop fusion | flops 49024 | bytes 1024 | tf_op jit(solution)/shard_map/reduce_sum | solution.py:738
  4.8 103.6 %indexer_key_gradient.1 = f32[16,256]{1,0:T(8,128)} custom-call(s32[72]{0:T(128)} %reshape.689.table, s32[128]{0:T(128)} %order.1, s32[128]{0:T(128)} %select_reduce_fusion.inverse, bf16[64,1152]{1,0:T(8,128)(2,1)} %lat_ref.1, bf16[64,256]{1,0:T(8,128)(2,1)} %idx_ref.1, f32[2,2,1,2048]{3,2,1,0:T(1,128)} %reshape.692.w_all, bf16[2,64,9216]{2,1,0:T(8,128)(2,1)} %mq_any.1, ...), custom_call_target="tpu_custom_call" | custom-call | tf_op jit(solution)/shard_map/indexer_key_gradient/pallas_call | solution.py:669
  108.5 1.3 %copy.13 = f32[16,256]{1,0:T(8,128)} copy(f32[16,256]{1,0:T(8,128)} %indexer_key_gradient.1) | data formatting | bytes 32768
  (7 shorter events, 0.0 us)

commit v4 on v3

--- a/solution.py
+++ b/solution.py
@@ -42,15 +42,19 @@
 ENTRIES = 9
 
 
-def entry_table(places):
-    i = jnp.arange(ENTRIES, dtype=jnp.int32)[None, :]
-    k = i - 5
-    flip = places[:, :1] // 16 + 1 > k
-    early = (i == 0) | ((i > 5) & flip)
-    block = jnp.where(i == 0, 0, jnp.where(i < 6, i - 1, jnp.where(flip, k, 8 - k)))
-    group = 2 * jnp.arange(2, dtype=jnp.int32)[:, None] + jnp.where(early, 0, 1)
-    limit = jnp.where(early, places[:, :1], places[:, 1:]) * HALF - block * 512
-    return jnp.stack([early.astype(jnp.int32), group, block, limit]).reshape(-1)
+def fill_table(order, seq, table):
+    for pair in range(2):
+        device = seq if pair == 0 else seq + 1 - 2 * (seq % 2)
+        early_place, late_place = order[2 * device], order[2 * device + 1]
+        for i in range(ENTRIES):
+            k = i - 5
+            flip = jnp.where(early_place // 16 >= k, 1, 0)
+            early = 1 if i == 0 else 0 if i < 6 else flip
+            block = 0 if i == 0 else i - 1 if i < 6 else flip * k + (1 - flip) * (8 - k)
+            place = early * early_place + (1 - early) * late_place
+            fields = (early, 2 * pair + 1 - early, block, place * HALF - block * 512)
+            for field, value in enumerate(fields):
+                table[(field * 2 + pair) * ENTRIES + i] = jnp.int32(value)
 
 
 def entry(table, pair, i):
@@ -61,28 +65,34 @@
     return jnp.zeros(shape, jnp.int32) + flag > 0
 
 
-def sort_keys(inverse, pq, keys):
-    pad = jnp.zeros((HALF, KPAD - KD), BF16)
-
+def split_cores(pq, slots, part, chip, lo, hi):
+    pad = jnp.zeros((hi - lo, KPAD - KD), BF16)
+    for core in range(2):
+        rows = pq[part, chip, lo:hi, core * KD : (core + 1) * KD]
+        slots[4 * chip + 2 * core + part, lo:hi, :] = jnp.concatenate([rows, pad], axis=1)
+
+
+def sort_keys(first, slots, keys):
     def step(p, carry):
-        slot = inverse[p]
-        chip, core, half = slot // 4, slot // 2 % 2, slot % 2
-        first, second = pq[half, chip, :, 0:KD], pq[half, chip, :, KD : 2 * KD]
-        rows = pl.ds(pl.multiple_of(p % 16 * HALF, HALF), HALF)
-        keys[p // 16, rows, :] = jnp.concatenate([jnp.where(core == 0, first, second), pad], axis=1)
+        slot = first[p]
+        low, high = p, HALVES - 1 - p
+        keys[low // 16, pl.ds(pl.multiple_of(low % 16 * HALF, HALF), HALF), :] = slots[slot]
+        keys[high // 16, pl.ds(pl.multiple_of(high % 16 * HALF, HALF), HALF), :] = slots[slot + 1]
         return carry
 
-    lax.fori_loop(0, HALVES, step, 0, unroll=2)
-
-
-def sort_index_keys(inverse, idxg, slots32, sorted32, idx_keys):
+    lax.fori_loop(0, HALVES // 2, step, 0, unroll=4)
+
+
+def sort_index_keys(first, idxg, slots32, sorted32, idx_keys):
     slots32[...] = idxg[...].astype(F32).reshape(HALVES, 8, IDX_DIM)
 
     def step(p, carry):
-        sorted32[p] = slots32[inverse[p]]
+        slot = first[p]
+        sorted32[p] = slots32[slot]
+        sorted32[HALVES - 1 - p] = slots32[slot + 1]
         return carry
 
-    lax.fori_loop(0, HALVES, step, 0, unroll=8)
+    lax.fori_loop(0, HALVES // 2, step, 0, unroll=4)
     idx_keys[...] = sorted32[...].reshape(8, 128, IDX_DIM).astype(BF16)
 
 
@@ -175,9 +185,31 @@
 def split_index_heads(pair, vidx, idx_q):
     for half in range(2):
         for j in range(IDX_HEADS):
-            idx_q[2 * pair + half, j * HALF : (j + 1) * HALF, :] = vidx[
+            at = (j % 16 * 4 + j // 16) * HALF
+            idx_q[2 * pair + half, at : at + HALF, :] = vidx[
                 pair, half * HALF : (half + 1) * HALF, j * IDX_DIM : (j + 1) * IDX_DIM
             ]
+
+
+def weight_rows(hw):
+    turned = jnp.concatenate([hw, hw], axis=0).T
+    return [
+        [
+            jnp.concatenate(
+                [
+                    turned[q * IDX_HEADS + a * 16 : q * IDX_HEADS + a * 16 + 16, half * HALF : (half + 1) * HALF]
+                    for a in range(4)
+                ],
+                axis=1,
+            )
+            for half in range(2)
+        ]
+        for q in range(2)
+    ]
+
+
+def weight_cut(w_ref, g, ch):
+    return jnp.concatenate([w_ref[g, 2 * ch : 2 * ch + 1, :], w_ref[g, 2 * ch + 1 : 2 * ch + 2, :]], axis=1)
 
 
 def logit_step(table, pair, i, y, idx_keys, idx_q, w_ref, inner_ref, logit_ref, tops):
@@ -189,7 +221,7 @@
         cut = slice(ch * 256, (ch + 1) * 256)
         inner = lax.dot_general(k, idx_q[g, cut, :], (((1,), (1,)), ((), ())), preferred_element_type=F32)
         inner_ref[pair, i, :, cut] = inner.astype(BF16)
-        part = jnp.maximum(inner, 0.0) * w_ref[g, :, cut]
+        part = jnp.maximum(inner, 0.0) * weight_cut(w_ref, g, ch)
         acc = acc + part[:, :128] + part[:, 128:]
     acc = acc + pltpu.roll(acc, 64, 1)
     acc = acc + pltpu.roll(acc, 32, 1)
@@ -255,7 +287,7 @@
     zero = jnp.zeros((), BF16)
     for ch in range(8):
         cut = slice(ch * 256, (ch + 1) * 256)
-        signal = (scaled * w_ref[g, :, cut]).astype(BF16)
+        signal = (scaled * weight_cut(w_ref, g, ch)).astype(BF16)
         signal = jnp.where(inner_ref[pair, i, :, cut] > zero, signal, zero)
         acc = acc + jnp.dot(signal, idx_q[g, cut, :], preferred_element_type=F32)
     grad_ref[pair, i] = acc
@@ -284,99 +316,129 @@
     lax.fori_loop(0, NX * NZ, store, 0, unroll=2)
 
 
+def final_targets(x, z, c, y):
+    return [
+        (core, d, half, (seq_at(x, (z + d) % NZ, 0) if core == 0 else seq_at((x + d) % NX, z, 1), y // 2 + 2 * half))
+        for core in range(2)
+        for d in range(NZ if core == 0 else NX)
+        for half in range(2)
+    ]
+
+
+def final_sources(x, z, core, y):
+    return [
+        (
+            d,
+            2 * odd + c,
+            (seq_at(x, (z - d + NZ) % NZ, c) if core == 0 else seq_at((x - d + NX) % NX, z, c), 2 * (y % 2) + odd),
+            d == 0 and c == core,
+        )
+        for d in range(NZ if core == 0 else NX)
+        for odd in range(2)
+        for c in range(2)
+    ]
+
+
 def scatter(
-    x, z, c, y, peers_x, peers_z, remote, part_ref, out_ref, xa, za, xb, zb, slab_x, slab_z, tail, pieces,
-    xa_sem, za_sem, xb_sem, zb_sem, piece_sem,
+    x, z, c, y, peers_x, peers_z, remote, part_ref, out_ref, xa, za, slab_x, slab_z, final,
+    xa_sem, za_sem, final_send, final_recv,
 ):
-    near = [(half, core) for half in range(2) for core in range(2)]
-    targets = [(seq_at(x, z, core), y // 2 + 2 * half) for half, core in near]
-    sources = [(seq_at(x, z, core), 2 * (y % 2) + odd) for odd in range(2) for core in range(2)]
     first_z = [
-        remote(part_ref.at[:, (z + d) % NZ, pl.ds(16, 16)], za.at[d - 1], za_sem.at[0, d - 1], za_sem.at[1, d - 1], peers_z[d - 1])
+        remote(
+            part_ref.at[:, (z + d) % NZ, pl.ds(16, 16)], za.at[d - 1], za_sem.at[0, d - 1], za_sem.at[1, d - 1],
+            peers_z[d - 1],
+        )
         for d in range(1, NZ)
     ]
     first_x = [
-        remote(part_ref.at[(x + d) % NX, :, pl.ds(0, 16)], xa.at[d - 1], xa_sem.at[0, d - 1], xa_sem.at[1, d - 1], peers_x[d - 1])
+        remote(
+            part_ref.at[(x + d) % NX, :, pl.ds(0, 16)], xa.at[d - 1], xa_sem.at[0, d - 1], xa_sem.at[1, d - 1],
+            peers_x[d - 1],
+        )
         for d in range(1, NX)
     ]
+    slot = 2 * (y % 2) + c
+    ends = final_targets(x, z, c, y)
+
+    def piece(core, d, half):
+        if core == 0:
+            return slab_x.at[(z + d) % NZ, pl.ds(8 * half, 8)]
+        return slab_z.at[(x + d) % NX, pl.ds(8 * half, 8)]
+
+    def last_copy(k):
+        core, d, half, to = ends[k]
+        return pltpu.make_async_remote_copy(
+            src_ref=piece(core, d, half), dst_ref=final.at[d, slot], send_sem=final_send.at[k],
+            recv_sem=final_recv.at[d, slot], device_id=to, device_id_type=MESH,
+        )
+
+    def here(k):
+        core, d, half, _ = ends[k]
+        return jnp.logical_and(c == core, y // 2 + 2 * half == y) if d == 0 else None
+
+    def send_last(wanted):
+        for k, (core, d, half, _) in enumerate(ends):
+            if core != wanted:
+                continue
+            if d > 0:
+                last_copy(k).start()
+                continue
+
+            @pl.when(jnp.logical_not(here(k)))
+            def _(k=k):
+                last_copy(k).start()
+
+            @pl.when(here(k))
+            def _(core=core, d=d, half=half):
+                final[0, slot] = piece(core, d, half)[...]
+
     for d in first_x:
         d.wait_recv()
     slab_x[...] = part_ref[x, :, 0:16, :] + xa[0] + xa[1] + xa[2]
-    second_z = [
-        remote(slab_x.at[(z + d) % NZ], zb.at[d - 1], zb_sem.at[0, d - 1], zb_sem.at[1, d - 1], peers_z[d - 1]) for d in range(1, NZ)
-    ]
+    send_last(0)
     for d in first_z:
         d.wait_recv()
     total = part_ref[:, z, 16:32, :]
     for k in range(NZ - 1):
         total = total + za[k]
     slab_z[...] = total
-    second_x = [
-        remote(slab_z.at[(x + d) % NX], xb.at[d - 1], xb_sem.at[0, d - 1], xb_sem.at[1, d - 1], peers_x[d - 1]) for d in range(1, NX)
-    ]
-    for d in second_z:
-        d.wait_recv()
-    total = slab_x[z]
-    for k in range(NZ - 1):
-        total = total + zb[k]
-    tail[0:16] = total
-    for d in second_x:
-        d.wait_recv()
-    tail[16:32] = slab_z[x] + xb[0] + xb[1] + xb[2]
-
-    slot = 2 * (y % 2) + c
-
-    for k, (half, core) in enumerate(near):
-        piece = tail.at[pl.ds(16 * core + 8 * half, 8)]
-        local = jnp.logical_and(core == c, y // 2 + 2 * half == y)
-
-        @pl.when(jnp.logical_not(local))
-        def _(piece=piece, k=k):
-            pltpu.make_async_remote_copy(
-                src_ref=piece, dst_ref=pieces.at[slot], send_sem=piece_sem.at[0, k],
-                recv_sem=piece_sem.at[1, slot], device_id=targets[k], device_id_type=MESH,
-            ).start()
-
-        @pl.when(local)
-        def _(piece=piece):
-            pieces[slot] = piece[...]
-
-    for k, (odd, core) in enumerate([(odd, core) for odd in range(2) for core in range(2)]):
-        away = jnp.logical_not(jnp.logical_and(core == c, 2 * (y % 2) + odd == y))
-
-        @pl.when(away)
-        def _(k=k, odd=odd, core=core):
-            ref = pieces.at[2 * odd + core]
-            pltpu.make_async_remote_copy(
-                src_ref=ref, dst_ref=ref, send_sem=piece_sem.at[0, k], recv_sem=piece_sem.at[1, 2 * odd + core],
-                device_id=sources[k], device_id_type=MESH,
-            ).wait_recv()
-
-    for odd in range(2):
-        for core in range(2):
-            out_ref[8 * odd : 8 * odd + 8, core * IDX_DIM : (core + 1) * IDX_DIM] = pieces[2 * odd + core]
-    for k, (half, core) in enumerate(near):
-        away = jnp.logical_not(jnp.logical_and(core == c, y // 2 + 2 * half == y))
-
-        @pl.when(away)
-        def _(k=k, half=half, core=core):
-            piece = tail.at[pl.ds(16 * core + 8 * half, 8)]
-            pltpu.make_async_remote_copy(
-                src_ref=piece, dst_ref=pieces.at[slot], send_sem=piece_sem.at[0, k],
-                recv_sem=piece_sem.at[1, slot], device_id=targets[k], device_id_type=MESH,
-            ).wait_send()
-
-    for d in first_x + first_z + second_x + second_z:
+    send_last(1)
+    for core in range(2):
+
+        @pl.when(c == core)
+        def _(core=core):
+            for d, at, source, maybe_here in final_sources(x, z, core, y):
+                ref = final.at[d, at]
+                arrival = pltpu.make_async_remote_copy(
+                    src_ref=ref, dst_ref=ref, send_sem=final_send.at[0], recv_sem=final_recv.at[d, at],
+                    device_id=source, device_id_type=MESH,
+                )
+                if maybe_here:
+                    pl.when(source[1] != y)(arrival.wait_recv)
+                else:
+                    arrival.wait_recv()
+            for at in range(4):
+                total = final[0, at]
+                for d in range(1, NZ if core == 0 else NX):
+                    total = total + final[d, at]
+                out_ref[at // 2 * 8 : at // 2 * 8 + 8, at % 2 * IDX_DIM : (at % 2 + 1) * IDX_DIM] = total
+
+    for k, (core, d, half, _) in enumerate(ends):
+        if d > 0:
+            last_copy(k).wait_send()
+        else:
+            pl.when(jnp.logical_not(here(k)))(last_copy(k).wait_send)
+    for d in first_x + first_z:
         d.wait_send()
 
 
 def whole_kernel(
-    table, order, inverse, lat_ref, idx_ref, w_all, mq_any, iq_any, out_ref,
-    pq, stage_out, stage_in, idx32, idx_stage_out, idx_stage_in, idxg, slots32, sorted32, idx_keys,
+    order, first, lat_any, idx_any, hw_any, mq_any, iq_any, out_ref,
+    table, lat_ref, idx_ref, hw_ref, w_other, pq, slots, stage_out, stage_in, idx32, idx_stage_out, idx_stage_in, idxg, slots32, sorted32, idx_keys,
     vmq, queries, keys, scores, tgt_ref, vidx, idx_q, w_ref, inner_ref, logit_ref, stat_ref, stats_ref, arrive,
-    grad_ref, part_ref, xa, za, xb, zb, slab_x, slab_z, tail, pieces,
+    grad_ref, part_ref, xa, za, slab_x, slab_z, final,
     load_sem, pair_send, pair_recv, ring_send, ring_recv, idx_z_sem, idx_x_sem,
-    tgt_send, tgt_recv, stat_send, stat_recv, xa_sem, za_sem, xb_sem, zb_sem, piece_sem,
+    tgt_send, tgt_recv, stat_send, stat_recv, xa_sem, za_sem, final_send, final_recv,
 ):
     x, z, c, y = coords()
     seq = lax.axis_index("seq")
@@ -386,17 +448,41 @@
     peers_y = [(seq, (y + d) % NY) for d in range(1, NY)]
     peers_x = [(seq_at((x + d) % NX, z, c), y) for d in range(1, NX)]
     peers_z = [(seq_at(x, (z + d) % NZ, c), y) for d in range(1, NZ)]
-    other = [(seq_at(x, z, 1 - c), t) for t in range(NY)]
     ring = {("x", 1): peers_x[0], ("x", -1): peers_x[-1], ("z", 1): peers_z[0], ("z", -1): peers_z[-1]}
-    for to in peers_x + peers_z + peers_y + other:
+
+    def tell(to):
         pl.semaphore_signal(barrier, inc=1, device_id=to, device_id_type=MESH)
+
+    for to in peers_x + peers_z + peers_y + [partner]:
+        tell(to)
     loads = [
-        pltpu.make_async_copy(mq_any.at[c], vmq.at[0], load_sem.at[0]),
-        pltpu.make_async_copy(iq_any.at[c], vidx.at[0], load_sem.at[1]),
+        pltpu.make_async_copy(src, dst, load_sem.at[k])
+        for k, (src, dst) in enumerate(
+            [
+                (lat_any, lat_ref), (idx_any, idx_ref), (hw_any, hw_ref), (iq_any.at[c], vidx.at[0]),
+                (mq_any.at[c], vmq.at[0]),
+            ]
+        )
     ]
     for d in loads:
         d.start()
-
+    for core in range(2):
+
+        @pl.when(c == core)
+        def _(core=core):
+            for _, _, source, maybe_here in final_sources(x, z, core, y):
+                if maybe_here:
+                    pl.when(source[1] != y)(functools.partial(tell, source))
+                else:
+                    tell(source)
+
+    fill_table(order, seq, table)
+    for d in loads[:3]:
+        d.wait()
+    weights = weight_rows(hw_ref[...])
+    for half in range(2):
+        w_other[half] = jnp.where(c == 0, weights[1][half], weights[0][half])
+        w_ref[half] = jnp.where(c == 0, weights[0][half], weights[1][half])
     lat = lat_ref[...]
     stage_out[:, 0:KD] = jnp.where(c == 0, lat[:, KD:], lat[:, :KD])
     stage_out[:, KD:] = jnp.zeros((TOK, KPAD - KD), BF16)
@@ -405,7 +491,8 @@
         [idx32[pl.ds(pl.multiple_of(y * 8, 8), 8), :], idx32[pl.ds(pl.multiple_of(HALF + y * 8, 8), 8), :]], axis=0
     )
     idx_stage_out[...] = jnp.where(c == 0, rows[:, IDX_DIM:], rows[:, :IDX_DIM]).astype(BF16)
-    pl.semaphore_wait(barrier, NX - 1 + NZ - 1 + 2 * NY - 1)
+    own = jnp.where(jnp.logical_or(y == 0, y == NY - 1), 1, 0)
+    pl.semaphore_wait(barrier, NX - 1 + NZ - 1 + NY - 1 + 1 + 2 * (NZ + NX) - own)
 
     def remote(src, dst, send, recv, to):
         d = pltpu.make_async_remote_copy(
@@ -422,11 +509,10 @@
         to_partner(1, idx_stage_out, idx_stage_in),
         to_partner(2, iq_any.at[1 - c], vidx.at[1]),
         to_partner(3, mq_any.at[1 - c], vmq.at[1]),
-        to_partner(4, w_all.at[1 - c], w_ref.at[pl.ds(2, 2)]),
+        to_partner(4, w_other, w_ref.at[pl.ds(2, 2)]),
     ]
     mine = jnp.where(c == 0, lat[:, :KD], lat[:, KD:])
     idx_mine = jnp.where(c == 0, rows[:, :IDX_DIM], rows[:, IDX_DIM:]).astype(BF16)
-    w_ref[0:2] = w_all[c]
     pair_copies[0].wait_recv()
     pair_copies[1].wait_recv()
     from_partner = stage_in[:, :KD]
@@ -438,7 +524,8 @@
     idxg[x, z, 16:32] = jnp.where(c == 0, idx_other, idx_mine)
 
     counter = [0]
-    live = {}
+    live, origin = {}, {}
+    landed = [(0, me, 0, HALF), (1, me, 0, HALF)]
 
     def send(part, axis, way, dx, dz, lo, hi):
         k = counter[0]
@@ -454,12 +541,15 @@
             device_id=ring[(axis, way)], device_id_type=MESH,
         )
         live[k] = [out, arrival, False]
+        ix, iz = (dx - way, dz) if axis == "x" else (dx, dz - way)
+        origin[k] = (part, (x + ix + 2 * NX) % NX * NZ + (z + iz + 2 * NZ) % NZ, lo, hi)
         return k
 
     def arrived(k):
         if not live[k][2]:
             live[k][1].wait_recv()
             live[k][2] = True
+            landed.append(origin[k])
 
     last_x, last_z = NX // 2, NZ // 2
 
@@ -521,7 +611,7 @@
                 src_ref=ref, dst_ref=ref, send_sem=idx_x_sem.at[0, d - 1], recv_sem=idx_x_sem.at[1, d - 1],
                 device_id=peers_x[d - 1], device_id_type=MESH,
             ).wait_recv()
-        sort_index_keys(inverse, idxg, slots32, sorted32, idx_keys)
+        sort_index_keys(first, idxg, slots32, sorted32, idx_keys)
 
     logit_tops = [(jnp.full((8, 128), NEG, F32),) * 2 for _ in range(2)]
     stat_copies = []
@@ -543,11 +633,11 @@
         stats_ref[0] = stat_ref[...]
 
     def own_queries():
-        loads[0].wait()
+        loads[4].wait()
         split_heads(0, vmq, queries)
 
     def own_index_queries():
-        loads[1].wait()
+        loads[3].wait()
         pair_copies[4].wait_recv()
         split_index_heads(0, vidx, idx_q)
 
@@ -568,6 +658,8 @@
     def between():
         if work:
             work.pop(0)()
+        for _ in range(min(4, len(landed))):
+            split_cores(pq, slots, *landed.pop(0))
 
     start_p(0)
     xp = hop(0, "x", 0, 0, 1, None)
@@ -619,7 +711,9 @@
         between()
     for k in live:
         arrived(k)
-    sort_keys(inverse, pq, keys)
+        while landed:
+            split_cores(pq, slots, *landed.pop(0))
+    sort_keys(first, slots, keys)
 
     tgt_copies = []
     for pair in range(2):
@@ -649,8 +743,8 @@
         lax.fori_loop(0, 9, step, 0)
     collect_gradients(table, order, grad_ref, sorted32, part_ref)
     scatter(
-        x, z, c, y, peers_x, peers_z, remote, part_ref, out_ref, xa, za, xb, zb, slab_x, slab_z, tail, pieces,
-        xa_sem, za_sem, xb_sem, zb_sem, piece_sem,
+        x, z, c, y, peers_x, peers_z, remote, part_ref, out_ref, xa, za, slab_x, slab_z, final,
+        xa_sem, za_sem, final_send, final_recv,
     )
     for k in live:
         live[k][0].wait_send()
@@ -661,7 +755,7 @@
 RING_COPIES = 76
 
 
-def whole_call(table, order, inverse, lat, idx, w_all, mq, iq):
+def whole_call(order, first, lat, idx, hw, mq, iq):
     any_spec = pl.BlockSpec(memory_space=pl.ANY)
     vmem = pl.BlockSpec(memory_space=pltpu.VMEM)
     smem = pl.BlockSpec(memory_space=pltpu.SMEM)
@@ -670,10 +764,16 @@
         whole_kernel,
         name="indexer_key_gradient",
         out_shape=jax.ShapeDtypeStruct((16, 2 * IDX_DIM), F32),
-        in_specs=[smem] * 3 + [vmem] * 3 + [any_spec] * 2,
+        in_specs=[smem] * 2 + [any_spec] * 5,
         out_specs=vmem,
         scratch_shapes=[
+            pltpu.SMEM((8 * ENTRIES,), jnp.int32),
+            pltpu.VMEM((TOK, 2 * KD), BF16),
+            pltpu.VMEM((TOK, 2 * IDX_DIM), BF16),
+            pltpu.VMEM((TOK, 2 * IDX_HEADS), F32),
+            pltpu.VMEM((2, 16, 128), F32),
             pltpu.VMEM((2, NX * NZ, HALF, 2 * KD), BF16),
+            pltpu.VMEM((HALVES, HALF, KPAD), BF16),
             pltpu.VMEM((TOK, KPAD), BF16),
             pltpu.VMEM((TOK, KPAD), BF16),
             pltpu.VMEM((TOK, 2 * IDX_DIM), F32),
@@ -690,7 +790,7 @@
             pltpu.VMEM((NY, 2, SLOTS, 8, 128), F32),
             pltpu.VMEM((2, TOK, IDX_HEADS * IDX_DIM), BF16),
             pltpu.VMEM((4, IDX_HEADS * HALF, IDX_DIM), BF16),
-            pltpu.VMEM((4, 1, IDX_HEADS * HALF), F32),
+            pltpu.VMEM((4, 16, 128), F32),
             pltpu.VMEM((2, ENTRIES, 128, IDX_HEADS * HALF), BF16),
             pltpu.VMEM((2, ENTRIES, 128, 128), F32),
             pltpu.VMEM((8, 128), F32),
@@ -700,13 +800,10 @@
             pltpu.VMEM((NX, NZ, 32, IDX_DIM), F32),
             pltpu.VMEM((NX - 1, NZ, 16, IDX_DIM), F32),
             pltpu.VMEM((NZ - 1, NX, 16, IDX_DIM), F32),
-            pltpu.VMEM((NX - 1, 16, IDX_DIM), F32),
-            pltpu.VMEM((NZ - 1, 16, IDX_DIM), F32),
             pltpu.VMEM((NZ, 16, IDX_DIM), F32),
             pltpu.VMEM((NX, 16, IDX_DIM), F32),
-            pltpu.VMEM((32, IDX_DIM), F32),
-            pltpu.VMEM((4, 8, IDX_DIM), F32),
-            dma((2,)),
+            pltpu.VMEM((NZ, 4, 8, IDX_DIM), F32),
+            dma((5,)),
             dma((5,)),
             dma((5,)),
             dma((RING_COPIES,)),
@@ -719,25 +816,20 @@
             dma((NY - 1,)),
             dma((2, NX - 1)),
             dma((2, NZ - 1)),
-            dma((2, NX - 1)),
-            dma((2, NZ - 1)),
-            dma((2, 4)),
+            dma((2 * (NX + NZ),)),
+            dma((NZ, 4)),
         ],
         compiler_params=pltpu.CompilerParams(
             collective_id=0, has_side_effects=True, vmem_limit_bytes=VMEM_BYTES
         ),
-    )(table, order, inverse, lat, idx, w_all, mq, iq)
+    )(order, first, lat, idx, hw, mq, iq)
 
 
 def per_device(mla_queries, latent_keys, index_queries, index_keys, head_weights, block_order):
-    s = lax.axis_index("seq")
-    mine = lax.dynamic_slice(block_order, (2 * s,), (2,))
-    others = lax.dynamic_slice(block_order, (2 * (s + 1 - 2 * (s % 2)),), (2,))
-    table = entry_table(jnp.stack([mine, others]))
-    slots = jnp.arange(HALVES, dtype=jnp.int32)
-    inverse = jnp.sum(jnp.where(block_order[None, :] == slots[:, None], slots[None, :], 0), axis=1)
-    w_all = head_weights.reshape(2, HALF, 2, IDX_HEADS).transpose(2, 0, 3, 1).reshape(2, 2, 1, IDX_HEADS * HALF)
-    return whole_call(table, block_order, inverse, latent_keys, index_keys, w_all, mla_queries, index_queries)
+    early = block_order.reshape(HALVES // 2, 2)[:, 0]
+    ids = jnp.arange(HALVES // 2, dtype=jnp.int32)
+    first = jnp.sum(jnp.where(early[None, :] == ids[:, None], 2 * ids[None, :], 0), axis=1)
+    return whole_call(block_order, first, latent_keys, index_keys, head_weights, mla_queries, index_queries)
 
 
 def solution(mesh):

time: 110 us -> 98 us (0.89)
  Pallas kernels: 104 us -> 94.9 us
  local copies, waits for them, and re-layouts: 4.4 us -> 2.21 us
    pallas_call x1, Pallas kernels: 104 us -> 94.9 us  [whole_call(): pl.pallas_call(whole_kernel, name='indexer_key_gradient', out_shape=jax.S...]
    reshape x4 -> x1, local copies, waits for them, and re-layouts: 2.27 us -> 0.78 us  [per_device(): early = block_order.reshape(HALVES // 2, 2)[:, 0]]
where the time goes in v4:
time: 98 us; the launch traced here: 97.8 us
  Pallas kernels  94.9 us (97%)
  local copies, waits for them, and re-layouts  2.21 us (2%)
    pallas_call x1, Pallas kernels, whole_call(): pl.pallas_call(whole_kernel, name='indexer_key_gradient', out_shape=jax.S...  94.9 us

profile of v4, /device:TPU:1, one launch (start us, length us, event | category | flops | bytes accessed | tf_op | source)
XLA Modules:
  0.0 97.8 jit_solution(12894197489352083874)
XLA Ops:
  0.0 0.8 reshape.9
  0.8 0.1 slice_reduce_fusion
  0.9 0.6 select_reduce_fusion.first
  1.5 94.9 %indexer_key_gradient.1 = f32[16,256]{1,0:T(8,128)} custom-call(s32[128]{0:T(128)} %order.1, s32[64]{0:T(128)} %select_reduce_fusion.first, bf16[64,1152]{1,0:T(8,128)(2,1)} %lat_any.1, bf16[64,256]{1,0:T(8,128)(2,1)} %idx_any.1, f32[64,128]{1,0:T(8,128)} %hw_any.1, bf16[2,64,9216]{2,1,0:T(8,128)(2,1)} %mq_any.1, bf16[2,64,8192]{2,1,0:T(8,128)(2,1)} %iq_any.1), custom_call_target="tpu_custom_call" | custom-call | tf_op jit(solution)/shard_map/indexer_key_gradient/pallas_call | solution.py:763
  96.4 1.3 %copy.8 = f32[16,256]{1,0:T(8,128)} copy(f32[16,256]{1,0:T(8,128)} %indexer_key_gradient.1) | data formatting | bytes 32768
  (1 shorter events, 0.0 us)

commit v5 on v4

--- a/solution.py
+++ b/solution.py
@@ -65,11 +65,23 @@
     return jnp.zeros(shape, jnp.int32) + flag > 0
 
 
-def split_cores(pq, slots, part, chip, lo, hi):
+P_LANES = 7 * 128
+Q_LANES = 4 * KD - P_LANES
+
+
+def split_cores(p_ref, q_ref, slots, part, chip, lo, hi):
     pad = jnp.zeros((hi - lo, KPAD - KD), BF16)
-    for core in range(2):
-        rows = pq[part, chip, lo:hi, core * KD : (core + 1) * KD]
-        slots[4 * chip + 2 * core + part, lo:hi, :] = jnp.concatenate([rows, pad], axis=1)
+
+    def padded(rows):
+        return jnp.concatenate([rows, pad], axis=1)
+
+    if part == 0:
+        slots[4 * chip, lo:hi, :] = padded(p_ref[chip, lo:hi, :KD])
+        slots[4 * chip + 2, lo:hi, : P_LANES - KD] = p_ref[chip, lo:hi, KD:]
+    else:
+        slots[4 * chip + 1, lo:hi, :] = padded(q_ref[chip, lo:hi, :KD])
+        slots[4 * chip + 3, lo:hi, :] = padded(q_ref[chip, lo:hi, KD : 2 * KD])
+        slots[4 * chip + 2, lo:hi, P_LANES - KD :] = padded(q_ref[chip, lo:hi, 2 * KD :])
 
 
 def sort_keys(first, slots, keys):
@@ -138,19 +150,22 @@
 def head_step(table, pair, i, scores, weights, tgt_ref):
     early = mask_of(entry(table, pair, i)[0], (1, LANES))
     group_of = lax.broadcasted_iota(jnp.int32, (8, 128), 1) // HALF
-    weight = jnp.where(early, weights[0], weights[1])
+    weight = jnp.broadcast_to(jnp.where(early, weights[0], weights[1]), (8, LANES))
+    low, even = group_of < 2, group_of % 2 == 0
+
+    def heads(first):
+        tiles = [slice(lt * 128, (lt + 1) * 128) for lt in range(LANES // 128)]
+        terms = [scores[i, first : first + 8, cut] * weight[:, cut] for cut in tiles]
+        return (terms[0] + terms[1]) + (terms[2] + terms[3])
+
     for part in range(4):
-        rows = slice(part * 128, (part + 1) * 128)
-        r = scores[i, rows, 0:128] * weight[:, 0:128]
-        for lt in range(1, LANES // 128):
-            r = r + scores[i, rows, lt * 128 : (lt + 1) * 128] * weight[:, lt * 128 : (lt + 1) * 128]
-        r = r + pltpu.roll(r, 64, 1)
-        r = r + pltpu.roll(r, 32, 1)
         for y in range(NY):
-            out = r[8 * y : 8 * y + 8]
-            for a in range(1, 4):
-                out = jnp.where(group_of == a, r[32 * a + 8 * y : 32 * a + 8 * y + 8], out)
-            tgt_ref[y, pair, 4 * i + part] = out
+            v = [heads(part * 128 + 32 * a + 8 * y) for a in range(4)]
+            t02 = jnp.where(low, v[0], v[2]) + pltpu.roll(jnp.where(low, v[2], v[0]), 64, 1)
+            t13 = jnp.where(low, v[1], v[3]) + pltpu.roll(jnp.where(low, v[3], v[1]), 64, 1)
+            swap = jnp.where(even, t13, t02)
+            swap = jnp.where(even, pltpu.roll(swap, 96, 1), pltpu.roll(swap, 32, 1))
+            tgt_ref[y, pair, 4 * i + part] = jnp.where(even, t02, t13) + swap
 
 
 def start_tops():
@@ -169,8 +184,8 @@
     return tuple(1.0 / (HEADS * jnp.sum(t, axis=0, keepdims=True)) for t in sums)
 
 
-def targets(table, pair, keys, queries, scores, tgt_ref):
-    tops = lax.fori_loop(0, 9, lambda i, t: score_step(table, pair, i, keys, queries, scores, t), start_tops())
+def targets(table, pair, keys, queries, scores, tgt_ref, send):
+    tops = lax.fori_loop(0, 9, lambda i, t: score_step(table, pair, i, keys, queries, scores, t), start_tops(), unroll=3)
     shifts = shifts_of(tops)
     sums = lax.fori_loop(0, 9, lambda i, t: exp_step(table, pair, i, scores, shifts, t), start_sums())
     weights = weights_of(sums)
@@ -179,7 +194,9 @@
         head_step(table, pair, i, scores, weights, tgt_ref)
         return carry
 
-    lax.fori_loop(0, 9, last, 0)
+    for first in range(0, ENTRIES, 3):
+        lax.fori_loop(first, first + 3, last, 0)
+        send(pair, first)
 
 
 def split_index_heads(pair, vidx, idx_q):
@@ -316,26 +333,35 @@
     lax.fori_loop(0, NX * NZ, store, 0, unroll=2)
 
 
-def final_targets(x, z, c, y):
-    return [
-        (core, d, half, (seq_at(x, (z + d) % NZ, 0) if core == 0 else seq_at((x + d) % NX, z, 1), y // 2 + 2 * half))
-        for core in range(2)
-        for d in range(NZ if core == 0 else NX)
-        for half in range(2)
-    ]
-
-
-def final_sources(x, z, core, y):
+X_ROWS = 24
+PIECES = [(core, half) for core in range(2) for half in range(2)]
+
+
+def along_x(core, half):
+    return (core, half) != (1, 1)
+
+
+def final_targets(x, z, y):
     return [
         (
-            d,
-            2 * odd + c,
-            (seq_at(x, (z - d + NZ) % NZ, c) if core == 0 else seq_at((x - d + NX) % NX, z, c), 2 * (y % 2) + odd),
-            d == 0 and c == core,
+            core, half, d,
+            (seq_at(x, (z + d) % NZ, core) if along_x(core, half) else seq_at((x + d) % NX, z, core), y // 2 + 2 * half),
         )
-        for d in range(NZ if core == 0 else NX)
+        for core, half in PIECES
+        for d in range(NZ if along_x(core, half) else NX)
+    ]
+
+
+def final_sources(x, z, y, summed_x):
+    return [
+        (
+            d, 2 * odd + core,
+            (seq_at(x, (z - d + NZ) % NZ, core) if summed_x else seq_at((x - d + NX) % NX, z, core), 2 * (y % 2) + odd),
+            core,
+        )
+        for d in range(NZ if summed_x else NX)
         for odd in range(2)
-        for c in range(2)
+        for core in range(2)
     ]
 
 
@@ -343,42 +369,43 @@
     x, z, c, y, peers_x, peers_z, remote, part_ref, out_ref, xa, za, slab_x, slab_z, final,
     xa_sem, za_sem, final_send, final_recv,
 ):
-    first_z = [
-        remote(
-            part_ref.at[:, (z + d) % NZ, pl.ds(16, 16)], za.at[d - 1], za_sem.at[0, d - 1], za_sem.at[1, d - 1],
-            peers_z[d - 1],
-        )
-        for d in range(1, NZ)
-    ]
     first_x = [
         remote(
-            part_ref.at[(x + d) % NX, :, pl.ds(0, 16)], xa.at[d - 1], xa_sem.at[0, d - 1], xa_sem.at[1, d - 1],
+            part_ref.at[(x + d) % NX, :, pl.ds(0, X_ROWS)], xa.at[d - 1], xa_sem.at[0, d - 1], xa_sem.at[1, d - 1],
             peers_x[d - 1],
         )
         for d in range(1, NX)
     ]
+    first_z = [
+        remote(
+            part_ref.at[:, (z + d) % NZ, pl.ds(X_ROWS, 32 - X_ROWS)], za.at[d - 1], za_sem.at[0, d - 1],
+            za_sem.at[1, d - 1], peers_z[d - 1],
+        )
+        for d in range(1, NZ)
+    ]
     slot = 2 * (y % 2) + c
-    ends = final_targets(x, z, c, y)
-
-    def piece(core, d, half):
-        if core == 0:
-            return slab_x.at[(z + d) % NZ, pl.ds(8 * half, 8)]
-        return slab_z.at[(x + d) % NX, pl.ds(8 * half, 8)]
+    ends = final_targets(x, z, y)
+
+    def piece(k):
+        core, half, d, _ = ends[k]
+        if along_x(core, half):
+            return slab_x.at[(z + d) % NZ, pl.ds(16 * core + 8 * half, 8)]
+        return slab_z.at[(x + d) % NX]
 
     def last_copy(k):
-        core, d, half, to = ends[k]
+        d, to = ends[k][2:]
         return pltpu.make_async_remote_copy(
-            src_ref=piece(core, d, half), dst_ref=final.at[d, slot], send_sem=final_send.at[k],
+            src_ref=piece(k), dst_ref=final.at[d, slot], send_sem=final_send.at[k],
             recv_sem=final_recv.at[d, slot], device_id=to, device_id_type=MESH,
         )
 
     def here(k):
-        core, d, half, _ = ends[k]
-        return jnp.logical_and(c == core, y // 2 + 2 * half == y) if d == 0 else None
-
-    def send_last(wanted):
-        for k, (core, d, half, _) in enumerate(ends):
-            if core != wanted:
+        core, half, _, _ = ends[k]
+        return jnp.logical_and(c == core, y // 2 + 2 * half == y)
+
+    def send_last(summed_x):
+        for k, (core, half, d, _) in enumerate(ends):
+            if along_x(core, half) != summed_x:
                 continue
             if d > 0:
                 last_copy(k).start()
@@ -389,41 +416,41 @@
                 last_copy(k).start()
 
             @pl.when(here(k))
-            def _(core=core, d=d, half=half):
-                final[0, slot] = piece(core, d, half)[...]
+            def _(k=k):
+                final[0, slot] = piece(k)[...]
 
     for d in first_x:
         d.wait_recv()
-    slab_x[...] = part_ref[x, :, 0:16, :] + xa[0] + xa[1] + xa[2]
-    send_last(0)
+    slab_x[...] = part_ref[x, :, 0:X_ROWS, :] + xa[0] + xa[1] + xa[2]
+    send_last(True)
     for d in first_z:
         d.wait_recv()
-    total = part_ref[:, z, 16:32, :]
+    total = part_ref[:, z, X_ROWS:32, :]
     for k in range(NZ - 1):
         total = total + za[k]
     slab_z[...] = total
-    send_last(1)
-    for core in range(2):
-
-        @pl.when(c == core)
-        def _(core=core):
-            for d, at, source, maybe_here in final_sources(x, z, core, y):
+    send_last(False)
+    for summed_x in (True, False):
+
+        @pl.when(by_x(c, y) if summed_x else jnp.logical_not(by_x(c, y)))
+        def _(summed_x=summed_x):
+            for d, at, source, core in final_sources(x, z, y, summed_x):
                 ref = final.at[d, at]
                 arrival = pltpu.make_async_remote_copy(
                     src_ref=ref, dst_ref=ref, send_sem=final_send.at[0], recv_sem=final_recv.at[d, at],
                     device_id=source, device_id_type=MESH,
                 )
-                if maybe_here:
-                    pl.when(source[1] != y)(arrival.wait_recv)
+                if d == 0:
+                    pl.when(jnp.logical_or(core != c, source[1] != y))(arrival.wait_recv)
                 else:
                     arrival.wait_recv()
             for at in range(4):
                 total = final[0, at]
-                for d in range(1, NZ if core == 0 else NX):
+                for d in range(1, NZ if summed_x else NX):
                     total = total + final[d, at]
                 out_ref[at // 2 * 8 : at // 2 * 8 + 8, at % 2 * IDX_DIM : (at % 2 + 1) * IDX_DIM] = total
 
-    for k, (core, d, half, _) in enumerate(ends):
+    for k, (core, half, d, _) in enumerate(ends):
         if d > 0:
             last_copy(k).wait_send()
         else:
@@ -432,9 +459,13 @@
         d.wait_send()
 
 
+def by_x(c, y):
+    return jnp.logical_or(c == 0, y < 2)
+
+
 def whole_kernel(
     order, first, lat_any, idx_any, hw_any, mq_any, iq_any, out_ref,
-    table, lat_ref, idx_ref, hw_ref, w_other, pq, slots, stage_out, stage_in, idx32, idx_stage_out, idx_stage_in, idxg, slots32, sorted32, idx_keys,
+    table, lat_ref, idx_ref, hw_ref, w_other, p_ref, q_ref, slots, stage_out, stage_in, idx32, idx_stage_out, idx_stage_in, idxg, slots32, sorted32, idx_keys,
     vmq, queries, keys, scores, tgt_ref, vidx, idx_q, w_ref, inner_ref, logit_ref, stat_ref, stats_ref, arrive,
     grad_ref, part_ref, xa, za, slab_x, slab_z, final,
     load_sem, pair_send, pair_recv, ring_send, ring_recv, idx_z_sem, idx_x_sem,
@@ -466,13 +497,13 @@
     ]
     for d in loads:
         d.start()
-    for core in range(2):
-
-        @pl.when(c == core)
-        def _(core=core):
-            for _, _, source, maybe_here in final_sources(x, z, core, y):
-                if maybe_here:
-                    pl.when(source[1] != y)(functools.partial(tell, source))
+    for summed_x in (True, False):
+
+        @pl.when(by_x(c, y) if summed_x else jnp.logical_not(by_x(c, y)))
+        def _(summed_x=summed_x):
+            for d, _, source, core in final_sources(x, z, y, summed_x):
+                if d == 0:
+                    pl.when(jnp.logical_or(core != c, source[1] != y))(functools.partial(tell, source))
                 else:
                     tell(source)
 
@@ -492,7 +523,7 @@
     )
     idx_stage_out[...] = jnp.where(c == 0, rows[:, IDX_DIM:], rows[:, :IDX_DIM]).astype(BF16)
     own = jnp.where(jnp.logical_or(y == 0, y == NY - 1), 1, 0)
-    pl.semaphore_wait(barrier, NX - 1 + NZ - 1 + NY - 1 + 1 + 2 * (NZ + NX) - own)
+    pl.semaphore_wait(barrier, NX - 1 + NZ - 1 + NY - 1 + 1 + 3 * NZ + NX - own)
 
     def remote(src, dst, send, recv, to):
         d = pltpu.make_async_remote_copy(
@@ -517,8 +548,8 @@
     pair_copies[1].wait_recv()
     from_partner = stage_in[:, :KD]
     both = jnp.concatenate([jnp.where(c == 0, mine, from_partner), jnp.where(c == 0, from_partner, mine)], axis=1)
-    pq[0, me] = both[:HALF]
-    pq[1, me] = both[HALF:]
+    p_ref[me] = both[:HALF, :P_LANES]
+    q_ref[me] = jnp.concatenate([both[HALF:], both[:HALF, P_LANES:]], axis=1)
     idx_other = idx_stage_in[...]
     idxg[x, z, 0:16] = jnp.where(c == 0, idx_mine, idx_other)
     idxg[x, z, 16:32] = jnp.where(c == 0, idx_other, idx_mine)
@@ -532,7 +563,8 @@
         counter[0] += 1
 
         def block(ox, oz):
-            return pq.at[part, (x + ox + 2 * NX) % NX * NZ + (z + oz + 2 * NZ) % NZ, pl.ds(lo, hi - lo)]
+            ref = q_ref if part else p_ref
+            return ref.at[(x + ox + 2 * NX) % NX * NZ + (z + oz + 2 * NZ) % NZ, pl.ds(lo, hi - lo)]
 
         out = remote(block(dx, dz), block(dx, dz), ring_send.at[k], ring_recv.at[k], ring[(axis, way)])
         here = block(dx - way, dz) if axis == "x" else block(dx, dz - way)
@@ -550,6 +582,14 @@
             live[k][1].wait_recv()
             live[k][2] = True
             landed.append(origin[k])
+
+    gone = set()
+
+    def left(ks):
+        for k in ks:
+            if k not in gone:
+                live[k][0].wait_send()
+                gone.add(k)
 
     last_x, last_z = NX // 2, NZ // 2
 
@@ -586,10 +626,13 @@
     def finish_q(dz):
         xq[dz][2] = hop(1, "x", 0, dz, 2, xq[dz][1])
 
-    idx_z = [
-        remote(idxg.at[x, z], idxg.at[x, z], idx_z_sem.at[0, d - 1], idx_z_sem.at[1, d - 1], peers_z[d - 1])
-        for d in range(1, NZ)
-    ]
+    idx_z = []
+
+    def start_index():
+        for d in range(1, NZ):
+            ref = idxg.at[x, z]
+            idx_z.append(remote(ref, ref, idx_z_sem.at[0, d - 1], idx_z_sem.at[1, d - 1], peers_z[d - 1]))
+
     idx_x = []
 
     def spread_index():
@@ -659,21 +702,24 @@
         if work:
             work.pop(0)()
         for _ in range(min(4, len(landed))):
-            split_cores(pq, slots, *landed.pop(0))
-
+            split_cores(p_ref, q_ref, slots, *landed.pop(0))
+
+    zq[1] = hop(1, "z", 0, 0, 1, None)
+    xp = hop(0, "x", 0, 0, 1, None)
+    left(zq[1])
     start_p(0)
-    xp = hop(0, "x", 0, 0, 1, None)
-    zq[1] = hop(1, "z", 0, 0, 1, None)
+    left(xp)
     xq[0] = {1: hop(1, "x", 0, 0, 1, None)}
-    between()
+    start_index()
+    between()
+    advance_q(2)
     xp2 = hop(0, "x", 0, 0, 2, xp)
     start_p(-1)
     start_p(1)
     between()
     advance_p(0, 2)
-    advance_q(2)
     finish_q(0)
-    between()
+    advance_q(3)
     arrived(xp2[0])
     arrived(xp2[1])
     start_p(2)
@@ -682,26 +728,24 @@
     advance_p(1, 2)
     between()
     advance_p(0, 3)
-    advance_q(3)
-    between()
+    advance_q(4)
     finish_q(-1)
     finish_q(1)
+    between()
     advance_p(2, 2)
     between()
     advance_p(-1, 3)
     advance_p(1, 3)
-    between()
-    advance_p(0, 4)
-    advance_q(4)
+    advance_q(5)
     between()
     finish_q(-2)
     finish_q(2)
+    advance_p(0, 4)
+    between()
     advance_p(2, 3)
     between()
     advance_p(-1, 4)
     advance_p(1, 4)
-    between()
-    advance_q(5)
     finish_q(-3)
     finish_q(3)
     between()
@@ -712,27 +756,27 @@
     for k in live:
         arrived(k)
         while landed:
-            split_cores(pq, slots, *landed.pop(0))
+            split_cores(p_ref, q_ref, slots, *landed.pop(0))
     sort_keys(first, slots, keys)
 
-    tgt_copies = []
+    tgt_copies = {}
+
+    def send_targets(pair, at):
+        cut = pl.ds(4 * at, 12)
+        tgt_copies[pair, at] = [
+            remote(
+                tgt_ref.at[(y + d) % NY, pair, cut], arrive.at[d - 1, pair, cut], tgt_send.at[pair, at // 3, d - 1],
+                tgt_recv.at[pair, at // 3, d - 1], peers_y[d - 1],
+            )
+            for d in range(1, NY)
+        ]
+
     for pair in range(2):
-        targets(table, pair, keys, queries, scores, tgt_ref)
-        tgt_copies.append(
-            [
-                remote(
-                    tgt_ref.at[(y + d) % NY, pair], arrive.at[d - 1, pair], tgt_send.at[pair, d - 1],
-                    tgt_recv.at[pair, d - 1], peers_y[d - 1],
-                )
-                for d in range(1, NY)
-            ]
-        )
+        targets(table, pair, keys, queries, scores, tgt_ref, send_targets)
     for d in stat_copies:
         d.wait_recv()
     for pair in range(2):
         norms = [norms_of(stats_ref, 2 * pair + half) for half in range(2)]
-        for d in tgt_copies[pair]:
-            d.wait_recv()
 
         def step(i, carry):
             gradient_step(
@@ -740,15 +784,17 @@
             )
             return carry
 
-        lax.fori_loop(0, 9, step, 0)
+        for at in range(0, ENTRIES, 3):
+            for d in tgt_copies[pair, at]:
+                d.wait_recv()
+            lax.fori_loop(at, at + 3, step, 0)
     collect_gradients(table, order, grad_ref, sorted32, part_ref)
     scatter(
         x, z, c, y, peers_x, peers_z, remote, part_ref, out_ref, xa, za, slab_x, slab_z, final,
         xa_sem, za_sem, final_send, final_recv,
     )
-    for k in live:
-        live[k][0].wait_send()
-    for d in pair_copies + idx_z + idx_x + stat_copies + tgt_copies[0] + tgt_copies[1]:
+    left(live)
+    for d in pair_copies + idx_z + idx_x + stat_copies + sum(tgt_copies.values(), []):
         d.wait_send()
 
 
@@ -772,7 +818,8 @@
             pltpu.VMEM((TOK, 2 * IDX_DIM), BF16),
             pltpu.VMEM((TOK, 2 * IDX_HEADS), F32),
             pltpu.VMEM((2, 16, 128), F32),
-            pltpu.VMEM((2, NX * NZ, HALF, 2 * KD), BF16),
+            pltpu.VMEM((NX * NZ, HALF, P_LANES), BF16),
+            pltpu.VMEM((NX * NZ, HALF, Q_LANES), BF16),
             pltpu.VMEM((HALVES, HALF, KPAD), BF16),
             pltpu.VMEM((TOK, KPAD), BF16),
             pltpu.VMEM((TOK, KPAD), BF16),
@@ -798,10 +845,10 @@
             pltpu.VMEM((NY - 1, 2, SLOTS, 8, 128), F32),
             pltpu.VMEM((2, ENTRIES, 128, IDX_DIM), F32),
             pltpu.VMEM((NX, NZ, 32, IDX_DIM), F32),
-            pltpu.VMEM((NX - 1, NZ, 16, IDX_DIM), F32),
-            pltpu.VMEM((NZ - 1, NX, 16, IDX_DIM), F32),
-            pltpu.VMEM((NZ, 16, IDX_DIM), F32),
-            pltpu.VMEM((NX, 16, IDX_DIM), F32),
+            pltpu.VMEM((NX - 1, NZ, X_ROWS, IDX_DIM), F32),
+            pltpu.VMEM((NZ - 1, NX, 32 - X_ROWS, IDX_DIM), F32),
+            pltpu.VMEM((NZ, X_ROWS, IDX_DIM), F32),
+            pltpu.VMEM((NX, 32 - X_ROWS, IDX_DIM), F32),
             pltpu.VMEM((NZ, 4, 8, IDX_DIM), F32),
             dma((5,)),
             dma((5,)),
@@ -810,13 +857,13 @@
             dma((RING_COPIES,)),
             dma((2, NZ - 1)),
             dma((2, NX - 1)),
-            dma((2, NY - 1)),
-            dma((2, NY - 1)),
+            dma((2, 3, NY - 1)),
+            dma((2, 3, NY - 1)),
             dma((NY - 1,)),
             dma((NY - 1,)),
             dma((2, NX - 1)),
             dma((2, NZ - 1)),
-            dma((2 * (NX + NZ),)),
+            dma((3 * NZ + NX,)),
             dma((NZ, 4)),
         ],
         compiler_params=pltpu.CompilerParams(
@@ -826,9 +873,9 @@
 
 
 def per_device(mla_queries, latent_keys, index_queries, index_keys, head_weights, block_order):
-    early = block_order.reshape(HALVES // 2, 2)[:, 0]
-    ids = jnp.arange(HALVES // 2, dtype=jnp.int32)
-    first = jnp.sum(jnp.where(early[None, :] == ids[:, None], 2 * ids[None, :], 0), axis=1)
+    places = jnp.arange(HALVES // 2, dtype=jnp.int32)[:, None]
+    slots = jnp.arange(HALVES, dtype=jnp.int32)[None, :]
+    first = jnp.sum(jnp.where(block_order[None, :] == places, slots, 0), axis=1)
     return whole_call(block_order, first, latent_keys, index_keys, head_weights, mla_queries, index_queries)
 
 

time: 98 us -> 88 us (0.90)
  Pallas kernels: 94.9 us -> 85.2 us
    pallas_call x1, Pallas kernels: 94.9 us -> 85.2 us  [whole_call(): pl.pallas_call(whole_kernel, name='indexer_key_gradient', out_shape=jax.S...]
where the time goes in v5:
time: 88 us; the launch traced here: 87.8 us
  Pallas kernels  85.2 us (97%)
  local copies, waits for them, and re-layouts  1.32 us (2%)
  other arithmetic  1.28 us (1%)
    pallas_call x1, Pallas kernels, whole_call(): pl.pallas_call(whole_kernel, name='indexer_key_gradient', out_shape=jax.S...  85.2 us

profile of v5, /device:TPU:1, one launch (start us, length us, event | category | flops | bytes accessed | tf_op | source)
XLA Modules:
  0.0 87.8 jit_solution(922625335935044530)
XLA Ops:
  0.0 1.3 %select_reduce_fusion.first = s32[64]{0:T(128)} fusion(s32[128]{0:T(128)} %order.1), kind=kLoop, calls=%fused_computation | loop fusion | flops 24512 | bytes 768 | tf_op jit(solution)/shard_map/reduce_sum | solution.py:878
  1.3 85.2 %indexer_key_gradient.1 = f32[16,256]{1,0:T(8,128)} custom-call(s32[128]{0:T(128)} %order.1, s32[64]{0:T(128)} %select_reduce_fusion.first, bf16[64,1152]{1,0:T(8,128)(2,1)} %lat_any.1, bf16[64,256]{1,0:T(8,128)(2,1)} %idx_any.1, f32[64,128]{1,0:T(8,128)} %hw_any.1, bf16[2,64,9216]{2,1,0:T(8,128)(2,1)} %mq_any.1, bf16[2,64,8192]{2,1,0:T(8,128)(2,1)} %iq_any.1), custom_call_target="tpu_custom_call" | custom-call | tf_op jit(solution)/shard_map/indexer_key_gradient/pallas_call | solution.py:809
  86.5 1.3 %copy.8 = f32[16,256]{1,0:T(8,128)} copy(f32[16,256]{1,0:T(8,128)} %indexer_key_gradient.1) | data formatting | bytes 32768

commit v6 on v5

--- a/solution.py
+++ b/solution.py
@@ -57,6 +57,13 @@
                 table[(field * 2 + pair) * ENTRIES + i] = jnp.int32(value)
 
 
+def slots_of(row):
+    slot = lax.broadcasted_iota(jnp.int32, (HALVES, HALVES), 0)
+    lane = lax.broadcasted_iota(jnp.int32, (HALVES, HALVES), 1)
+    column = jnp.sum(jnp.where(slot == lane, row, 0), axis=1, keepdims=True)
+    return jnp.max(jnp.where(column == lane, slot - slot % 2, 0), axis=0, keepdims=True)
+
+
 def entry(table, pair, i):
     return [table[(field * 2 + pair) * ENTRIES + i] for field in range(4)]
 
@@ -86,7 +93,7 @@
 
 def sort_keys(first, slots, keys):
     def step(p, carry):
-        slot = first[p]
+        slot = first[0, p]
         low, high = p, HALVES - 1 - p
         keys[low // 16, pl.ds(pl.multiple_of(low % 16 * HALF, HALF), HALF), :] = slots[slot]
         keys[high // 16, pl.ds(pl.multiple_of(high % 16 * HALF, HALF), HALF), :] = slots[slot + 1]
@@ -99,7 +106,7 @@
     slots32[...] = idxg[...].astype(F32).reshape(HALVES, 8, IDX_DIM)
 
     def step(p, carry):
-        slot = first[p]
+        slot = first[0, p]
         sorted32[p] = slots32[slot]
         sorted32[HALVES - 1 - p] = slots32[slot + 1]
         return carry
@@ -365,24 +372,23 @@
     ]
 
 
+def await_bytes(ref, sem):
+    pltpu.make_async_copy(ref, ref, sem).wait()
+
+
 def scatter(
     x, z, c, y, peers_x, peers_z, remote, part_ref, out_ref, xa, za, slab_x, slab_z, final,
-    xa_sem, za_sem, final_send, final_recv,
+    xa_sem, za_sem, final_sem, meanwhile,
 ):
-    first_x = [
+    for d in range(1, NX):
         remote(
-            part_ref.at[(x + d) % NX, :, pl.ds(0, X_ROWS)], xa.at[d - 1], xa_sem.at[0, d - 1], xa_sem.at[1, d - 1],
-            peers_x[d - 1],
+            part_ref.at[(x + d) % NX, :, pl.ds(0, X_ROWS)], xa.at[d - 1], xa_sem.at[0], xa_sem.at[1], peers_x[d - 1],
         )
-        for d in range(1, NX)
-    ]
-    first_z = [
+    for d in range(1, NZ):
         remote(
-            part_ref.at[:, (z + d) % NZ, pl.ds(X_ROWS, 32 - X_ROWS)], za.at[d - 1], za_sem.at[0, d - 1],
-            za_sem.at[1, d - 1], peers_z[d - 1],
+            part_ref.at[:, (z + d) % NZ, pl.ds(X_ROWS, 32 - X_ROWS)], za.at[d - 1], za_sem.at[0], za_sem.at[1],
+            peers_z[d - 1],
         )
-        for d in range(1, NZ)
-    ]
     slot = 2 * (y % 2) + c
     ends = final_targets(x, z, y)
 
@@ -395,8 +401,8 @@
     def last_copy(k):
         d, to = ends[k][2:]
         return pltpu.make_async_remote_copy(
-            src_ref=piece(k), dst_ref=final.at[d, slot], send_sem=final_send.at[k],
-            recv_sem=final_recv.at[d, slot], device_id=to, device_id_type=MESH,
+            src_ref=piece(k), dst_ref=final.at[4 * d + slot], send_sem=final_sem.at[0],
+            recv_sem=final_sem.at[1], device_id=to, device_id_type=MESH,
         )
 
     def here(k):
@@ -417,46 +423,39 @@
 
             @pl.when(here(k))
             def _(k=k):
-                final[0, slot] = piece(k)[...]
-
-    for d in first_x:
-        d.wait_recv()
+                final[slot] = piece(k)[...]
+
+    await_bytes(xa, xa_sem.at[1])
     slab_x[...] = part_ref[x, :, 0:X_ROWS, :] + xa[0] + xa[1] + xa[2]
     send_last(True)
-    for d in first_z:
-        d.wait_recv()
+    await_bytes(za, za_sem.at[1])
     total = part_ref[:, z, X_ROWS:32, :]
     for k in range(NZ - 1):
         total = total + za[k]
     slab_z[...] = total
     send_last(False)
+    meanwhile()
+    await_bytes(xa, xa_sem.at[0])
+    await_bytes(za, za_sem.at[0])
+    own = jnp.logical_or(y == 0, y == NY - 1)
+
+    def await_pieces(count, sem):
+        pl.when(own)(functools.partial(await_bytes, final.at[pl.ds(0, count - 1)], sem))
+        pl.when(jnp.logical_not(own))(functools.partial(await_bytes, final.at[pl.ds(0, count)], sem))
+
     for summed_x in (True, False):
 
         @pl.when(by_x(c, y) if summed_x else jnp.logical_not(by_x(c, y)))
         def _(summed_x=summed_x):
-            for d, at, source, core in final_sources(x, z, y, summed_x):
-                ref = final.at[d, at]
-                arrival = pltpu.make_async_remote_copy(
-                    src_ref=ref, dst_ref=ref, send_sem=final_send.at[0], recv_sem=final_recv.at[d, at],
-                    device_id=source, device_id_type=MESH,
-                )
-                if d == 0:
-                    pl.when(jnp.logical_or(core != c, source[1] != y))(arrival.wait_recv)
-                else:
-                    arrival.wait_recv()
+            count = NZ if summed_x else NX
+            await_pieces(4 * count, final_sem.at[1])
             for at in range(4):
-                total = final[0, at]
-                for d in range(1, NZ if summed_x else NX):
-                    total = total + final[d, at]
+                total = final[at]
+                for d in range(1, count):
+                    total = total + final[4 * d + at]
                 out_ref[at // 2 * 8 : at // 2 * 8 + 8, at % 2 * IDX_DIM : (at % 2 + 1) * IDX_DIM] = total
 
-    for k, (core, half, d, _) in enumerate(ends):
-        if d > 0:
-            last_copy(k).wait_send()
-        else:
-            pl.when(jnp.logical_not(here(k)))(last_copy(k).wait_send)
-    for d in first_x + first_z:
-        d.wait_send()
+    await_pieces(3 * NZ + NX, final_sem.at[0])
 
 
 def by_x(c, y):
@@ -464,12 +463,12 @@
 
 
 def whole_kernel(
-    order, first, lat_any, idx_any, hw_any, mq_any, iq_any, out_ref,
-    table, lat_ref, idx_ref, hw_ref, w_other, p_ref, q_ref, slots, stage_out, stage_in, idx32, idx_stage_out, idx_stage_in, idxg, slots32, sorted32, idx_keys,
+    order, order_row, lat_any, idx_any, hw_any, mq_any, iq_any, out_ref,
+    table, first_row, first, lat_ref, idx_ref, hw_ref, w_other, p_ref, q_ref, slots, stage_out, stage_in, idx32, idx_stage_out, idx_stage_in, idxg, slots32, sorted32, idx_keys,
     vmq, queries, keys, scores, tgt_ref, vidx, idx_q, w_ref, inner_ref, logit_ref, stat_ref, stats_ref, arrive,
     grad_ref, part_ref, xa, za, slab_x, slab_z, final,
-    load_sem, pair_send, pair_recv, ring_send, ring_recv, idx_z_sem, idx_x_sem,
-    tgt_send, tgt_recv, stat_send, stat_recv, xa_sem, za_sem, final_send, final_recv,
+    load_sem, pair_send, pair_recv, ring_send, ring_recv, idx_sem,
+    tgt_sem, stat_sem, xa_sem, za_sem, final_sem,
 ):
     x, z, c, y = coords()
     seq = lax.axis_index("seq")
@@ -508,6 +507,9 @@
                     tell(source)
 
     fill_table(order, seq, table)
+    first_row[...] = jnp.broadcast_to(slots_of(order_row[...]), (8, HALVES))
+    to_scalars = pltpu.make_async_copy(first_row, first, load_sem.at[5])
+    to_scalars.start()
     for d in loads[:3]:
         d.wait()
     weights = weight_rows(hw_ref[...])
@@ -538,9 +540,9 @@
     pair_copies = [
         to_partner(0, stage_out, stage_in),
         to_partner(1, idx_stage_out, idx_stage_in),
-        to_partner(2, iq_any.at[1 - c], vidx.at[1]),
-        to_partner(3, mq_any.at[1 - c], vmq.at[1]),
-        to_partner(4, w_other, w_ref.at[pl.ds(2, 2)]),
+        to_partner(2, w_other, w_ref.at[pl.ds(2, 2)]),
+        to_partner(3, iq_any.at[1 - c], vidx.at[1]),
+        to_partner(4, mq_any.at[1 - c], vmq.at[1]),
     ]
     mine = jnp.where(c == 0, lat[:, :KD], lat[:, KD:])
     idx_mine = jnp.where(c == 0, rows[:, :IDX_DIM], rows[:, IDX_DIM:]).astype(BF16)
@@ -566,10 +568,11 @@
             ref = q_ref if part else p_ref
             return ref.at[(x + ox + 2 * NX) % NX * NZ + (z + oz + 2 * NZ) % NZ, pl.ds(lo, hi - lo)]
 
-        out = remote(block(dx, dz), block(dx, dz), ring_send.at[k], ring_recv.at[k], ring[(axis, way)])
+        gone_sem = ring_send.at[k if k < 4 else 4 + part]
+        out = remote(block(dx, dz), block(dx, dz), gone_sem, ring_recv.at[k], ring[(axis, way)])
         here = block(dx - way, dz) if axis == "x" else block(dx, dz - way)
         arrival = pltpu.make_async_remote_copy(
-            src_ref=here, dst_ref=here, send_sem=ring_send.at[k], recv_sem=ring_recv.at[k],
+            src_ref=here, dst_ref=here, send_sem=gone_sem, recv_sem=ring_recv.at[k],
             device_id=ring[(axis, way)], device_id_type=MESH,
         )
         live[k] = [out, arrival, False]
@@ -583,13 +586,9 @@
             live[k][2] = True
             landed.append(origin[k])
 
-    gone = set()
-
     def left(ks):
         for k in ks:
-            if k not in gone:
-                live[k][0].wait_send()
-                gone.add(k)
+            live[k][0].wait_send()
 
     last_x, last_z = NX // 2, NZ // 2
 
@@ -626,38 +625,23 @@
     def finish_q(dz):
         xq[dz][2] = hop(1, "x", 0, dz, 2, xq[dz][1])
 
-    idx_z = []
-
     def start_index():
         for d in range(1, NZ):
             ref = idxg.at[x, z]
-            idx_z.append(remote(ref, ref, idx_z_sem.at[0, d - 1], idx_z_sem.at[1, d - 1], peers_z[d - 1]))
-
-    idx_x = []
+            remote(ref, ref, idx_sem.at[0], idx_sem.at[1], peers_z[d - 1])
 
     def spread_index():
-        for d in range(1, NZ):
-            ref = idxg.at[x, (z - d + NZ) % NZ]
-            pltpu.make_async_remote_copy(
-                src_ref=ref, dst_ref=ref, send_sem=idx_z_sem.at[0, d - 1], recv_sem=idx_z_sem.at[1, d - 1],
-                device_id=peers_z[d - 1], device_id_type=MESH,
-            ).wait_recv()
+        await_bytes(idxg.at[x, pl.ds(0, NZ - 1)], idx_sem.at[1])
         for d in range(1, NX):
-            idx_x.append(
-                remote(idxg.at[x], idxg.at[x], idx_x_sem.at[0, d - 1], idx_x_sem.at[1, d - 1], peers_x[d - 1])
-            )
+            remote(idxg.at[x], idxg.at[x], idx_sem.at[2], idx_sem.at[3], peers_x[d - 1])
 
     def have_index():
-        for d in range(1, NX):
-            ref = idxg.at[(x - d + NX) % NX]
-            pltpu.make_async_remote_copy(
-                src_ref=ref, dst_ref=ref, send_sem=idx_x_sem.at[0, d - 1], recv_sem=idx_x_sem.at[1, d - 1],
-                device_id=peers_x[d - 1], device_id_type=MESH,
-            ).wait_recv()
+        await_bytes(idxg.at[pl.ds(0, NX - 1)], idx_sem.at[3])
+        pair_copies[2].wait_recv()
+        to_scalars.wait()
         sort_index_keys(first, idxg, slots32, sorted32, idx_keys)
 
     logit_tops = [(jnp.full((8, 128), NEG, F32),) * 2 for _ in range(2)]
-    stat_copies = []
 
     def logits(pair, first, last):
         logit_tops[pair] = lax.fori_loop(
@@ -670,9 +654,7 @@
 
     def send_stats():
         for d in range(1, NY):
-            stat_copies.append(
-                remote(stat_ref, stats_ref.at[d], stat_send.at[d - 1], stat_recv.at[d - 1], peers_y[d - 1])
-            )
+            remote(stat_ref, stats_ref.at[d], stat_sem.at[0], stat_sem.at[1], peers_y[d - 1])
         stats_ref[0] = stat_ref[...]
 
     def own_queries():
@@ -681,15 +663,14 @@
 
     def own_index_queries():
         loads[3].wait()
+        split_index_heads(0, vidx, idx_q)
+
+    def other_index_queries():
+        pair_copies[3].wait_recv()
+        split_index_heads(1, vidx, idx_q)
+
+    def other_queries():
         pair_copies[4].wait_recv()
-        split_index_heads(0, vidx, idx_q)
-
-    def other_index_queries():
-        pair_copies[2].wait_recv()
-        split_index_heads(1, vidx, idx_q)
-
-    def other_queries():
-        pair_copies[3].wait_recv()
         split_heads(1, vmq, queries)
 
     work = [own_index_queries, spread_index, own_queries, have_index]
@@ -759,22 +740,17 @@
             split_cores(p_ref, q_ref, slots, *landed.pop(0))
     sort_keys(first, slots, keys)
 
-    tgt_copies = {}
-
     def send_targets(pair, at):
         cut = pl.ds(4 * at, 12)
-        tgt_copies[pair, at] = [
+        for d in range(1, NY):
             remote(
-                tgt_ref.at[(y + d) % NY, pair, cut], arrive.at[d - 1, pair, cut], tgt_send.at[pair, at // 3, d - 1],
-                tgt_recv.at[pair, at // 3, d - 1], peers_y[d - 1],
+                tgt_ref.at[(y + d) % NY, pair, cut], arrive.at[d - 1, pair, cut], tgt_sem.at[0],
+                tgt_sem.at[1 + pair * 3 + at // 3], peers_y[d - 1],
             )
-            for d in range(1, NY)
-        ]
 
     for pair in range(2):
         targets(table, pair, keys, queries, scores, tgt_ref, send_targets)
-    for d in stat_copies:
-        d.wait_recv()
+    await_bytes(stats_ref.at[pl.ds(1, NY - 1)], stat_sem.at[1])
     for pair in range(2):
         norms = [norms_of(stats_ref, 2 * pair + half) for half in range(2)]
 
@@ -785,23 +761,31 @@
             return carry
 
         for at in range(0, ENTRIES, 3):
-            for d in tgt_copies[pair, at]:
-                d.wait_recv()
+            await_bytes(arrive.at[:, pair, pl.ds(4 * at, 12)], tgt_sem.at[1 + pair * 3 + at // 3])
             lax.fori_loop(at, at + 3, step, 0)
     collect_gradients(table, order, grad_ref, sorted32, part_ref)
+
+    def settle():
+        blocks = NX * NZ - 1 - 2
+        await_bytes(p_ref.at[pl.ds(0, blocks)], ring_send.at[4])
+        await_bytes(q_ref.at[pl.ds(0, blocks)], ring_send.at[5])
+        await_bytes(idxg.at[x, pl.ds(0, NZ - 1)], idx_sem.at[0])
+        await_bytes(idxg.at[pl.ds(0, NX - 1)], idx_sem.at[2])
+        await_bytes(stats_ref.at[pl.ds(1, NY - 1)], stat_sem.at[0])
+        await_bytes(arrive, tgt_sem.at[0])
+        for d in pair_copies:
+            d.wait_send()
+
     scatter(
         x, z, c, y, peers_x, peers_z, remote, part_ref, out_ref, xa, za, slab_x, slab_z, final,
-        xa_sem, za_sem, final_send, final_recv,
+        xa_sem, za_sem, final_sem, settle,
     )
-    left(live)
-    for d in pair_copies + idx_z + idx_x + stat_copies + sum(tgt_copies.values(), []):
-        d.wait_send()
 
 
 RING_COPIES = 76
 
 
-def whole_call(order, first, lat, idx, hw, mq, iq):
+def whole_call(order, order_row, lat, idx, hw, mq, iq):
     any_spec = pl.BlockSpec(memory_space=pl.ANY)
     vmem = pl.BlockSpec(memory_space=pltpu.VMEM)
     smem = pl.BlockSpec(memory_space=pltpu.SMEM)
@@ -810,10 +794,12 @@
         whole_kernel,
         name="indexer_key_gradient",
         out_shape=jax.ShapeDtypeStruct((16, 2 * IDX_DIM), F32),
-        in_specs=[smem] * 2 + [any_spec] * 5,
+        in_specs=[smem, vmem] + [any_spec] * 5,
         out_specs=vmem,
         scratch_shapes=[
             pltpu.SMEM((8 * ENTRIES,), jnp.int32),
+            pltpu.VMEM((8, HALVES), jnp.int32),
+            pltpu.SMEM((8, HALVES), jnp.int32),
             pltpu.VMEM((TOK, 2 * KD), BF16),
             pltpu.VMEM((TOK, 2 * IDX_DIM), BF16),
             pltpu.VMEM((TOK, 2 * IDX_HEADS), F32),
@@ -849,34 +835,28 @@
             pltpu.VMEM((NZ - 1, NX, 32 - X_ROWS, IDX_DIM), F32),
             pltpu.VMEM((NZ, X_ROWS, IDX_DIM), F32),
             pltpu.VMEM((NX, 32 - X_ROWS, IDX_DIM), F32),
-            pltpu.VMEM((NZ, 4, 8, IDX_DIM), F32),
+            pltpu.VMEM((4 * NZ, 8, IDX_DIM), F32),
+            dma((6,)),
             dma((5,)),
             dma((5,)),
-            dma((5,)),
+            dma((6,)),
             dma((RING_COPIES,)),
-            dma((RING_COPIES,)),
-            dma((2, NZ - 1)),
-            dma((2, NX - 1)),
-            dma((2, 3, NY - 1)),
-            dma((2, 3, NY - 1)),
-            dma((NY - 1,)),
-            dma((NY - 1,)),
-            dma((2, NX - 1)),
-            dma((2, NZ - 1)),
-            dma((3 * NZ + NX,)),
-            dma((NZ, 4)),
+            dma((4,)),
+            dma((7,)),
+            dma((2,)),
+            dma((2,)),
+            dma((2,)),
+            dma((2,)),
         ],
         compiler_params=pltpu.CompilerParams(
             collective_id=0, has_side_effects=True, vmem_limit_bytes=VMEM_BYTES
         ),
-    )(order, first, lat, idx, hw, mq, iq)
+    )(order, order_row, lat, idx, hw, mq, iq)
 
 
 def per_device(mla_queries, latent_keys, index_queries, index_keys, head_weights, block_order):
-    places = jnp.arange(HALVES // 2, dtype=jnp.int32)[:, None]
-    slots = jnp.arange(HALVES, dtype=jnp.int32)[None, :]
-    first = jnp.sum(jnp.where(block_order[None, :] == places, slots, 0), axis=1)
-    return whole_call(block_order, first, latent_keys, index_keys, head_weights, mla_queries, index_queries)
+    row = block_order.reshape(1, HALVES)
+    return whole_call(block_order, row, latent_keys, index_keys, head_weights, mla_queries, index_queries)
 
 
 def solution(mesh):

time: 88 us -> 84.8 us (0.964)
  Pallas kernels: 85.2 us -> 83.3 us
  other arithmetic: 1.28 us -> 0 us
    pallas_call x1, Pallas kernels: 85.2 us -> 83.3 us  [whole_call(): pl.pallas_call(whole_kernel, name='indexer_key_gradient', out_shape=jax.S...]
    reduce_sum x1 -> x0, other arithmetic: 1.28 us -> none  [per_device(): first = jnp.sum(jnp.where(block_order[None, :] == places, slots, 0), axis=1)]
where the time goes in v6:
time: 84.8 us; the launch traced here: 84.6 us
  Pallas kernels  83.3 us (98%)
  local copies, waits for them, and re-layouts  1.32 us (2%)
    pallas_call x1, Pallas kernels, whole_call(): pl.pallas_call(whole_kernel, name='indexer_key_gradient', out_shape=jax.S...  83.3 us

profile of v6, /device:TPU:1, one launch (start us, length us, event | category | flops | bytes accessed | tf_op | source)
XLA Modules:
  0.0 84.6 jit_solution(17568257718718627849)
XLA Ops:
  0.0 83.3 %indexer_key_gradient.1 = f32[16,256]{1,0:T(8,128)} custom-call(s32[128]{0:T(128)} %order.1, s32[1,128]{1,0:T(1,128)} %bitcast.1, bf16[64,1152]{1,0:T(8,128)(2,1)} %lat_any.1, bf16[64,256]{1,0:T(8,128)(2,1)} %idx_any.1, f32[64,128]{1,0:T(8,128)} %hw_any.1, bf16[2,64,9216]{2,1,0:T(8,128)(2,1)} %mq_any.1, bf16[2,64,8192]{2,1,0:T(8,128)(2,1)} %iq_any.1), custom_call_target="tpu_custom_call" | custom-call | tf_op jit(solution)/shard_map/indexer_key_gradient/pallas_call | solution.py:793
  83.3 1.3 %copy.8 = f32[16,256]{1,0:T(8,128)} copy(f32[16,256]{1,0:T(8,128)} %indexer_key_gradient.1) | data formatting | bytes 32768

commit v7 on v6

--- a/solution.py
+++ b/solution.py
@@ -541,8 +541,6 @@
         to_partner(0, stage_out, stage_in),
         to_partner(1, idx_stage_out, idx_stage_in),
         to_partner(2, w_other, w_ref.at[pl.ds(2, 2)]),
-        to_partner(3, iq_any.at[1 - c], vidx.at[1]),
-        to_partner(4, mq_any.at[1 - c], vmq.at[1]),
     ]
     mine = jnp.where(c == 0, lat[:, :KD], lat[:, KD:])
     idx_mine = jnp.where(c == 0, rows[:, :IDX_DIM], rows[:, IDX_DIM:]).astype(BF16)
@@ -663,6 +661,8 @@
 
     def own_index_queries():
         loads[3].wait()
+        pair_copies.append(to_partner(3, iq_any.at[1 - c], vidx.at[1]))
+        pair_copies.append(to_partner(4, mq_any.at[1 - c], vmq.at[1]))
         split_index_heads(0, vidx, idx_q)
 
     def other_index_queries():

time: 84.8 us -> 84.8 us (level)
  no operation moved by 1% of the time
where the time goes in v7:
time: 84.8 us; the launch traced here: 84.6 us
  Pallas kernels  83.3 us (98%)
  local copies, waits for them, and re-layouts  1.32 us (2%)
    pallas_call x1, Pallas kernels, whole_call(): pl.pallas_call(whole_kernel, name='indexer_key_gradient', out_shape=jax.S...  83.3 us

profile of v7, /device:TPU:1, one launch (start us, length us, event | category | flops | bytes accessed | tf_op | source)
XLA Modules:
  0.0 84.6 jit_solution(1285749428807999612)
XLA Ops:
  0.0 83.3 %indexer_key_gradient.1 = f32[16,256]{1,0:T(8,128)} custom-call(s32[128]{0:T(128)} %order.1, s32[1,128]{1,0:T(1,128)} %bitcast.1, bf16[64,1152]{1,0:T(8,128)(2,1)} %lat_any.1, bf16[64,256]{1,0:T(8,128)(2,1)} %idx_any.1, f32[64,128]{1,0:T(8,128)} %hw_any.1, bf16[2,64,9216]{2,1,0:T(8,128)(2,1)} %mq_any.1, bf16[2,64,8192]{2,1,0:T(8,128)(2,1)} %iq_any.1), custom_call_target="tpu_custom_call" | custom-call | tf_op jit(solution)/shard_map/indexer_key_gradient/pallas_call | solution.py:793
  83.3 1.3 %copy.8 = f32[16,256]{1,0:T(8,128)} copy(f32[16,256]{1,0:T(8,128)} %indexer_key_gradient.1) | data formatting | bytes 32768
